TPU v7x, 32 devices: a whole 2x2x4 slice. The times are simulated.
32 devices in a mesh: seq: 8 (over y, x, core), row: 4 (over z).
Axes of the slice: x: 2, y: 2, z: 4, core: 2. Of those that a mesh axis runs over, the one named last changes fastest.
Arguments:
- hidden_in: bfloat16 [4, 1024, 2304], P('row', 'seq'), may hold values from -6 to 6
- cotangent: bfloat16 [4, 1024, 2304], P('row', 'seq'), may hold values from -6 to 6
- doc_lengths: int32 [4, 8], P('row'), may hold values from 1 to 896, as said below
- gain_attn_in: float32 [2304], replicated, may hold values from 0.1 to 1.9
- gain_attn_out: float32 [2304], replicated, may hold values from 0.1 to 1.9
- gain_ffw_in: float32 [2304], replicated, may hold values from 0.1 to 1.9
- gain_ffw_out: float32 [2304], replicated, may hold values from 0.1 to 1.9
- query_codes: int32 [2304, 2048], P('seq'), may hold values from -128 to 127
- key_integer_codes: int32 [2304, 1024], P('seq'), may hold values from -128 to 127
- value_integer_codes: int32 [2304, 1024], P('seq'), may hold values from -128 to 127
- out_codes: int32 [2304, 2048], P('seq'), may hold values from -128 to 127
- gate_codes: int32 [2304, 9216], P('seq'), may hold values from -128 to 127
- up_codes: int32 [2304, 9216], P('seq'), may hold values from -128 to 127
- down_codes: int32 [2304, 9216], P('seq'), may hold values from -128 to 127
Outputs:
- block_out: bfloat16 [4, 1024, 2304], P('row', 'seq')
- grad_input: float32 [4, 1024, 2304], P('row', 'seq')
- grad_gain_attn_in: float32 [2304], P('seq')
- grad_gain_attn_out: float32 [2304], P('seq')
- grad_gain_ffw_in: float32 [2304], P('seq')
- grad_gain_ffw_out: float32 [2304], P('seq')
- grad_query: float32 [2304, 2048], P('seq')
- grad_key: float32 [2304, 1024], P('seq')
- grad_value: float32 [2304, 1024], P('seq')
- grad_out: float32 [2304, 2048], P('seq')
- grad_gate: float32 [2304, 9216], P('seq')
- grad_up: float32 [2304, 9216], P('seq')
- grad_down: float32 [2304, 9216], P('seq')
Inputs may be any that keep to these rules, and one draw needn't show every extreme that they name: `doc_lengths`: in each row the lengths sum to 1024; one document, never the first or the last, holds 896 tokens, and the others hold 128 tokens together.
All inputs are finite; a program needn't handle non-finite values.
Results may differ from a plain program's by a relative error of at most 0.023.
Values may be sent and summed in bfloat16 or wider, within the bound.
No kernel may reach another device: no remote copies, remote signals or barrier semaphores. Data moves between devices by JAX's collectives and lax.ppermute only.
A program may use at most 640 MiB of HBM per device.

v0:
```python
import jax
import jax.numpy as jnp
from jax import lax
from jax.sharding import PartitionSpec as P

MODEL_WIDTH = 2304
QUERY_HEADS = 8
KEY_VALUE_HEADS = 4
HEAD_SIZE = 256
FF = 9216
SOFTCAP = 15


epsilon = 1e-06
code_unit = 1.0 / 72.0
key_unit = 1.0 / 44.0
large_negative_fill = -1e30


def codes_eight(code_block):
    return code_block.astype(jnp.bfloat16)


def codes_four(code_block):
    return (code_block // 16 * 16 + 8).astype(jnp.bfloat16)


def codes_two(code_block):
    return (code_block // 64 * 64 + 32).astype(jnp.bfloat16)


def rms_scale(values):
    return lax.rsqrt(jnp.mean(values * values, axis=-1, keepdims=True) + epsilon)


def norm_gain(values, gain_vector):
    return values * rms_scale(values) * gain_vector


def geglu(gate_values, up_values):
    return jax.nn.gelu(gate_values, approximate=True) * up_values


def cross_rows(left_side, right_side):
    return lax.dot_general(
        left_side, right_side, (((0,), (0,)), ((), ())), preferred_element_type=jnp.float32
    )


def times_transposed(left_side, right_side):
    return lax.dot_general(
        left_side, right_side, (((1,), (1,)), ((), ())), preferred_element_type=jnp.float32
    )


def doc_layout(lengths, first_index, row_count):
    doc_ends = jnp.cumsum(lengths)
    starts = doc_ends - lengths
    token_index = first_index + jnp.arange(row_count, dtype=jnp.int32)
    doc_number = jnp.sum((token_index[:, None] >= doc_ends[None, :]).astype(jnp.int32), axis=1)
    picked = doc_number[:, None] == jnp.arange(lengths.shape[0], dtype=jnp.int32)[None, :]
    doc_start = jnp.sum(jnp.where(picked, starts[None, :], 0), axis=1)
    return (token_index, doc_start)


def rotary_tables(positions, head_size):
    half_size = head_size // 2
    frequencies = 10000.0 ** (-(2.0 * jnp.arange(half_size, dtype=jnp.float32)) / head_size)
    angles = positions.astype(jnp.float32)[:, None] * frequencies[None, :]
    return (jnp.cos(angles), jnp.sin(angles))


def apply_rotary(values, cosine_table, sine_table):
    half_size = values.shape[-1] // 2
    first_half = values[..., :half_size]
    second_half = values[..., half_size:]
    cos_wide = cosine_table[:, None, :]
    sin_wide = sine_table[:, None, :]
    return jnp.concatenate(
        [
            first_half * cos_wide - second_half * sin_wide,
            second_half * cos_wide + first_half * sin_wide,
        ],
        axis=-1,
    )


def inverse_rotary(value_gradients, cosine_table, sine_table):
    half_size = value_gradients.shape[-1] // 2
    first_half = value_gradients[..., :half_size]
    second_half = value_gradients[..., half_size:]
    cos_wide = cosine_table[:, None, :]
    sin_wide = sine_table[:, None, :]
    return jnp.concatenate(
        [
            first_half * cos_wide + second_half * sin_wide,
            second_half * cos_wide - first_half * sin_wide,
        ],
        axis=-1,
    )


def score_grads(
    heads_of_queries,
    head_gradients,
    log_totals,
    deltas,
    query_index,
    query_start,
    heads_of_keys,
    heads_of_values,
    key_index,
):
    head_scale = HEAD_SIZE ** (-0.5)
    raw_scores = (
        jnp.einsum(
            "tkgd,rkd->kgtr", heads_of_queries, heads_of_keys, preferred_element_type=jnp.float32
        )
        * head_scale
    )
    capped = SOFTCAP * jnp.tanh(raw_scores / SOFTCAP)
    visible = (key_index[None, :] <= query_index[:, None]) & (
        key_index[None, :] >= query_start[:, None]
    )
    probs = jnp.where(visible, jnp.exp(capped - log_totals[..., None]), 0.0)
    grad_probs = jnp.einsum(
        "tkgd,rkd->kgtr", head_gradients, heads_of_values, preferred_element_type=jnp.float32
    )
    grad_capped = probs * (grad_probs - deltas[..., None])
    grad_raw = (grad_capped * (1.0 - (capped / SOFTCAP) ** 2)).astype(jnp.bfloat16)
    return (grad_raw, probs.astype(jnp.bfloat16))


def reduce_terms(grad_terms):
    shares = lax.psum_scatter(grad_terms, "seq", scatter_dimension=0, tiled=True)
    return lax.psum(shares, "row")


def body(
    hidden_in,
    cotangent,
    doc_lengths,
    gain_attn_in,
    gain_attn_out,
    gain_ffw_in,
    gain_ffw_out,
    query_codes,
    key_integer_codes,
    value_integer_codes,
    out_codes,
    gate_codes,
    up_codes,
    down_codes,
):
    tokens = hidden_in[0].astype(jnp.float32)
    upstream = cotangent[0].astype(jnp.float32)
    lengths = doc_lengths[0]
    resident_rows = tokens.shape[0]
    heads_per_group = QUERY_HEADS // KEY_VALUE_HEADS
    head_scale = HEAD_SIZE ** (-0.5)
    scale_qk = key_unit * MODEL_WIDTH ** (-0.5)
    scale_in = code_unit * MODEL_WIDTH ** (-0.5)
    scale_out = code_unit * (QUERY_HEADS * HEAD_SIZE) ** (-0.5)
    scale_down = code_unit * FF ** (-0.5)
    part_count = 8
    part_width = gate_codes.shape[1] // part_count
    first_row = lax.axis_index("seq") * resident_rows
    local_index, local_start = doc_layout(lengths, first_row, resident_rows)
    cosine_table, sine_table = rotary_tables(local_index - local_start, HEAD_SIZE)

    def attention_weights():
        return (
            lax.all_gather(codes_eight(query_codes), "seq", axis=0, tiled=True),
            lax.all_gather(codes_eight(key_integer_codes), "seq", axis=0, tiled=True),
            lax.all_gather(codes_eight(value_integer_codes), "seq", axis=0, tiled=True),
            lax.all_gather(codes_eight(out_codes), "seq", axis=0, tiled=True),
        )

    def ffn_weights(part_number):
        column_start = part_number * part_width
        column_end = column_start + part_width
        return (
            lax.all_gather(
                codes_four(gate_codes[:, column_start:column_end]), "seq", axis=0, tiled=True
            ),
            lax.all_gather(
                codes_four(up_codes[:, column_start:column_end]), "seq", axis=0, tiled=True
            ),
            lax.all_gather(
                codes_two(down_codes[:, column_start:column_end]), "seq", axis=0, tiled=True
            ),
        )

    attn_set = attention_weights()
    w_query, w_key, w_value, w_out = attn_set
    normed_in = norm_gain(tokens, gain_attn_in).astype(jnp.bfloat16)
    query_lin = jnp.dot(normed_in, w_query, preferred_element_type=jnp.float32) * scale_qk
    key_linear = jnp.dot(normed_in, w_key, preferred_element_type=jnp.float32) * scale_qk
    value_linear = jnp.dot(normed_in, w_value, preferred_element_type=jnp.float32) * scale_in
    rows_of_queries = (
        apply_rotary(
            query_lin.reshape(resident_rows, QUERY_HEADS, HEAD_SIZE), cosine_table, sine_table
        )
        .astype(jnp.bfloat16)
        .reshape(resident_rows, QUERY_HEADS * HEAD_SIZE)
    )
    rows_of_keys = (
        apply_rotary(
            key_linear.reshape(resident_rows, KEY_VALUE_HEADS, HEAD_SIZE), cosine_table, sine_table
        )
        .astype(jnp.bfloat16)
        .reshape(resident_rows, KEY_VALUE_HEADS * HEAD_SIZE)
    )
    rows_of_values = value_linear.astype(jnp.bfloat16)
    heads_of_queries = rows_of_queries.reshape(
        resident_rows, KEY_VALUE_HEADS, heads_per_group, HEAD_SIZE
    )
    running_maximum = jnp.full(
        (KEY_VALUE_HEADS, heads_per_group, resident_rows), large_negative_fill, jnp.float32
    )
    block_of_keys = lax.all_gather(rows_of_keys, "seq", axis=0, tiled=True)
    block_of_values = lax.all_gather(rows_of_values, "seq", axis=0, tiled=True)
    rows_per_block = block_of_keys.shape[0]
    heads_of_keys = block_of_keys.reshape(rows_per_block, KEY_VALUE_HEADS, HEAD_SIZE)
    heads_of_values = block_of_values.reshape(rows_per_block, KEY_VALUE_HEADS, HEAD_SIZE)
    key_index = jnp.arange(rows_per_block, dtype=jnp.int32)
    raw_scores = (
        jnp.einsum(
            "tkgd,rkd->kgtr", heads_of_queries, heads_of_keys, preferred_element_type=jnp.float32
        )
        * head_scale
    )
    capped = SOFTCAP * jnp.tanh(raw_scores / SOFTCAP)
    visible = (key_index[None, :] <= local_index[:, None]) & (
        key_index[None, :] >= local_start[:, None]
    )
    masked = jnp.where(visible, capped, large_negative_fill)
    new_max = jnp.maximum(running_maximum, jnp.max(masked, axis=-1))
    weights = jnp.where(visible, jnp.exp(masked - new_max[..., None]), 0.0)
    run_total = jnp.sum(weights, axis=-1)
    weighted = jnp.einsum(
        "kgtr,rkd->kgtd",
        weights.astype(jnp.bfloat16),
        heads_of_values,
        preferred_element_type=jnp.float32,
    )
    weighted, running_maximum, run_total = (weighted, new_max, run_total)
    attn_heads = weighted / run_total[..., None]
    log_totals = running_maximum + jnp.log(run_total)
    attended = (
        attn_heads.transpose(2, 0, 1, 3)
        .reshape(resident_rows, QUERY_HEADS * HEAD_SIZE)
        .astype(jnp.bfloat16)
    )
    attn_proj = times_transposed(attended, w_out) * scale_out
    middle = tokens + norm_gain(attn_proj, gain_attn_out)
    normed_mid = norm_gain(middle, gain_ffw_in).astype(jnp.bfloat16)
    ffn_proj = jnp.zeros((resident_rows, tokens.shape[1]), jnp.float32)
    gate_store = []
    up_store = []
    mixed_store = []
    ffn_sets = []
    for part_number in range(part_count):
        ffn_set = ffn_weights(part_number)
        w_gate, w_up, w_down = ffn_set
        gate_lin = jnp.dot(normed_mid, w_gate, preferred_element_type=jnp.float32) * scale_in
        up_lin = jnp.dot(normed_mid, w_up, preferred_element_type=jnp.float32) * scale_in
        mixed_rows = geglu(gate_lin, up_lin).astype(jnp.bfloat16)
        ffn_proj = ffn_proj + times_transposed(mixed_rows, w_down) * scale_down
        gate_store.append(gate_lin)
        up_store.append(up_lin)
        mixed_store.append(mixed_rows)
        ffn_sets.append(ffn_set)
    block_out = (middle + norm_gain(ffn_proj, gain_ffw_out)).astype(jnp.bfloat16)
    _, post_pull = jax.vjp(norm_gain, ffn_proj, gain_ffw_out)
    grad_ffn_proj, grad_gain_four = post_pull(upstream)
    grad_ffn_low = grad_ffn_proj.astype(jnp.bfloat16)
    grad_normed_mid = jnp.zeros((resident_rows, tokens.shape[1]), jnp.float32)
    gate_shares = []
    up_shares = []
    down_shares = []
    for part_number in range(part_count):
        back_ffn = ffn_weights(part_number)
        w_gate, w_up, w_down = back_ffn
        grad_mixed = jnp.dot(grad_ffn_low, w_down, preferred_element_type=jnp.float32) * scale_down
        _, geglu_pull = jax.vjp(geglu, gate_store[part_number], up_store[part_number])
        grad_gate_lin, grad_up_lin = geglu_pull(grad_mixed)
        grad_gate_low = grad_gate_lin.astype(jnp.bfloat16)
        grad_up_low = grad_up_lin.astype(jnp.bfloat16)
        grad_normed_mid = (
            grad_normed_mid
            + (times_transposed(grad_gate_low, w_gate) + times_transposed(grad_up_low, w_up))
            * scale_in
        )
        gate_share, up_share, down_share = reduce_terms(
            (
                cross_rows(normed_mid, grad_gate_low),
                cross_rows(normed_mid, grad_up_low),
                cross_rows(grad_ffn_low, mixed_store[part_number]),
            )
        )
        gate_shares.append(gate_share)
        up_shares.append(up_share)
        down_shares.append(down_share)
    _, mid_pull = jax.vjp(norm_gain, middle, gain_ffw_in)
    grad_middle_part, grad_gain_three = mid_pull(grad_normed_mid)
    grad_middle = upstream + grad_middle_part
    _, attn_pull = jax.vjp(norm_gain, attn_proj, gain_attn_out)
    grad_attn_proj, grad_gain_two = attn_pull(grad_middle)
    grad_proj_low = grad_attn_proj.astype(jnp.bfloat16)
    back_attn = attention_weights()
    back_query, back_key, back_value, back_out = back_attn
    grad_attended = jnp.dot(grad_proj_low, back_out, preferred_element_type=jnp.float32) * scale_out
    gradient_attention_narrow = grad_attended.astype(jnp.bfloat16)
    head_gradients = gradient_attention_narrow.reshape(
        resident_rows, KEY_VALUE_HEADS, heads_per_group, HEAD_SIZE
    )
    deltas = jnp.sum(
        gradient_attention_narrow.astype(jnp.float32)
        .reshape(resident_rows, KEY_VALUE_HEADS, heads_per_group, HEAD_SIZE)
        .transpose(1, 2, 0, 3)
        * attn_heads,
        axis=-1,
    )
    block_of_keys = lax.all_gather(rows_of_keys, "seq", axis=0, tiled=True)
    block_of_values = lax.all_gather(rows_of_values, "seq", axis=0, tiled=True)
    rows_per_block = block_of_keys.shape[0]
    heads_of_keys = block_of_keys.reshape(rows_per_block, KEY_VALUE_HEADS, HEAD_SIZE)
    heads_of_values = block_of_values.reshape(rows_per_block, KEY_VALUE_HEADS, HEAD_SIZE)
    key_index = jnp.arange(rows_per_block, dtype=jnp.int32)
    grad_raw, probs_low = score_grads(
        heads_of_queries,
        head_gradients,
        log_totals,
        deltas,
        local_index,
        local_start,
        heads_of_keys,
        heads_of_values,
        key_index,
    )
    grad_query_heads = (
        jnp.einsum("kgtr,rkd->tkgd", grad_raw, heads_of_keys, preferred_element_type=jnp.float32)
        * head_scale
    )
    resident_keys = rows_of_keys.reshape(resident_rows, KEY_VALUE_HEADS, HEAD_SIZE)
    resident_values = rows_of_values.reshape(resident_rows, KEY_VALUE_HEADS, HEAD_SIZE)
    block_of_queries = lax.all_gather(
        rows_of_queries.astype(jnp.float32), "seq", axis=0, tiled=True
    )
    block_gradient = lax.all_gather(
        gradient_attention_narrow.astype(jnp.float32), "seq", axis=0, tiled=True
    )
    lse_block = lax.all_gather(log_totals.transpose(2, 0, 1), "seq", axis=0, tiled=True)
    delta_block = lax.all_gather(deltas.transpose(2, 0, 1), "seq", axis=0, tiled=True)
    rows_per_block = block_of_queries.shape[0]
    foreign_queries = block_of_queries.astype(jnp.bfloat16).reshape(
        rows_per_block, KEY_VALUE_HEADS, heads_per_group, HEAD_SIZE
    )
    foreign_gradients = block_gradient.astype(jnp.bfloat16).reshape(
        rows_per_block, KEY_VALUE_HEADS, heads_per_group, HEAD_SIZE
    )
    remote_index, remote_start = doc_layout(lengths, jnp.int32(0), rows_per_block)
    grad_raw, probs_low = score_grads(
        foreign_queries,
        foreign_gradients,
        lse_block.transpose(1, 2, 0),
        delta_block.transpose(1, 2, 0),
        remote_index,
        remote_start,
        resident_keys,
        resident_values,
        local_index,
    )
    key_gradients = (
        jnp.einsum("kgtr,tkgd->rkd", grad_raw, foreign_queries, preferred_element_type=jnp.float32)
        * head_scale
    )
    value_gradients = jnp.einsum(
        "kgtr,tkgd->rkd", probs_low, foreign_gradients, preferred_element_type=jnp.float32
    )
    grad_query_lin = (
        inverse_rotary(
            grad_query_heads.reshape(resident_rows, QUERY_HEADS, HEAD_SIZE),
            cosine_table,
            sine_table,
        )
        .reshape(resident_rows, QUERY_HEADS * HEAD_SIZE)
        .astype(jnp.bfloat16)
    )
    grad_key_lin = (
        inverse_rotary(key_gradients, cosine_table, sine_table)
        .reshape(resident_rows, KEY_VALUE_HEADS * HEAD_SIZE)
        .astype(jnp.bfloat16)
    )
    value_linear_gradient = value_gradients.reshape(
        resident_rows, KEY_VALUE_HEADS * HEAD_SIZE
    ).astype(jnp.bfloat16)
    grad_normed_in = (
        times_transposed(grad_query_lin, back_query) + times_transposed(grad_key_lin, back_key)
    ) * scale_qk + times_transposed(value_linear_gradient, back_value) * scale_in
    _, in_pull = jax.vjp(norm_gain, tokens, gain_attn_in)
    grad_tokens_part, grad_gain_one = in_pull(grad_normed_in)
    grad_input = grad_middle + grad_tokens_part
    attn_shares = reduce_terms(
        (
            cross_rows(normed_in, grad_query_lin),
            cross_rows(normed_in, grad_key_lin),
            cross_rows(normed_in, value_linear_gradient),
            cross_rows(grad_proj_low, attended),
            grad_gain_one,
            grad_gain_two,
            grad_gain_three,
            grad_gain_four,
        )
    )
    return (
        block_out[None],
        grad_input[None],
        attn_shares[4],
        attn_shares[5],
        attn_shares[6],
        attn_shares[7],
        attn_shares[0],
        attn_shares[1],
        attn_shares[2],
        attn_shares[3],
        jnp.concatenate(gate_shares, axis=1),
        jnp.concatenate(up_shares, axis=1),
        jnp.concatenate(down_shares, axis=1),
    )


def solution(mesh):
    return jax.shard_map(
        body,
        mesh=mesh,
        in_specs=(
            P("row", "seq", None),
            P("row", "seq", None),
            P("row", None),
            P(),
            P(),
            P(),
            P(),
            P("seq", None),
            P("seq", None),
            P("seq", None),
            P("seq", None),
            P("seq", None),
            P("seq", None),
            P("seq", None),
        ),
        out_specs=(
            P("row", "seq", None),
            P("row", "seq", None),
            P("seq"),
            P("seq"),
            P("seq"),
            P("seq"),
            P("seq", None),
            P("seq", None),
            P("seq", None),
            P("seq", None),
            P("seq", None),
            P("seq", None),
            P("seq", None),
        ),
        check_vma=False,
    )
```

profile of v0, /device:TPU:0, one launch (start us, length us, event | category | flops | bytes accessed | tf_op | source)
XLA Modules:
  0.0 5319.8 jit_solution(9898163797185335501)
XLA Ops:
  10.8 41.3 all-gather.39.cloned.1.call-done
  223.6 52.6 all-gather.43.cloned.1.call-done
  496.9 39.5 all-gather.63.cloned.1.call-done
  540.7 39.6 all-gather.69.cloned.1.call-done
  584.6 39.5 all-gather.75.cloned.1.call-done
  1631.1 86.3 %reduce-scatter.41.cloned.1.call-done = f32[288,1152]{1,0:T(8,128)} async-done(((f32[2304,1152]{1,0:T(8,128)}), f32[288,1152]{1,0:T(8,128)}) %reduce-scatter.41.cloned.1.call-update) | async-done | bytes 1327120 | tf_op jit(solution)/shard_map/reduce_scatter | solution.py:135
  1717.5 85.6 %reduce-scatter.43.cloned.1.call-done = f32[288,1152]{1,0:T(8,128)} async-done(((f32[2304,1152]{1,0:T(8,128)}), f32[288,1152]{1,0:T(8,128)}) %reduce-scatter.43.cloned.1.call-update) | async-done | bytes 1327120 | tf_op jit(solution)/shard_map/reduce_scatter | solution.py:135
  1803.1 85.6 %reduce-scatter.45.cloned.1.call-done = f32[288,1152]{1,0:T(8,128)} async-done(((f32[2304,1152]{1,0:T(8,128)}), f32[288,1152]{1,0:T(8,128)}) %reduce-scatter.45.cloned.1.call-update) | async-done | bytes 1327120 | tf_op jit(solution)/shard_map/reduce_scatter | solution.py:135
  1888.7 85.8 %reduce-scatter.47.cloned.1.call-done = f32[288,1152]{1,0:T(8,128)} async-done(((f32[2304,1152]{1,0:T(8,128)}), f32[288,1152]{1,0:T(8,128)}) %reduce-scatter.47.cloned.1.call-update) | async-done | bytes 1327120 | tf_op jit(solution)/shard_map/reduce_scatter | solution.py:135
  1974.4 85.6 %reduce-scatter.49.cloned.1.call-done = f32[288,1152]{1,0:T(8,128)} async-done(((f32[2304,1152]{1,0:T(8,128)}), f32[288,1152]{1,0:T(8,128)}) %reduce-scatter.49.cloned.1.call-update) | async-done | bytes 1327120 | tf_op jit(solution)/shard_map/reduce_scatter | solution.py:135
  2060.0 85.7 %reduce-scatter.51.cloned.1.call-done = f32[288,1152]{1,0:T(8,128)} async-done(((f32[2304,1152]{1,0:T(8,128)}), f32[288,1152]{1,0:T(8,128)}) %reduce-scatter.51.cloned.1.call-update) | async-done | bytes 1327120 | tf_op jit(solution)/shard_map/reduce_scatter | solution.py:135
  2145.8 85.8 %reduce-scatter.53.cloned.1.call-done = f32[288,1152]{1,0:T(8,128)} async-done(((f32[2304,1152]{1,0:T(8,128)}), f32[288,1152]{1,0:T(8,128)}) %reduce-scatter.53.cloned.1.call-update) | async-done | bytes 1327120 | tf_op jit(solution)/shard_map/reduce_scatter | solution.py:135
  2231.5 85.8 %reduce-scatter.55.cloned.1.call-done = f32[288,1152]{1,0:T(8,128)} async-done(((f32[2304,1152]{1,0:T(8,128)}), f32[288,1152]{1,0:T(8,128)}) %reduce-scatter.55.cloned.1.call-update) | async-done | bytes 1327120 | tf_op jit(solution)/shard_map/reduce_scatter | solution.py:135
  2317.3 85.6 %reduce-scatter.57.cloned.1.call-done = f32[288,1152]{1,0:T(8,128)} async-done(((f32[2304,1152]{1,0:T(8,128)}), f32[288,1152]{1,0:T(8,128)}) %reduce-scatter.57.cloned.1.call-update) | async-done | bytes 1327120 | tf_op jit(solution)/shard_map/reduce_scatter | solution.py:135
  2402.9 85.8 %reduce-scatter.59.cloned.1.call-done = f32[288,1152]{1,0:T(8,128)} async-done(((f32[2304,1152]{1,0:T(8,128)}), f32[288,1152]{1,0:T(8,128)}) %reduce-scatter.59.cloned.1.call-update) | async-done | bytes 1327120 | tf_op jit(solution)/shard_map/reduce_scatter | solution.py:135
  2488.6 85.6 %reduce-scatter.61.cloned.1.call-done = f32[288,1152]{1,0:T(8,128)} async-done(((f32[2304,1152]{1,0:T(8,128)}), f32[288,1152]{1,0:T(8,128)}) %reduce-scatter.61.cloned.1.call-update) | async-done | bytes 1327120 | tf_op jit(solution)/shard_map/reduce_scatter | solution.py:135
  2574.3 85.6 %reduce-scatter.63.cloned.1.call-done = f32[288,1152]{1,0:T(8,128)} async-done(((f32[2304,1152]{1,0:T(8,128)}), f32[288,1152]{1,0:T(8,128)}) %reduce-scatter.63.cloned.1.call-update) | async-done | bytes 1327120 | tf_op jit(solution)/shard_map/reduce_scatter | solution.py:135
  2659.9 85.6 %reduce-scatter.65.cloned.1.call-done = f32[288,1152]{1,0:T(8,128)} async-done(((f32[2304,1152]{1,0:T(8,128)}), f32[288,1152]{1,0:T(8,128)}) %reduce-scatter.65.cloned.1.call-update) | async-done | bytes 1327120 | tf_op jit(solution)/shard_map/reduce_scatter | solution.py:135
  2745.5 85.6 %reduce-scatter.67.cloned.1.call-done = f32[288,1152]{1,0:T(8,128)} async-done(((f32[2304,1152]{1,0:T(8,128)}), f32[288,1152]{1,0:T(8,128)}) %reduce-scatter.67.cloned.1.call-update) | async-done | bytes 1327120 | tf_op jit(solution)/shard_map/reduce_scatter | solution.py:135
  2831.1 85.6 %reduce-scatter.69.cloned.1.call-done = f32[288,1152]{1,0:T(8,128)} async-done(((f32[2304,1152]{1,0:T(8,128)}), f32[288,1152]{1,0:T(8,128)}) %reduce-scatter.69.cloned.1.call-update) | async-done | bytes 1327120 | tf_op jit(solution)/shard_map/reduce_scatter | solution.py:135
  2916.7 85.8 %reduce-scatter.71.cloned.1.call-done = f32[288,1152]{1,0:T(8,128)} async-done(((f32[2304,1152]{1,0:T(8,128)}), f32[288,1152]{1,0:T(8,128)}) %reduce-scatter.71.cloned.1.call-update) | async-done | bytes 1327120 | tf_op jit(solution)/shard_map/reduce_scatter | solution.py:135
  3002.4 85.6 %reduce-scatter.73.cloned.1.call-done = f32[288,1152]{1,0:T(8,128)} async-done(((f32[2304,1152]{1,0:T(8,128)}), f32[288,1152]{1,0:T(8,128)}) %reduce-scatter.73.cloned.1.call-update) | async-done | bytes 1327120 | tf_op jit(solution)/shard_map/reduce_scatter | solution.py:135
  3088.1 85.8 %reduce-scatter.75.cloned.1.call-done = f32[288,1152]{1,0:T(8,128)} async-done(((f32[2304,1152]{1,0:T(8,128)}), f32[288,1152]{1,0:T(8,128)}) %reduce-scatter.75.cloned.1.call-update) | async-done | bytes 1327120 | tf_op jit(solution)/shard_map/reduce_scatter | solution.py:135
  3173.8 85.6 %reduce-scatter.77.cloned.1.call-done = f32[288,1152]{1,0:T(8,128)} async-done(((f32[2304,1152]{1,0:T(8,128)}), f32[288,1152]{1,0:T(8,128)}) %reduce-scatter.77.cloned.1.call-update) | async-done | bytes 1327120 | tf_op jit(solution)/shard_map/reduce_scatter | solution.py:135
  3259.4 85.8 %reduce-scatter.79.cloned.1.call-done = f32[288,1152]{1,0:T(8,128)} async-done(((f32[2304,1152]{1,0:T(8,128)}), f32[288,1152]{1,0:T(8,128)}) %reduce-scatter.79.cloned.1.call-update) | async-done | bytes 1327120 | tf_op jit(solution)/shard_map/reduce_scatter | solution.py:135
  3345.2 85.8 %reduce-scatter.81.cloned.1.call-done = f32[288,1152]{1,0:T(8,128)} async-done(((f32[2304,1152]{1,0:T(8,128)}), f32[288,1152]{1,0:T(8,128)}) %reduce-scatter.81.cloned.1.call-update) | async-done | bytes 1327120 | tf_op jit(solution)/shard_map/reduce_scatter | solution.py:135
  3430.9 85.8 %reduce-scatter.83.cloned.1.call-done = f32[288,1152]{1,0:T(8,128)} async-done(((f32[2304,1152]{1,0:T(8,128)}), f32[288,1152]{1,0:T(8,128)}) %reduce-scatter.83.cloned.1.call-update) | async-done | bytes 1327120 | tf_op jit(solution)/shard_map/reduce_scatter | solution.py:135
  3516.7 80.0 %reduce-scatter.31.cloned.1.call-done = f32[288,1024]{1,0:T(8,128)} async-done(((f32[2304,1024]{1,0:T(8,128)}), f32[288,1024]{1,0:T(8,128)}) %reduce-scatter.31.cloned.1.call-update) | async-done | bytes 1179664 | tf_op jit(solution)/shard_map/reduce_scatter | solution.py:135
  3596.7 79.9 %reduce-scatter.33.cloned.1.call-done = f32[288,1024]{1,0:T(8,128)} async-done(((f32[2304,1024]{1,0:T(8,128)}), f32[288,1024]{1,0:T(8,128)}) %reduce-scatter.33.cloned.1.call-update) | async-done | bytes 1179664 | tf_op jit(solution)/shard_map/reduce_scatter | solution.py:135
  3676.6 129.6 %reduce-scatter.29.cloned.1.call-done = f32[288,2048]{1,0:T(8,128)} async-done(((f32[2304,2048]{1,0:T(8,128)}), f32[288,2048]{1,0:T(8,128)}) %reduce-scatter.29.cloned.1.call-update) | async-done | bytes 2359312 | tf_op jit(solution)/shard_map/reduce_scatter | solution.py:135
  3806.2 129.8 %reduce-scatter.35.cloned.1.call-done = f32[288,2048]{1,0:T(8,128)} async-done(((f32[2304,2048]{1,0:T(8,128)}), f32[288,2048]{1,0:T(8,128)}) %reduce-scatter.35.cloned.1.call-update) | async-done | bytes 2359312 | tf_op jit(solution)/shard_map/reduce_scatter | solution.py:135
  3994.0 1274.0 %all-reduce.9.cloned.1.call-done = (f32[288,2048]{1,0:T(8,128)}, f32[288,1024]{1,0:T(8,128)}, f32[288,1024]{1,0:T(8,128)}, f32[288,2048]{1,0:T(8,128)}, f32[288,...) async-done(((f32[288,2048]{1,0:T(8,128)}, ...) | async-done | bytes 38928400 | tf_op jit(solution)/shard_map/psum | solution.py:136
  (787 shorter events, 1510.1 us)
Async XLA Ops:
  140.2 786.9 %all-gather.65.cloned.1.call-start = ((), (), s32[]{:S(2)}) async-start(), calls=%async_computation.44 | async-start | bytes 5971968 | tf_op jit(solution)/shard_map/all_gather | solution.py:186
  140.9 829.4 %all-gather.67.cloned.1.call-start = ((), (), s32[]{:S(2)}) async-start(), calls=%async_computation.45 | async-start | bytes 5971968 | tf_op jit(solution)/shard_map/all_gather | solution.py:189
  141.6 872.0 %all-gather.71.cloned.1.call-start = ((), (), s32[]{:S(2)}) async-start(), calls=%async_computation.47 | async-start | bytes 5971968 | tf_op jit(solution)/shard_map/all_gather | solution.py:186
  142.4 914.4 %all-gather.73.cloned.1.call-start = ((), (), s32[]{:S(2)}) async-start(), calls=%async_computation.48 | async-start | bytes 5971968 | tf_op jit(solution)/shard_map/all_gather | solution.py:189
  143.0 957.2 %all-gather.77.cloned.1.call-start = ((), (), s32[]{:S(2)}) async-start(), calls=%async_computation.50 | async-start | bytes 5971968 | tf_op jit(solution)/shard_map/all_gather | solution.py:186
  143.7 999.6 %all-gather.79.cloned.1.call-start = ((), (), s32[]{:S(2)}) async-start(), calls=%async_computation.51 | async-start | bytes 5971968 | tf_op jit(solution)/shard_map/all_gather | solution.py:189
  144.3 1042.2 %all-gather.83.cloned.1.call-start = ((), (), s32[]{:S(2)}) async-start(), calls=%async_computation.53 | async-start | bytes 5971968 | tf_op jit(solution)/shard_map/all_gather | solution.py:186
  144.9 1084.9 %all-gather.85.cloned.1.call-start = ((), (), s32[]{:S(2)}) async-start(), calls=%async_computation.54 | async-start | bytes 5971968 | tf_op jit(solution)/shard_map/all_gather | solution.py:189
  145.6 1127.5 %all-gather.89.cloned.1.call-start = ((), (), s32[]{:S(2)}) async-start(), calls=%async_computation.56 | async-start | bytes 5971968 | tf_op jit(solution)/shard_map/all_gather | solution.py:186
  146.4 1169.9 %all-gather.91.cloned.1.call-start = ((), (), s32[]{:S(2)}) async-start(), calls=%async_computation.57 | async-start | bytes 5971968 | tf_op jit(solution)/shard_map/all_gather | solution.py:189
  146.9 1416.4 %all-gather.95.cloned.1.call-start = ((), (), s32[]{:S(2)}) async-start(), calls=%async_computation.59 | async-start | bytes 4718592 | tf_op jit(solution)/shard_map/all_gather | solution.py:351
  1435.5 796.0 %reduce-scatter.53.cloned.1.call-start = ((), (), s32[]{:S(2)}) async-start(), calls=%async_computation.72 | async-start | bytes 11943936 | tf_op jit(solution)/shard_map/reduce_scatter | solution.py:135
  1441.9 875.4 %reduce-scatter.55.cloned.1.call-start = ((), (), s32[]{:S(2)}) async-start(), calls=%async_computation.73 | async-start | bytes 11943936 | tf_op jit(solution)/shard_map/reduce_scatter | solution.py:135
  1448.3 954.6 %reduce-scatter.57.cloned.1.call-start = ((), (), s32[]{:S(2)}) async-start(), calls=%async_computation.74 | async-start | bytes 11943936 | tf_op jit(solution)/shard_map/reduce_scatter | solution.py:135
  1454.9 1033.8 %reduce-scatter.59.cloned.1.call-start = ((), (), s32[]{:S(2)}) async-start(), calls=%async_computation.75 | async-start | bytes 11943936 | tf_op jit(solution)/shard_map/reduce_scatter | solution.py:135
  1461.3 1113.0 %reduce-scatter.61.cloned.1.call-start = ((), (), s32[]{:S(2)}) async-start(), calls=%async_computation.76 | async-start | bytes 11943936 | tf_op jit(solution)/shard_map/reduce_scatter | solution.py:135
  1467.8 1192.0 %reduce-scatter.63.cloned.1.call-start = ((), (), s32[]{:S(2)}) async-start(), calls=%async_computation.77 | async-start | bytes 11943936 | tf_op jit(solution)/shard_map/reduce_scatter | solution.py:135
  1476.7 1268.7 %reduce-scatter.65.cloned.1.call-start = ((), (), s32[]{:S(2)}) async-start(), calls=%async_computation.78 | async-start | bytes 11943936 | tf_op jit(solution)/shard_map/reduce_scatter | solution.py:135
  1483.3 1347.8 %reduce-scatter.67.cloned.1.call-start = ((), (), s32[]{:S(2)}) async-start(), calls=%async_computation.79 | async-start | bytes 11943936 | tf_op jit(solution)/shard_map/reduce_scatter | solution.py:135
  1490.3 1426.4 %reduce-scatter.69.cloned.1.call-start = ((), (), s32[]{:S(2)}) async-start(), calls=%async_computation.80 | async-start | bytes 11943936 | tf_op jit(solution)/shard_map/reduce_scatter | solution.py:135
  1496.7 1505.7 %reduce-scatter.71.cloned.1.call-start = ((), (), s32[]{:S(2)}) async-start(), calls=%async_computation.81 | async-start | bytes 11943936 | tf_op jit(solution)/shard_map/reduce_scatter | solution.py:135
  1503.2 1584.9 %reduce-scatter.73.cloned.1.call-start = ((), (), s32[]{:S(2)}) async-start(), calls=%async_computation.82 | async-start | bytes 11943936 | tf_op jit(solution)/shard_map/reduce_scatter | solution.py:135
  1509.8 1664.1 %reduce-scatter.75.cloned.1.call-start = ((), (), s32[]{:S(2)}) async-start(), calls=%async_computation.83 | async-start | bytes 11943936 | tf_op jit(solution)/shard_map/reduce_scatter | solution.py:135
  1516.2 1743.2 %reduce-scatter.77.cloned.1.call-start = ((), (), s32[]{:S(2)}) async-start(), calls=%async_computation.84 | async-start | bytes 11943936 | tf_op jit(solution)/shard_map/reduce_scatter | solution.py:135
  1522.8 1822.4 %reduce-scatter.79.cloned.1.call-start = ((), (), s32[]{:S(2)}) async-start(), calls=%async_computation.85 | async-start | bytes 11943936 | tf_op jit(solution)/shard_map/reduce_scatter | solution.py:135
  1529.7 1901.2 %reduce-scatter.81.cloned.1.call-start = ((), (), s32[]{:S(2)}) async-start(), calls=%async_computation.86 | async-start | bytes 11943936 | tf_op jit(solution)/shard_map/reduce_scatter | solution.py:135
  1536.2 1980.5 %reduce-scatter.83.cloned.1.call-start = ((), (), s32[]{:S(2)}) async-start(), calls=%async_computation.87 | async-start | bytes 11943936 | tf_op jit(solution)/shard_map/reduce_scatter | solution.py:135
  1542.7 2054.0 %reduce-scatter.31.cloned.1.call-start = ((), (), s32[]{:S(2)}) async-start(), calls=%async_computation.61 | async-start | bytes 10616832 | tf_op jit(solution)/shard_map/reduce_scatter | solution.py:135
  1589.7 2086.9 %reduce-scatter.33.cloned.1.call-start = ((), (), s32[]{:S(2)}) async-start(), calls=%async_computation.62 | async-start | bytes 10616832 | tf_op jit(solution)/shard_map/reduce_scatter | solution.py:135
  1599.9 2206.3 %reduce-scatter.29.cloned.1.call-start = ((), (), s32[]{:S(2)}) async-start(), calls=%async_computation.60 | async-start | bytes 21233664 | tf_op jit(solution)/shard_map/reduce_scatter | solution.py:135
  1618.4 2317.6 %reduce-scatter.35.cloned.1.call-start = ((), (), s32[]{:S(2)}) async-start(), calls=%async_computation.63 | async-start | bytes 21233664 | tf_op jit(solution)/shard_map/reduce_scatter | solution.py:135
  1627.8 3640.2 %all-reduce.9.cloned.1.call-start = ((), (), s32[]{:S(2)}) async-start(), calls=%async_computation.88 | async-start | bytes 77856768 | tf_op jit(solution)/shard_map/psum | solution.py:136
  (238 other events, 12677.3 us)
Sparse Core Ops, SparseCore 0:
  10.5 41.6 all-gather.38
  125.7 58.8 all-gather.36
  217.4 58.8 all-gather.42
  1462.6 82.1 reduce-scatter.36
  1548.9 82.2 reduce-scatter.38
  1635.2 82.2 reduce-scatter.40
  1720.8 82.2 reduce-scatter.42
  1806.4 82.2 reduce-scatter.44
  1892.2 82.2 reduce-scatter.46
  1977.8 82.2 reduce-scatter.48
  2063.6 82.1 reduce-scatter.50
  2149.3 82.2 reduce-scatter.52
  2235.0 82.2 reduce-scatter.54
  2320.6 82.2 reduce-scatter.56
  2406.4 82.1 reduce-scatter.58
  2492.0 82.1 reduce-scatter.60
  2577.6 82.2 reduce-scatter.62
  2663.2 82.2 reduce-scatter.64
  2748.8 82.2 reduce-scatter.66
  2834.4 82.2 reduce-scatter.68
  2920.2 82.2 reduce-scatter.70
  3005.8 82.1 reduce-scatter.72
  3091.6 82.2 reduce-scatter.74
  3177.2 82.2 reduce-scatter.76
  3262.9 82.2 reduce-scatter.78
  3348.7 82.2 reduce-scatter.80
  3434.4 82.1 reduce-scatter.82
  3520.2 76.4 reduce-scatter.30
  3600.1 76.4 reduce-scatter.32
  3680.1 126.1 reduce-scatter.28
  3809.8 126.1 reduce-scatter.34
  3942.4 1325.5 all-reduce.8
  (29 shorter events, 1160.8 us)
where the time goes:
time: 5330 us; the launch traced here: 5320 us
  waiting for transfers between devices  4700 us (88%)
  matrix products  389 us (7%)
  local copies, waits for them, and re-layouts  99.1 us (2%)
  blocking collectives  55.6 us (1%)
    reduce_scatter x28, waiting for transfers between devices, reduce_terms(): lax.psum_scatter(grad_terms, 'seq', scatter_dimension=0, tiled=True)  2310 us
    psum x1, waiting for transfers between devices, reduce_terms(): return lax.psum(shares, 'row')  1270 us
    all_gather x8, waiting for transfers between devices, ffn_weights(): lax.all_gather(codes_two(down_codes[:, column_start:column_end]), 'seq',...  310 us
    all_gather x8, waiting for transfers between devices, ffn_weights(): lax.all_gather(codes_four(gate_codes[:, column_start:column_end]), 'seq',...  309 us
    all_gather x8, waiting for transfers between devices, ffn_weights(): lax.all_gather(codes_four(up_codes[:, column_start:column_end]), 'seq', a...  305 us
    dot_general x28, matrix products, cross_rows(): lax.dot_general(left_side, right_side, (((0,), (0,)), ((), ())), preferre...  163 us
  transfers between devices with their start and end apart: 61, of which 57 were waited for; matrix products, arithmetic and copies ran while one was open for 8% of the time, Pallas kernels for 0%

commit v1 on v0

--- a/solution.py
+++ b/solution.py
@@ -136,7 +136,7 @@
     return lax.psum(shares, "row")
 
 
-def body(
+def token_body(
     hidden_in,
     cotangent,
     doc_lengths,
@@ -431,7 +431,292 @@
     )
 
 
+def seq_swap(block, bit):
+    return lax.ppermute(block, "seq", [(place, place ^ bit) for place in range(8)])
+
+
+def row_swap(block, bit):
+    return lax.ppermute(block, "row", [(place, place ^ bit) for place in range(4)])
+
+
+def bf(values):
+    return values.astype(jnp.bfloat16)
+
+
+def wide(values):
+    return values.astype(jnp.float32)
+
+
+RELATIVE = (0, 2, 4, 6, 1, 3, 5, 7)
+
+
+def gather_row(block):
+    half = block.shape[0] // 2
+    from_x = seq_swap(block, 2)
+    from_y = seq_swap(block, 4)
+    far_first = seq_swap(from_y[:half], 2)
+    far_last = seq_swap(from_x[half:], 4)
+    mine = jnp.concatenate([block, from_x, from_y, far_first, far_last])
+    return jnp.concatenate([mine, seq_swap(mine, 1)])
+
+
+def other_core(rows):
+    middle = rows.shape[0] // 2
+    theirs = seq_swap(rows, 1)
+    return jnp.concatenate([theirs[middle:], theirs[:middle]])
+
+
+def scatter_row(partial_rows, row_count):
+    middle = row_count // 2
+    unit = row_count // 8
+    half = unit // 2
+    theirs = seq_swap(bf(partial_rows(middle, row_count)), 1)
+    mine = partial_rows(0, middle) + wide(theirs)
+    here, by_x, by_y, far = (mine[i * unit : (i + 1) * unit] for i in range(4))
+    from_x = seq_swap(bf(jnp.concatenate([by_x[:half], far[:half]])), 2)
+    from_y = seq_swap(bf(jnp.concatenate([by_y[half:], far[half:]])), 4)
+    last_y = seq_swap(bf(by_y[:half] + wide(from_x[half:])), 4)
+    last_x = seq_swap(bf(by_x[half:] + wide(from_y[half:])), 2)
+    return jnp.concatenate(
+        [
+            here[:half] + wide(from_x[:half]) + wide(last_y),
+            here[half:] + wide(from_y[:half]) + wide(last_x),
+        ]
+    )
+
+
+def spread_columns(code_rows):
+    rows, columns = code_rows.shape
+    blocks = code_rows.reshape(rows, 8, columns // 8).transpose(1, 0, 2)
+    return lax.all_to_all(blocks, "seq", 0, 0, tiled=True).reshape(rows * 8, columns // 8)
+
+
+def spread_rows(gradient):
+    rows, columns = gradient.shape
+    blocks = lax.all_to_all(
+        bf(gradient).reshape(8, rows // 8, columns), "seq", 0, 0, tiled=True
+    )
+    return wide(blocks.transpose(1, 0, 2).reshape(rows // 8, columns * 8))
+
+
+def dot(left, right):
+    return jnp.dot(left, right, preferred_element_type=jnp.float32)
+
+
+def turn(values, cosine, sine):
+    half = values.shape[-1] // 2
+    first, last = values[..., :half], values[..., half:]
+    return jnp.concatenate([first * cosine - last * sine, last * cosine + first * sine], axis=-1)
+
+
+def norm_back(values, gain, upstream):
+    scale = rms_scale(values)
+    lifted = upstream * gain
+    shared = jnp.mean(lifted * values, axis=-1, keepdims=True)
+    gradient = scale * lifted - values * (scale * scale * scale) * shared
+    return gradient, jnp.sum(upstream * values * scale, axis=0)
+
+
+def geglu_back(gate, up, grad_mixed):
+    mixed, pull = jax.vjp(geglu, gate, up)
+    grad_gate, grad_up = pull(grad_mixed)
+    return bf(mixed), bf(grad_gate), bf(grad_up)
+
+
+def plane_body(
+    hidden_in,
+    cotangent,
+    doc_lengths,
+    gain_attn_in,
+    gain_attn_out,
+    gain_ffw_in,
+    gain_ffw_out,
+    query_codes,
+    key_integer_codes,
+    value_integer_codes,
+    out_codes,
+    gate_codes,
+    up_codes,
+    down_codes,
+):
+    lengths = doc_lengths[0]
+    block_rows, width = hidden_in.shape[1:]
+    row_length = block_rows * 8
+    place = lax.axis_index("seq")
+    core = place % 2
+    head = HEAD_SIZE
+    half = head // 2
+    scale_qk = key_unit * MODEL_WIDTH ** (-0.5)
+    scale_in = code_unit * MODEL_WIDTH ** (-0.5)
+    scale_out = code_unit * (QUERY_HEADS * HEAD_SIZE) ** (-0.5)
+    scale_down = code_unit * FF ** (-0.5)
+    head_scale = HEAD_SIZE ** (-0.5)
+
+    model_rows = query_codes.shape[0]
+    attn_blocks = jnp.concatenate(
+        [
+            codes_eight(codes).reshape(model_rows, 8, codes.shape[1] // 8)
+            for codes in (query_codes, key_integer_codes, value_integer_codes, out_codes)
+        ],
+        axis=2,
+    )
+    attn_weights = spread_columns(attn_blocks.reshape(model_rows, -1))
+    w_attn_in = attn_weights[:, : 2 * head]
+    w_out = attn_weights[:, 2 * head :]
+    w_gate = spread_columns(codes_four(gate_codes))
+    w_up = spread_columns(codes_four(up_codes))
+    w_down = spread_columns(codes_two(down_codes))
+
+    token_blocks = [(place ^ k) * block_rows + jnp.arange(block_rows) for k in RELATIVE]
+    token_index = jnp.concatenate(token_blocks).astype(jnp.int32)
+    ends = jnp.cumsum(lengths)
+    past = token_index[:, None] >= ends[None, :]
+    doc_start = jnp.max(jnp.where(past, ends[None, :], 0), axis=1)
+    cosine, sine = rotary_tables(token_index - doc_start, head)
+    visible = (token_index[None, :] <= token_index[:, None]) & (
+        token_index[None, :] >= doc_start[:, None]
+    )
+
+    tokens = wide(hidden_in[0])
+    upstream = wide(cotangent[0])
+    row_tokens = gather_row(hidden_in[0])
+    normed_in = bf(norm_gain(wide(row_tokens), gain_attn_in))
+    linear = dot(normed_in, w_attn_in)
+    query = bf(turn(linear[:, :head] * scale_qk, cosine, sine))
+    key_half = linear[:, head : head + half] * scale_qk
+    value_half = bf(linear[:, head + half :] * scale_in)
+    key_other = other_core(key_half)
+    value_other = other_core(value_half)
+
+    def pair(own, other):
+        return jnp.where(
+            core == 0,
+            jnp.concatenate([own, other], axis=-1),
+            jnp.concatenate([other, own], axis=-1),
+        )
+
+    key = bf(turn(pair(key_half, key_other), cosine, sine))
+    value = pair(value_half, value_other)
+    bend = jnp.tanh(times_transposed(query, key) * (head_scale / SOFTCAP))
+    weights = jnp.where(visible, jnp.exp(SOFTCAP * bend), 0.0)
+    totals = jnp.sum(weights, axis=-1, keepdims=True)
+    attended_wide = dot(bf(weights), value) / totals
+    attended = bf(attended_wide)
+    attn_proj = scale_out * scatter_row(
+        lambda a, b: times_transposed(attended[a:b], w_out), row_length
+    )
+    middle = tokens + norm_gain(attn_proj, gain_attn_out)
+    normed_mid = bf(norm_gain(middle, gain_ffw_in))
+
+    row_mid = gather_row(normed_mid)
+    gate = dot(row_mid, w_gate) * scale_in
+    up = dot(row_mid, w_up) * scale_in
+    mixed = bf(geglu(gate, up))
+    ffn_proj = scale_down * scatter_row(
+        lambda a, b: times_transposed(mixed[a:b], w_down), row_length
+    )
+    block_out = bf(middle + norm_gain(ffn_proj, gain_ffw_out))
+    grad_ffn, grad_gain_four = norm_back(ffn_proj, gain_ffw_out, upstream)
+    grad_ffn_low = bf(grad_ffn)
+
+    others_mid = gather_row(jnp.concatenate([row_swap(normed_mid, bit) for bit in (1, 2, 3)]))
+    others_ffn = gather_row(jnp.concatenate([row_swap(grad_ffn_low, bit) for bit in (1, 2, 3)]))
+
+    row_ffn = gather_row(grad_ffn_low)
+    grad_mixed = dot(row_ffn, w_down) * scale_down
+    _, grad_gate, grad_up = geglu_back(gate, up, grad_mixed)
+    grad_mid = scale_in * scatter_row(
+        lambda a, b: times_transposed(grad_gate[a:b], w_gate)
+        + times_transposed(grad_up[a:b], w_up),
+        row_length,
+    )
+    grad_middle_part, grad_gain_three = norm_back(middle, gain_ffw_in, grad_mid)
+    grad_middle = upstream + grad_middle_part
+    grad_proj, grad_gain_two = norm_back(attn_proj, gain_attn_out, grad_middle)
+
+    row_proj = gather_row(bf(grad_proj))
+    grad_attended = bf(dot(row_proj, w_out) * scale_out)
+    delta = jnp.sum(wide(grad_attended) * attended_wide, axis=-1, keepdims=True)
+    probs = weights / totals
+    grad_probs = times_transposed(grad_attended, value)
+    grad_raw = bf(probs * (grad_probs - delta) * (1.0 - bend * bend))
+    grad_query = bf(turn(dot(grad_raw, key) * head_scale, cosine, -sine))
+    key_part = cross_rows(grad_raw, query) * head_scale
+    value_part = cross_rows(bf(probs), grad_attended)
+
+    def own_half(values, side):
+        return lax.dynamic_slice_in_dim(values, side * half, half, axis=1)
+
+    key_sum = key_part + other_core(key_part)
+    grad_key = bf(own_half(turn(key_sum, cosine, -sine), core))
+    grad_value = bf(own_half(value_part, core) + other_core(own_half(value_part, 1 - core)))
+    grad_linear = jnp.concatenate([grad_query, grad_key, grad_value], axis=1)
+    scaled_linear = (grad_linear[:, : head + half], grad_linear[:, head + half :])
+    grad_in = scatter_row(
+        lambda a, b: scale_qk * times_transposed(scaled_linear[0][a:b], w_attn_in[:, : head + half])
+        + scale_in * times_transposed(scaled_linear[1][a:b], w_attn_in[:, head + half :]),
+        row_length,
+    )
+    grad_tokens, grad_gain_one = norm_back(tokens, gain_attn_in, grad_in)
+    grad_input = grad_middle + grad_tokens
+
+    other_gate = dot(others_mid, w_gate) * scale_in
+    other_up = dot(others_mid, w_up) * scale_in
+    other_grad = dot(others_ffn, w_down) * scale_down
+    other_mixed, other_grad_gate, other_grad_up = geglu_back(other_gate, other_up, other_grad)
+    grad_w_down = spread_rows(cross_rows(row_ffn, mixed) + cross_rows(others_ffn, other_mixed))
+    grad_w_gate = spread_rows(
+        cross_rows(row_mid, grad_gate) + cross_rows(others_mid, other_grad_gate)
+    )
+    grad_w_up = spread_rows(cross_rows(row_mid, grad_up) + cross_rows(others_mid, other_grad_up))
+
+    own_part = jnp.concatenate(
+        [cross_rows(normed_in, grad_linear), cross_rows(row_proj, attended)], axis=1
+    )
+    columns = own_part.shape[1]
+    quarter = model_rows // 4
+    row_place = lax.axis_index("row")
+    low_bit, high_bit = row_place % 2, row_place // 2
+    quarters = bf(own_part).reshape(8, 2, 2, quarter, columns)
+
+    def halve(terms, bit, axis, side):
+        kept = lax.dynamic_index_in_dim(terms, side, axis, keepdims=False)
+        sent = lax.dynamic_index_in_dim(terms, 1 - side, axis, keepdims=False)
+        return bf(wide(kept) + wide(row_swap(sent, bit)))
+
+    summed = halve(halve(quarters, 1, 2, low_bit), 2, 1, high_bit)
+    blocks = lax.all_to_all(summed, "seq", 0, 0, tiled=True).transpose(1, 0, 2)
+    blocks = wide(lax.all_gather(blocks, "row", axis=0, tiled=True))
+    cuts = (0, head, head + half, 2 * head, 3 * head)
+    attn_grads = [
+        blocks[:, :, a:b].reshape(model_rows, 8 * (b - a)) for a, b in zip(cuts, cuts[1:])
+    ]
+
+    gain_terms = jnp.stack(
+        [grad_gain_one, grad_gain_two, grad_gain_three, grad_gain_four], axis=1
+    )
+    gains = lax.psum(
+        lax.psum_scatter(gain_terms, "seq", scatter_dimension=0, tiled=True), "row"
+    )
+    return (
+        block_out[None],
+        grad_input[None],
+        gains[:, 0],
+        gains[:, 1],
+        gains[:, 2],
+        gains[:, 3],
+        attn_grads[0],
+        attn_grads[1],
+        attn_grads[2],
+        attn_grads[3],
+        grad_w_gate,
+        grad_w_up,
+        grad_w_down,
+    )
+
+
 def solution(mesh):
+    body = plane_body if dict(mesh.shape) == {"seq": 8, "row": 4} else token_body
     return jax.shard_map(
         body,
         mesh=mesh,

time: 5330 us -> 1250 us (0.23)
  waiting for transfers between devices: 4700 us -> 578 us
  starting transfers between devices: 3.72 us -> 127 us
  matrix products: 389 us -> 317 us
    reduce_scatter x28 -> x0, waiting for transfers between devices: 2310 us -> none  [reduce_terms(): lax.psum_scatter(grad_terms, 'seq', scatter_dimension=0, tiled=True)]
    psum x1 -> x0, waiting for transfers between devices: 1270 us -> none  [reduce_terms(): return lax.psum(shares, 'row')]
    all_gather x32 -> x1, waiting for transfers between devices: 1110 us -> 0.01 us  [plane_body(): blocks = wide(lax.all_gather(blocks, 'row', axis=0, tiled=True))]
    ppermute x0 -> x62, waiting for transfers between devices: none -> 459 us  [the longest x54 338 us: seq_swap(): lax.ppermute(block, 'seq', [(place, place ^ bit) for place in range(8)])]
    ppermute x0 -> x62, starting transfers between devices: none -> 89.9 us  [the longest x54 48 us: seq_swap(): lax.ppermute(block, 'seq', [(place, place ^ bit) for place in range(8)])]
    all_to_all x0 -> x8, waiting for transfers between devices: none -> 67.7 us  [the longest x4 67.7 us: spread_columns(): lax.all_to_all(blocks, 'seq', 0, 0, tiled=True)]
    dot_general x28 -> x10, matrix products: 163 us -> 136 us  [cross_rows(): lax.dot_general(left_side, right_side, (((0,), (0,)), ((), ())), preferre...]
    dot_general x34 -> x10, matrix products: 134 us -> 122 us  [dot(): return jnp.dot(left, right, preferred_element_type=jnp.float32)]
  transfers between devices with their start and end apart: 61 -> 72, of which waited for: 57 -> 34; matrix products, arithmetic and copies ran while one was open for 8% -> 36% of each run, Pallas kernels for 0% -> 0%
where the time goes in v1:
time: 1250 us
  waiting for transfers between devices  578 us (46%)
  matrix products  317 us (25%)
  starting transfers between devices  127 us (10%)
  local copies, waits for them, and re-layouts  110 us (9%)
  other arithmetic  82.8 us (7%)
  between operations  17.8 us (1%)
  blocking collectives  12.5 us (1%)
    ppermute x54, waiting for transfers between devices, seq_swap(): lax.ppermute(block, 'seq', [(place, place ^ bit) for place in range(8)])  338 us
    dot_general x10, matrix products, cross_rows(): lax.dot_general(left_side, right_side, (((0,), (0,)), ((), ())), preferre...  136 us
    dot_general x10, matrix products, dot(): return jnp.dot(left, right, preferred_element_type=jnp.float32)  122 us
    ppermute x8, waiting for transfers between devices, row_swap(): lax.ppermute(block, 'row', [(place, place ^ bit) for place in range(4)])  121 us
    all_to_all x4, waiting for transfers between devices, spread_columns(): lax.all_to_all(blocks, 'seq', 0, 0, tiled=True)  67.7 us
    dot_general x14, matrix products, times_transposed(): lax.dot_general(left_side, right_side, (((1,), (1,)), ((), ())), preferre...  58.7 us
    unnamed x3, waiting for transfers between devices  51 us
    ppermute x54, starting transfers between devices, seq_swap(): lax.ppermute(block, 'seq', [(place, place ^ bit) for place in range(8)])  48 us
  transfers between devices with their start and end apart: 72, of which 34 were waited for; matrix products, arithmetic and copies ran while one was open for 36% of the time, Pallas kernels for 0%

profile of v1, /device:TPU:0, one launch (start us, length us, event | category | flops | bytes accessed | tf_op | source)
XLA Modules:
  0.0 1245.8 jit_solution(10618868628179935949)
XLA Ops:
  52.3 33.8 %all-to-all-done = bf16[8,288,768]{2,1,0:T(8,128)(2,1)S(1)} async-done(((bf16[8,288,768]{2,1,0:T(8,128)(2,1)}), bf16[8,288,768]{2,1,0:T(8,128)(2,1)S(1)}, u32[]{:S(2)}, u32[]{:S(2)}) %all-to-all-start) | async-done | bytes 3538976 | tf_op jit(solution)/shard_map/all_to_all | solution.py:491
  114.5 14.1 %collective-permute-done.8 = bf16[128,2304]{1,0:T(8,128)(2,1)S(1)} collective-permute-done((bf16[128,2304]{1,0:T(8,128)(2,1)S(1)}, bf16[128,2304]{1,0:T(8,128)(2,1)S(1)}, u32[]{:S(2)}, u32[]{:S(2)}) %collective-permute-start.8) | collective-permute-done | bytes 589856 | tf_op jit(solution)/shard_map/ppermute | solution.py:435
  161.9 49.8 %collective-permute-done.11 = bf16[64,2304]{1,0:T(8,128)(2,1)S(1)} collective-permute-done((bf16[64,2304]{1,0:T(8,128)(2,1)S(1)}, bf16[64,2304]{1,0:T(8,128)(2,1)S(1)}, u32[]{:S(2)}, u32[]{:S(2)}) %collective-permute-start.11) | collective-permute-done | bytes 294944 | tf_op jit(solution)/shard_map/ppermute | solution.py:435
  223.0 68.1 %collective-permute-done.13 = bf16[128,2304]{1,0:T(8,128)(2,1)S(1)} collective-permute-done((bf16[128,2304]{1,0:T(8,128)(2,1)S(1)}, bf16[128,2304]{1,0:T(8,128)(2,1)S(1)}, u32[]{:S(2)}, u32[]{:S(2)}) %collective-permute-start.13) | collective-permute-done | bytes 589856 | tf_op jit(solution)/shard_map/ppermute | solution.py:435
  325.6 9.8 convolution_multiply_fusion.9
  337.5 11.9 multiply_convert_fusion.5
  349.5 33.9 %all-to-all-done.3 = bf16[8,288,1152]{2,1,0:T(8,128)(2,1)} async-done(((bf16[8,288,1152]{2,1,0:T(8,128)(2,1)}), bf16[8,288,1152]{2,1,0:T(8,128)(2,1)}, u32[]{:S(2)}, u32[]{:S(2)}) %all-to-all-start.3) | async-done | bytes 5308448 | tf_op jit(solution)/shard_map/all_to_all | solution.py:491
  394.0 23.5 %collective-permute-done.46 = bf16[128,2304]{1,0:T(8,128)(2,1)S(1)} collective-permute-done((bf16[128,2304]{1,0:T(8,128)(2,1)S(1)}, bf16[128,2304]{1,0:T(8,128)(2,1)S(1)}, u32[]{:S(2)}, u32[]{:S(2)}) %collective-permute-start.46) | collective-permute-done | bytes 589856 | tf_op jit(solution)/shard_map/ppermute | solution.py:439
  418.4 15.2 %collective-permute-done.47 = bf16[128,2304]{1,0:T(8,128)(2,1)S(1)} collective-permute-done((bf16[128,2304]{1,0:T(8,128)(2,1)S(1)}, bf16[128,2304]{1,0:T(8,128)(2,1)S(1)}, u32[]{:S(2)}, u32[]{:S(2)}) %collective-permute-start.47) | collective-permute-done | bytes 589856 | tf_op jit(solution)/shard_map/ppermute | solution.py:439
  446.7 11.2 collective-permute-done.18
  458.5 33.9 %collective-permute-done.20 = bf16[128,2304]{1,0:T(8,128)(2,1)S(1)} collective-permute-done((bf16[128,2304]{1,0:T(8,128)(2,1)S(1)}, bf16[128,2304]{1,0:T(8,128)(2,1)S(1)}, u32[]{:S(2)}, u32[]{:S(2)}) %collective-permute-start.20) | collective-permute-done | bytes 589856 | tf_op jit(solution)/shard_map/ppermute | solution.py:435
  510.4 17.1 %collective-permute-done.23 = bf16[128,2304]{1,0:T(8,128)(2,1)S(1)} collective-permute-done((bf16[128,2304]{1,0:T(8,128)(2,1)S(1)}, bf16[128,2304]{1,0:T(8,128)(2,1)S(1)}, u32[]{:S(2)}, u32[]{:S(2)}) %collective-permute-start.23) | collective-permute-done | bytes 589856 | tf_op jit(solution)/shard_map/ppermute | solution.py:435
  536.4 19.5 %collective-permute-start.54 = (bf16[128,2304]{1,0:T(8,128)(2,1)S(1)}, bf16[128,2304]{1,0:T(8,128)(2,1)S(1)}, u32[]{:S(2)}, u32[]{:S(2)}) collective-permute-start(bf16[128,2304]{1,0:T(8,128)(2,1)S(1)} %get-tuple-element.31), channel_id=1, source_target_pairs={{0,1},{1,0},{2,3},{3,2},{4,5},{5,4},{6,7},{7,6},{8,9},{9,8},{10,11... | collective-permute-start | bytes 1769480 | tf_op jit(solution)/shard_map/ppermute | solution.py:439
  560.7 20.7 %collective-permute-done.54 = bf16[128,2304]{1,0:T(8,128)(2,1)S(1)} collective-permute-done((bf16[128,2304]{1,0:T(8,128)(2,1)S(1)}, bf16[128,2304]{1,0:T(8,128)(2,1)S(1)}, u32[]{:S(2)}, u32[]{:S(2)}) %collective-permute-start.54) | collective-permute-done | bytes 589856 | tf_op jit(solution)/shard_map/ppermute | solution.py:439
  582.7 16.6 %collective-permute-done.55 = bf16[128,2304]{1,0:T(8,128)(2,1)S(1)} collective-permute-done((bf16[128,2304]{1,0:T(8,128)(2,1)S(1)}, bf16[128,2304]{1,0:T(8,128)(2,1)S(1)}, u32[]{:S(2)}, u32[]{:S(2)}) %collective-permute-start.55) | collective-permute-done | bytes 589856 | tf_op jit(solution)/shard_map/ppermute | solution.py:439
  603.3 15.9 %multiply_convert_fusion.4 = (bf16[1024,1152]{1,0:T(8,128)(2,1)S(1)}, bf16[1024,1152]{1,0:T(8,128)(2,1)}) fusion(f32[1024,1152]{1,0:T(8,128)} %copy-done.88, f32[1024,1152]{1,0:T(8,128)} %get-tuple-element.168, bf16[1024,2304]{1,0:T(8,128)(2,1)S(1)} %constant_dynamic-update-slice_fusion.28, bf16[2304,1152]{1,0:T(8,128)(2,1)} %bitcast.12), kind=kOutput, calls=%fused_computation.84 | convolution fusion | flops 5465309184 | bytes 24182784 | tf_op jit(solution)/shard_map/dot_general | solution.py:503
  699.3 24.3 %convolution_multiply_fusion = f32[3072,1152]{1,0:T(8,128)} fusion(bf16[3072,2304]{1,0:T(8,128)(2,1)} %constant_dynamic-update-slice_fusion.55, bf16[2304,1152]{1,0:T(8,128)(2,1)} %bitcast.8), kind=kOutput, calls=%fused_computation.14 | convolution fusion | flops 16310992896 | bytes 33619968 | tf_op jit(solution)/shard_map/dot_general | solution.py:503
  731.6 24.8 %convolution_multiply_fusion.1 = f32[3072,1152]{1,0:T(8,128)} fusion(bf16[3072,2304]{1,0:T(8,128)(2,1)} %constant_dynamic-update-slice_fusion.55, bf16[2304,1152]{1,0:T(8,128)(2,1)} %bitcast.10), kind=kOutput, calls=%fused_computation.15 | convolution fusion | flops 16310992896 | bytes 33619968 | tf_op jit(solution)/shard_map/dot_general | solution.py:503
  780.3 24.3 %convolution_multiply_fusion.2 = f32[3072,1152]{1,0:T(8,128)} fusion(bf16[3072,2304]{1,0:T(8,128)(2,1)} %constant_dynamic-update-slice_fusion.73, bf16[2304,1152]{1,0:T(8,128)(2,1)} %bitcast.12), kind=kOutput, calls=%fused_computation.16 | convolution fusion | flops 16310992896 | bytes 33619968 | tf_op jit(solution)/shard_map/dot_general | solution.py:503
  804.7 35.8 %fusion.30 = f32[2304,1152]{1,0:T(8,128)} fusion(bf16[3072,2304]{1,0:T(8,128)(2,1)} %constant_dynamic-update-slice_fusion.55, f32[3072,1152]{1,0:T(8,128)} %convolution_multiply_fusion, f32[3072,1152]{1,0:T(8,128)} %convolution_multiply_fusion.2, f32[3072,1152]{1,0:T(8,128)} %convolution_multiply_fusion.1), kind=kOutput, calls=%fused_computation.61 | convolution fusion | flops 16381771776 | bytes 67239936 | tf_op jit(solution)/shard_map/dot_general | solution.py:45
  854.1 12.7 %collective-permute-start.44 = (bf16[8,2,72,768]{3,2,1,0:T(8,128)(2,1)S(1)}, bf16[8,2,72,768]{3,2,1,0:T(8,128)(2,1)S(1)}, u32[]{:S(2)}, u32[]{:S(2)}) collective-permute-start(bf16[8,2,72,768]{3,2,1,0:T(8,128)(2,1)S(1)} %fusion.51), channel_id=1, source_target_pairs={{0,1},{1,0},{2,3},{3,2},{4,5},{5,4},{6,7},{7,6},{8,9},{9,8},{10,11... | collective-permute-start | bytes 5308424 | tf_op jit(solution)/shard_map/ppermute | solution.py:439
  866.8 28.2 %fusion.28 = f32[2304,1152]{1,0:T(8,128)} fusion(bf16[3072,2304]{1,0:T(8,128)(2,1)} %constant_dynamic-update-slice_fusion.55, f32[3072,1152]{1,0:T(8,128)} %convolution_multiply_fusion.2, f32[3072,1152]{1,0:T(8,128)} %convolution_multiply_fusion), kind=kOutput, calls=%fused_computation.59 | convolution fusion | flops 16342843392 | bytes 53084160 | tf_op jit(solution)/shard_map/dot_general | solution.py:45
  894.9 11.1 collective-permute-done.44
  914.0 34.0 %collective-permute-done.45 = bf16[8,72,768]{2,1,0:T(8,128)(2,1)S(1)} collective-permute-done((bf16[8,72,768]{2,1,0:T(8,128)(2,1)S(1)}, bf16[8,72,768]{2,1,0:T(8,128)(2,1)S(1)}, u32[]{:S(2)}, u32[]{:S(2)}) %collective-permute-start.45) | collective-permute-done | bytes 884768 | tf_op jit(solution)/shard_map/ppermute | solution.py:439
  953.8 12.0 fusion.8
  980.4 12.7 %fusion.7 = bf16[2304,1152]{1,0:T(8,128)(2,1)} fusion(f32[2304,1152]{1,0:T(8,128)} %fusion.30, bf16[1024,2304]{1,0:T(8,128)(2,1)} %constant_dynamic-update-slice_fusion.17, bf16[1024,1152]{1,0:T(8,128)(2,1)S(1)} %copy-done.85), kind=kOutput, calls=%fused_computation.32 | convolution fusion | flops 5441126400 | bytes 23003136 | tf_op jit(solution)/shard_map/dot_general | solution.py:45
  994.6 52.2 %collective-permute-done.40 = bf16[128,2304]{1,0:T(8,128)(2,1)S(1)} collective-permute-done((bf16[128,2304]{1,0:T(8,128)(2,1)S(1)}, bf16[128,2304]{1,0:T(8,128)(2,1)S(1)}, u32[]{:S(2)}, u32[]{:S(2)}) %collective-permute-start.40) | collective-permute-done | bytes 589856 | tf_op jit(solution)/shard_map/ppermute | solution.py:435
  1053.3 25.9 %fusion.29 = f32[2304,1152]{1,0:T(8,128)S(1)} fusion(bf16[3072,2304]{1,0:T(8,128)(2,1)} %constant_dynamic-update-slice_fusion.73, f32[3072,1152]{1,0:T(8,128)} %convolution_multiply_fusion.1, f32[3072,1152]{1,0:T(8,128)} %convolution_multiply_fusion), kind=kOutput, calls=%fused_computation.60 | convolution fusion | flops 16342843392 | bytes 53084160 | tf_op jit(solution)/shard_map/dot_general | solution.py:45
  1082.6 10.1 fusion.9
  1092.7 26.9 %collective-permute-done.43 = bf16[64,2304]{1,0:T(8,128)(2,1)S(1)} collective-permute-done((bf16[64,2304]{1,0:T(8,128)(2,1)S(1)}, bf16[64,2304]{1,0:T(8,128)(2,1)S(1)}, u32[]{:S(2)}, u32[]{:S(2)}) %collective-permute-start.43) | collective-permute-done | bytes 294944 | tf_op jit(solution)/shard_map/ppermute | solution.py:435
  1139.2 50.5 %reduce-scatter.4.cloned.1.call-done = f32[288,4]{1,0:T(8,128)} async-done(((f32[2304,4]{1,0:T(8,128)}), f32[288,4]{1,0:T(8,128)}) %reduce-scatter.4.cloned.1.call-update) | async-done | bytes 4624
  1190.7 12.5 %psum.7 = f32[288,4]{0,1:T(4,128)S(1)} all-reduce(f32[288,4]{0,1:T(4,128)S(1)} %copy.81), channel_id=1, replica_groups=mesh['seq'=8,'row'=4] {'row'}, use_global_device_ids=true, to_apply=%region_18.19 | all-reduce | flops 1152 | bytes 9216 | tf_op jit(solution)/shard_map/psum | solution.py:698
  (510 shorter events, 435.1 us)
Async XLA Ops:
  39.8 46.4 %all-to-all-start = ((bf16[8,288,768]{2,1,0:T(8,128)(2,1)}), bf16[8,288,768]{2,1,0:T(8,128)(2,1)S(1)}, u32[]{:S(2)}, u32[]{:S(2)}) async-start(bf16[8,288,768]{2,1,0:T(8,128)(2,1)} %copy.67), calls=%async_computation | async-start | bytes 7077888 | tf_op jit(solution)/shard_map/all_to_all | solution.py:491
  140.7 72.9 %all-to-all-start.1 = ((bf16[8,288,1152]{2,1,0:T(8,128)(2,1)}), bf16[8,288,1152]{2,1,0:T(8,128)(2,1)}, u32[]{:S(2)}, u32[]{:S(2)}) async-start(bf16[8,288,1152]{2,1,0:T(8,128)(2,1)} %copy.68), calls=%async_computation.1 | async-start | bytes 10616832 | tf_op jit(solution)/shard_map/all_to_all | solution.py:491
  146.7 64.9 %collective-permute-start.11 = (bf16[64,2304]{1,0:T(8,128)(2,1)S(1)}, bf16[64,2304]{1,0:T(8,128)(2,1)S(1)}, u32[]{:S(2)}, u32[]{:S(2)}) collective-permute-start(bf16[64,2304]{1,0:T(8,128)(2,1)S(1)} %get-tuple-element.51), channel_id=1, source_target_pairs={{0,8},{4,12},{8,0},{12,4},{16,24},{20,28},{24,16},{28,20},{1,9},{5... | collective-permute-start | bytes 884744 | tf_op jit(solution)/shard_map/ppermute | solution.py:435
  213.6 104.0 %all-to-all-start.2 = ((bf16[8,288,1152]{2,1,0:T(8,128)(2,1)}), bf16[8,288,1152]{2,1,0:T(8,128)(2,1)}, u32[]{:S(2)}, u32[]{:S(2)}) async-start(bf16[8,288,1152]{2,1,0:T(8,128)(2,1)} %copy.69), calls=%async_computation.2 | async-start | bytes 10616832 | tf_op jit(solution)/shard_map/all_to_all | solution.py:491
  219.5 71.6 %collective-permute-start.13 = (bf16[128,2304]{1,0:T(8,128)(2,1)S(1)}, bf16[128,2304]{1,0:T(8,128)(2,1)S(1)}, u32[]{:S(2)}, u32[]{:S(2)}) collective-permute-start(bf16[128,2304]{1,0:T(8,128)(2,1)S(1)} %get-tuple-element.35), channel_id=1, source_target_pairs={{0,16},{4,20},{8,24},{12,28},{16,0},{20,4},{24,8},{28,12},{1,17},{... | collective-permute-start | bytes 1769480 | tf_op jit(solution)/shard_map/ppermute | solution.py:435
  221.5 71.2 %collective-permute-start.12 = (bf16[128,2304]{1,0:T(8,128)(2,1)S(1)}, bf16[128,2304]{1,0:T(8,128)(2,1)S(1)}, u32[]{:S(2)}, u32[]{:S(2)}) collective-permute-start(bf16[128,2304]{1,0:T(8,128)(2,1)S(1)} %get-tuple-element.35), channel_id=1, source_target_pairs={{0,8},{4,12},{8,0},{12,4},{16,24},{20,28},{24,16},{28,20},{1,9},{5... | collective-permute-start | bytes 1769480 | tf_op jit(solution)/shard_map/ppermute | solution.py:435
  317.6 65.7 %all-to-all-start.3 = ((bf16[8,288,1152]{2,1,0:T(8,128)(2,1)}), bf16[8,288,1152]{2,1,0:T(8,128)(2,1)}, u32[]{:S(2)}, u32[]{:S(2)}) async-start(bf16[8,288,1152]{2,1,0:T(8,128)(2,1)} %copy.70), calls=%async_computation.3 | async-start | bytes 10616832 | tf_op jit(solution)/shard_map/all_to_all | solution.py:491
  389.5 45.1 %collective-permute-start.17 = (bf16[512,2304]{1,0:T(8,128)(2,1)S(1)}, bf16[512,2304]{1,0:T(8,128)(2,1)}, u32[]{:S(2)}, u32[]{:S(2)}) collective-permute-start(bf16[512,2304]{1,0:T(8,128)(2,1)S(1)} %convolution_convert_fusion), channel_id=1, source_target_pairs={{0,4},{4,0},{8,12},{12,8},{16,20},{20,16},{24,28},{28,24},{1,5},{5... | collective-permute-start | bytes 7077896 | tf_op jit(solution)/shard_map/ppermute | solution.py:435
  391.2 42.4 %collective-permute-start.47 = (bf16[128,2304]{1,0:T(8,128)(2,1)S(1)}, bf16[128,2304]{1,0:T(8,128)(2,1)S(1)}, u32[]{:S(2)}, u32[]{:S(2)}) collective-permute-start(bf16[128,2304]{1,0:T(8,128)(2,1)S(1)} %get-tuple-element.35), channel_id=1, source_target_pairs={{0,2},{1,3},{2,0},{3,1},{4,6},{5,7},{6,4},{7,5},{8,10},{9,11},{10,... | collective-permute-start | bytes 1769480 | tf_op jit(solution)/shard_map/ppermute | solution.py:439
  393.8 48.3 %collective-permute-start.48 = (bf16[128,2304]{1,0:T(8,128)(2,1)S(1)}, bf16[128,2304]{1,0:T(8,128)(2,1)S(1)}, u32[]{:S(2)}, u32[]{:S(2)}) collective-permute-start(bf16[128,2304]{1,0:T(8,128)(2,1)S(1)} %get-tuple-element.35), channel_id=1, source_target_pairs={{0,3},{1,2},{2,1},{3,0},{4,7},{5,6},{6,5},{7,4},{8,11},{9,10},{10,... | collective-permute-start | bytes 1769480 | tf_op jit(solution)/shard_map/ppermute | solution.py:439
  443.0 56.7 %collective-permute-start.50 = (bf16[384,2304]{1,0:T(8,128)(2,1)S(1)}, bf16[384,2304]{1,0:T(8,128)(2,1)S(1)}, u32[]{:S(2)}, u32[]{:S(2)}) collective-permute-start(bf16[384,2304]{1,0:T(8,128)(2,1)S(1)} %get-tuple-element.107), channel_id=1, source_target_pairs={{0,16},{4,20},{8,24},{12,28},{16,0},{20,4},{24,8},{28,12},{1,17},{... | collective-permute-start | bytes 5308424 | tf_op jit(solution)/shard_map/ppermute | solution.py:435
  443.6 57.5 %collective-permute-start.49 = (bf16[384,2304]{1,0:T(8,128)(2,1)S(1)}, bf16[384,2304]{1,0:T(8,128)(2,1)S(1)}, u32[]{:S(2)}, u32[]{:S(2)}) collective-permute-start(bf16[384,2304]{1,0:T(8,128)(2,1)S(1)} %get-tuple-element.107), channel_id=1, source_target_pairs={{0,8},{4,12},{8,0},{12,4},{16,24},{20,28},{24,16},{28,20},{1,9},{5... | collective-permute-start | bytes 5308424 | tf_op jit(solution)/shard_map/ppermute | solution.py:435
  445.1 47.3 %collective-permute-start.20 = (bf16[128,2304]{1,0:T(8,128)(2,1)S(1)}, bf16[128,2304]{1,0:T(8,128)(2,1)S(1)}, u32[]{:S(2)}, u32[]{:S(2)}) collective-permute-start(bf16[128,2304]{1,0:T(8,128)(2,1)S(1)} %pad_maximum_fusion.8), channel_id=1, source_target_pairs={{0,16},{4,20},{8,24},{12,28},{16,0},{20,4},{24,8},{28,12},{1,17},{... | collective-permute-start | bytes 1769480 | tf_op jit(solution)/shard_map/ppermute | solution.py:435
  499.8 56.1 %collective-permute-start.51 = (bf16[192,2304]{1,0:T(8,128)(2,1)S(1)}, bf16[192,2304]{1,0:T(8,128)(2,1)S(1)}, u32[]{:S(2)}, u32[]{:S(2)}) collective-permute-start(bf16[192,2304]{1,0:T(8,128)(2,1)S(1)} %slice.582), channel_id=1, source_target_pairs={{0,8},{4,12},{8,0},{12,4},{16,24},{20,28},{24,16},{28,20},{1,9},{5... | collective-permute-start | bytes 2654216 | tf_op jit(solution)/shard_map/ppermute | solution.py:435
  501.2 56.7 %collective-permute-start.52 = (bf16[192,2304]{1,0:T(8,128)(2,1)S(1)}, bf16[192,2304]{1,0:T(8,128)(2,1)S(1)}, u32[]{:S(2)}, u32[]{:S(2)}) collective-permute-start(bf16[192,2304]{1,0:T(8,128)(2,1)S(1)} %slice.583), channel_id=1, source_target_pairs={{0,16},{4,20},{8,24},{12,28},{16,0},{20,4},{24,8},{28,12},{1,17},{... | collective-permute-start | bytes 2654216 | tf_op jit(solution)/shard_map/ppermute | solution.py:435
  534.9 68.2 %collective-permute-start.26 = (bf16[512,2304]{1,0:T(8,128)(2,1)S(1)}, bf16[512,2304]{1,0:T(8,128)(2,1)S(1)}, u32[]{:S(2)}, u32[]{:S(2)}) collective-permute-start(bf16[512,2304]{1,0:T(8,128)(2,1)S(1)} %get-tuple-element.141), channel_id=1, source_target_pairs={{0,4},{4,0},{8,12},{12,8},{16,20},{20,16},{24,28},{28,24},{1,5},{5... | collective-permute-start | bytes 7077896 | tf_op jit(solution)/shard_map/ppermute | solution.py:435
  536.4 45.0 %collective-permute-start.54 = (bf16[128,2304]{1,0:T(8,128)(2,1)S(1)}, bf16[128,2304]{1,0:T(8,128)(2,1)S(1)}, u32[]{:S(2)}, u32[]{:S(2)}) collective-permute-start(bf16[128,2304]{1,0:T(8,128)(2,1)S(1)} %get-tuple-element.31), channel_id=1, source_target_pairs={{0,1},{1,0},{2,3},{3,2},{4,5},{5,4},{6,7},{7,6},{8,9},{9,8},{10,11... | collective-permute-start | bytes 1769480 | tf_op jit(solution)/shard_map/ppermute | solution.py:439
  556.9 42.4 %collective-permute-start.55 = (bf16[128,2304]{1,0:T(8,128)(2,1)S(1)}, bf16[128,2304]{1,0:T(8,128)(2,1)S(1)}, u32[]{:S(2)}, u32[]{:S(2)}) collective-permute-start(bf16[128,2304]{1,0:T(8,128)(2,1)S(1)} %get-tuple-element.31), channel_id=1, source_target_pairs={{0,2},{1,3},{2,0},{3,1},{4,6},{5,7},{6,4},{7,5},{8,10},{9,11},{10,... | collective-permute-start | bytes 1769480 | tf_op jit(solution)/shard_map/ppermute | solution.py:439
  559.0 128.9 %collective-permute-start.53 = (bf16[1536,2304]{1,0:T(8,128)(2,1)}, bf16[1536,2304]{1,0:T(8,128)(2,1)}, u32[]{:S(2)}, u32[]{:S(2)}) collective-permute-start(bf16[1536,2304]{1,0:T(8,128)(2,1)} %get-tuple-element.92), channel_id=1, source_target_pairs={{0,4},{4,0},{8,12},{12,8},{16,20},{20,16},{24,28},{28,24},{1,5},{5... | collective-permute-start | bytes 21233672 | tf_op jit(solution)/shard_map/ppermute | solution.py:435
  559.2 41.4 %collective-permute-start.56 = (bf16[128,2304]{1,0:T(8,128)(2,1)S(1)}, bf16[128,2304]{1,0:T(8,128)(2,1)S(1)}, u32[]{:S(2)}, u32[]{:S(2)}) collective-permute-start(bf16[128,2304]{1,0:T(8,128)(2,1)S(1)} %get-tuple-element.31), channel_id=1, source_target_pairs={{0,3},{1,2},{2,1},{3,0},{4,7},{5,6},{6,5},{7,4},{8,11},{9,10},{10,... | collective-permute-start | bytes 1769480 | tf_op jit(solution)/shard_map/ppermute | solution.py:439
  680.4 96.6 %collective-permute-start.61 = (bf16[1536,2304]{1,0:T(8,128)(2,1)}, bf16[1536,2304]{1,0:T(8,128)(2,1)S(1)}, u32[]{:S(2)}, u32[]{:S(2)}) collective-permute-start(bf16[1536,2304]{1,0:T(8,128)(2,1)} %get-tuple-element.88), channel_id=1, source_target_pairs={{0,4},{4,0},{8,12},{12,8},{16,20},{20,16},{24,28},{28,24},{1,5},{5... | collective-permute-start | bytes 21233672 | tf_op jit(solution)/shard_map/ppermute | solution.py:435
  763.8 76.7 %collective-permute-start.38 = (f32[1024,128]{0,1:T(8,128)}, f32[1024,128]{0,1:T(8,128)}, u32[]{:S(2)}, u32[]{:S(2)}) collective-permute-start(f32[1024,128]{0,1:T(8,128)} %constant_dynamic-slice_fusion), channel_id=1, source_target_pairs={{0,4},{4,0},{8,12},{12,8},{16,20},{20,16},{24,28},{28,24},{1,5},{5... | collective-permute-start | bytes 1572872 | tf_op jit(solution)/shard_map/ppermute | solution.py:435
  770.4 72.3 %collective-permute-start.37 = (f32[1024,256]{0,1:T(8,128)}, f32[1024,256]{0,1:T(8,128)}, u32[]{:S(2)}, u32[]{:S(2)}) collective-permute-start(f32[1024,256]{0,1:T(8,128)} %convolution_multiply_fusion.12), channel_id=1, source_target_pairs={{0,4},{4,0},{8,12},{12,8},{16,20},{20,16},{24,28},{28,24},{1,5},{5... | collective-permute-start | bytes 3145736 | tf_op jit(solution)/shard_map/ppermute | solution.py:435
  854.1 51.9 %collective-permute-start.44 = (bf16[8,2,72,768]{3,2,1,0:T(8,128)(2,1)S(1)}, bf16[8,2,72,768]{3,2,1,0:T(8,128)(2,1)S(1)}, u32[]{:S(2)}, u32[]{:S(2)}) collective-permute-start(bf16[8,2,72,768]{3,2,1,0:T(8,128)(2,1)S(1)} %fusion.51), channel_id=1, source_target_pairs={{0,1},{1,0},{2,3},{3,2},{4,5},{5,4},{6,7},{7,6},{8,9},{9,8},{10,11... | collective-permute-start | bytes 5308424 | tf_op jit(solution)/shard_map/ppermute | solution.py:439
  914.0 60.1 %collective-permute-start.39 = (bf16[512,2304]{1,0:T(8,128)(2,1)}, bf16[512,2304]{1,0:T(8,128)(2,1)}, u32[]{:S(2)}, u32[]{:S(2)}) collective-permute-start(bf16[512,2304]{1,0:T(8,128)(2,1)} %fusion.42), channel_id=1, source_target_pairs={{0,4},{4,0},{8,12},{12,8},{16,20},{20,16},{24,28},{28,24},{1,5},{5... | collective-permute-start | bytes 7077896 | tf_op jit(solution)/shard_map/ppermute | solution.py:435
  969.4 79.0 %all-to-all-start.6 = ((bf16[8,288,1152]{2,1,0:T(8,128)(2,1)}), bf16[8,288,1152]{2,1,0:T(8,128)(2,1)}, u32[]{:S(2)}, u32[]{:S(2)}) async-start(bf16[8,288,1152]{2,1,0:T(8,128)(2,1)} %bitcast.183), calls=%async_computation.6 | async-start | bytes 10616832 | tf_op jit(solution)/shard_map/all_to_all | solution.py:496
  978.4 68.4 %collective-permute-start.40 = (bf16[128,2304]{1,0:T(8,128)(2,1)S(1)}, bf16[128,2304]{1,0:T(8,128)(2,1)S(1)}, u32[]{:S(2)}, u32[]{:S(2)}) collective-permute-start(bf16[128,2304]{1,0:T(8,128)(2,1)S(1)} %pad_maximum_fusion.11), channel_id=1, source_target_pairs={{0,8},{4,12},{8,0},{12,4},{16,24},{20,28},{24,16},{28,20},{1,9},{5... | collective-permute-start | bytes 1769480 | tf_op jit(solution)/shard_map/ppermute | solution.py:435
  993.1 86.0 %collective-permute-start.42 = (bf16[128,2304]{1,0:T(8,128)(2,1)S(1)}, bf16[128,2304]{1,0:T(8,128)(2,1)S(1)}, u32[]{:S(2)}, u32[]{:S(2)}) collective-permute-start(bf16[128,2304]{1,0:T(8,128)(2,1)S(1)} %pad_maximum_fusion.12), channel_id=1, source_target_pairs={{0,16},{4,20},{8,24},{12,28},{16,0},{20,4},{24,8},{28,12},{1,17},{... | collective-permute-start | bytes 1769480 | tf_op jit(solution)/shard_map/ppermute | solution.py:435
  1048.4 74.6 %all-to-all-start.5 = ((bf16[8,288,1152]{2,1,0:T(8,128)(2,1)}), bf16[8,288,1152]{2,1,0:T(8,128)(2,1)}, u32[]{:S(2)}, u32[]{:S(2)}) async-start(bf16[8,288,1152]{2,1,0:T(8,128)(2,1)} %bitcast.182), calls=%async_computation.5 | async-start | bytes 10616832 | tf_op jit(solution)/shard_map/all_to_all | solution.py:496
  1123.1 98.1 %all-to-all-start.7 = ((bf16[8,288,1152]{2,1,0:T(8,128)(2,1)}), bf16[8,288,1152]{2,1,0:T(8,128)(2,1)}, u32[]{:S(2)}, u32[]{:S(2)}) async-start(bf16[8,288,1152]{2,1,0:T(8,128)(2,1)} %bitcast.181), calls=%async_computation.7 | async-start | bytes 10616832 | tf_op jit(solution)/shard_map/all_to_all | solution.py:496
  1127.9 61.8 %reduce-scatter.4.cloned.1.call-start = ((), (), s32[]{:S(2)}) async-start(), calls=%async_computation.10 | async-start | bytes 1327104
  1131.6 98.2 %all-gather.2.cloned.1.call-start = ((), (), s32[]{:S(2)}) async-start(), calls=%async_computation.9 | async-start | bytes 4423680 | tf_op jit(solution)/shard_map/all_gather | solution.py:689
  (134 other events, 3954.2 us)
Sparse Core Ops, SparseCore 0:
  1132.6 57.1 reduce-scatter.3
Sparse Core Ops, SparseCore 1:
  1133.8 70.8 all-gather.1

commit v2 on v1

--- a/solution.py
+++ b/solution.py
@@ -1,6 +1,10 @@
+import functools
+
 import jax
 import jax.numpy as jnp
 from jax import lax
+from jax.experimental import pallas as pl
+from jax.experimental.pallas import tpu as pltpu
 from jax.sharding import PartitionSpec as P
 
 MODEL_WIDTH = 2304
@@ -431,6 +435,14 @@
     )
 
 
+VMEM_BYTES = 56 * 1024 * 1024
+TILE_VMEM_BYTES = 28 * 1024 * 1024
+CROSS_VMEM_BYTES = 40 * 1024 * 1024
+GELU_RATE = 0.7978845608028654
+TILE = 512
+CHUNK = 768
+
+
 def seq_swap(block, bit):
     return lax.ppermute(block, "seq", [(place, place ^ bit) for place in range(8)])
 
@@ -439,6 +451,47 @@
     return lax.ppermute(block, "row", [(place, place ^ bit) for place in range(4)])
 
 
+def row_shift(block, step):
+    return lax.ppermute(
+        block, "row", [(place, place + step) for place in range(4) if 0 <= place + step < 4]
+    )
+
+
+def join_kernel(place_ref, own, *refs):
+    below, above, (out_ref, sems) = refs[:3], refs[3:6], refs[6:]
+
+    def join(place):
+        copies = [
+            pltpu.make_async_copy(
+                own if q == place else below[place - q - 1] if q < place else above[q - place - 1],
+                out_ref.at[:, q],
+                sems.at[q],
+            )
+            for q in range(4)
+        ]
+        for copy in copies:
+            copy.start()
+        for copy in copies:
+            copy.wait()
+
+    for place in range(4):
+        pl.when(place_ref[0] == place)(functools.partial(join, place))
+
+
+def ordered_quarters(own, below, above):
+    _, rows, columns = own.shape
+    joined = pl.pallas_call(
+        join_kernel,
+        in_specs=[pl.BlockSpec(memory_space=pltpu.SMEM)] + [pl.BlockSpec(memory_space=pl.ANY)] * 7,
+        out_specs=pl.BlockSpec(memory_space=pltpu.VMEM),
+        out_shape=jax.ShapeDtypeStruct((8, 4, rows, columns), own.dtype),
+        scratch_shapes=[pltpu.SemaphoreType.DMA((4,))],
+        compiler_params=pltpu.CompilerParams(vmem_limit_bytes=TILE_VMEM_BYTES),
+        cost_estimate=pl.CostEstimate(flops=1, bytes_accessed=1, transcendentals=0),
+    )(jnp.full((1,), lax.axis_index("row"), jnp.int32), own, *below, *above)
+    return joined.reshape(32 * rows, columns)
+
+
 def bf(values):
     return values.astype(jnp.bfloat16)
 
@@ -450,14 +503,24 @@
 RELATIVE = (0, 2, 4, 6, 1, 3, 5, 7)
 
 
-def gather_row(block):
+def pin(*values):
+    return lax.optimization_barrier(values)
+
+
+def gather_near(block):
+    return block, seq_swap(block, 2), seq_swap(block, 4)
+
+
+def gather_far(block, from_x, from_y):
     half = block.shape[0] // 2
-    from_x = seq_swap(block, 2)
-    from_y = seq_swap(block, 4)
     far_first = seq_swap(from_y[:half], 2)
     far_last = seq_swap(from_x[half:], 4)
-    mine = jnp.concatenate([block, from_x, from_y, far_first, far_last])
-    return jnp.concatenate([mine, seq_swap(mine, 1)])
+    return jnp.concatenate([block, from_x, from_y, far_first, far_last])
+
+
+def gather_row(block):
+    mine = gather_far(*gather_near(block))
+    return mine, seq_swap(mine, 1)
 
 
 def other_core(rows):
@@ -466,17 +529,24 @@
     return jnp.concatenate([theirs[middle:], theirs[:middle]])
 
 
-def scatter_row(partial_rows, row_count):
-    middle = row_count // 2
-    unit = row_count // 8
+def scatter_core(partial_half):
+    theirs = seq_swap(partial_half(1, jnp.bfloat16), 1)
+    return partial_half(0, jnp.float32) + wide(theirs)
+
+
+def scatter_near(mine):
+    unit = mine.shape[0] // 4
     half = unit // 2
-    theirs = seq_swap(bf(partial_rows(middle, row_count)), 1)
-    mine = partial_rows(0, middle) + wide(theirs)
     here, by_x, by_y, far = (mine[i * unit : (i + 1) * unit] for i in range(4))
     from_x = seq_swap(bf(jnp.concatenate([by_x[:half], far[:half]])), 2)
     from_y = seq_swap(bf(jnp.concatenate([by_y[half:], far[half:]])), 4)
-    last_y = seq_swap(bf(by_y[:half] + wide(from_x[half:])), 4)
-    last_x = seq_swap(bf(by_x[half:] + wide(from_y[half:])), 2)
+    return here, by_x[half:], by_y[:half], from_x, from_y
+
+
+def scatter_far(here, by_x, by_y, from_x, from_y):
+    half = here.shape[0] // 2
+    last_y = seq_swap(bf(by_y + wide(from_x[half:])), 4)
+    last_x = seq_swap(bf(by_x + wide(from_y[half:])), 2)
     return jnp.concatenate(
         [
             here[:half] + wide(from_x[:half]) + wide(last_y),
@@ -485,18 +555,83 @@
     )
 
 
-def spread_columns(code_rows):
-    rows, columns = code_rows.shape
-    blocks = code_rows.reshape(rows, 8, columns // 8).transpose(1, 0, 2)
-    return lax.all_to_all(blocks, "seq", 0, 0, tiled=True).reshape(rows * 8, columns // 8)
-
-
-def spread_rows(gradient):
-    rows, columns = gradient.shape
-    blocks = lax.all_to_all(
-        bf(gradient).reshape(8, rows // 8, columns), "seq", 0, 0, tiled=True
-    )
-    return wide(blocks.transpose(1, 0, 2).reshape(rows // 8, columns * 8))
+def scatter_row(partial_half):
+    return scatter_far(*scatter_near(scatter_core(partial_half)))
+
+
+def pack_kernel(decoders, place_ref, *refs):
+    codes, outs = refs[: len(decoders)], refs[len(decoders) :]
+    rows = [bf(wide(decode(code_ref[...]))) for decode, code_ref in zip(decoders, codes)]
+    if len(outs) == 1:
+        column = 0
+        for part in rows:
+            outs[0][0, :, column : column + part.shape[1]] = part
+            column += part.shape[1]
+    else:
+        column = 0
+        for out_ref in outs:
+            out_ref[0] = rows[0][:, column : column + out_ref.shape[2]]
+            column += out_ref.shape[2]
+
+
+def exact_eight(codes):
+    return codes
+
+
+def exact_four(codes):
+    return (codes & -16) + 8
+
+
+def exact_two(codes):
+    return (codes & -64) + 32
+
+
+def pack_codes(code_arrays, decoders, parts, part, widths=None):
+    rows = code_arrays[0].shape[0] // parts
+    columns = [codes.shape[1] // 8 for codes in code_arrays]
+    widths = widths or [sum(columns)]
+    found = pl.pallas_call(
+        functools.partial(pack_kernel, decoders),
+        grid_spec=pltpu.PrefetchScalarGridSpec(
+            num_scalar_prefetch=1,
+            grid=(8,),
+            in_specs=[pl.BlockSpec((rows, c), lambda j, p: (p[0], j)) for c in columns],
+            out_specs=[pl.BlockSpec((1, rows, w), lambda j, p: (j, 0, 0)) for w in widths],
+        ),
+        out_shape=[jax.ShapeDtypeStruct((8, rows, w), jnp.bfloat16) for w in widths],
+        compiler_params=pltpu.CompilerParams(vmem_limit_bytes=VMEM_BYTES),
+        cost_estimate=pl.CostEstimate(
+            flops=0, bytes_accessed=rows * sum(columns) * 48, transcendentals=0
+        ),
+    )(jnp.full((1,), part, jnp.int32), *code_arrays)
+    return found if len(widths) > 1 else found[0]
+
+
+def unpack_kernel(block_ref, *out_refs):
+    rows = block_ref.shape[2]
+    column = 0
+    for out_ref in out_refs:
+        end = column + out_ref.shape[1]
+        for part in range(block_ref.shape[0]):
+            out_ref[part * rows : (part + 1) * rows, :] = wide(block_ref[part, 0, :, column:end])
+        column = end
+
+
+def unpack_blocks(blocks, widths):
+    parts, _, rows, columns = blocks.shape
+    return pl.pallas_call(
+        unpack_kernel,
+        grid=(8,),
+        in_specs=[pl.BlockSpec((parts, 1, rows, columns), lambda j: (0, j, 0, 0))],
+        out_specs=[pl.BlockSpec((parts * rows, w), lambda j: (0, j)) for w in widths],
+        out_shape=[jax.ShapeDtypeStruct((parts * rows, 8 * w), jnp.float32) for w in widths],
+        compiler_params=pltpu.CompilerParams(vmem_limit_bytes=VMEM_BYTES),
+        cost_estimate=pl.CostEstimate(flops=0, bytes_accessed=6 * blocks.size, transcendentals=0),
+    )(blocks)
+
+
+def trade(blocks):
+    return lax.all_to_all(blocks, "seq", 0, 0, tiled=True)
 
 
 def dot(left, right):
@@ -517,10 +652,193 @@
     return gradient, jnp.sum(upstream * values * scale, axis=0)
 
 
-def geglu_back(gate, up, grad_mixed):
-    mixed, pull = jax.vjp(geglu, gate, up)
-    grad_gate, grad_up = pull(grad_mixed)
-    return bf(mixed), bf(grad_gate), bf(grad_up)
+def gelu_parts(values):
+    inner = GELU_RATE * (values + 0.044715 * values * values * values)
+    bent = jnp.tanh(inner)
+    slope = 0.5 * (1.0 + bent) + 0.5 * values * (1.0 - bent * bent) * GELU_RATE * (
+        1.0 + 3.0 * 0.044715 * values * values
+    )
+    return 0.5 * values * (1.0 + bent), slope
+
+
+def whole_spec(weight):
+    return pl.BlockSpec(memory_space=pltpu.VMEM)
+
+
+def tile_calls(kernel, grid, in_specs, arrays, out_specs, out_shape, scratch=()):
+    return pl.pallas_call(
+        kernel,
+        grid=grid,
+        in_specs=in_specs,
+        out_specs=out_specs,
+        out_shape=out_shape,
+        scratch_shapes=scratch,
+        compiler_params=pltpu.CompilerParams(vmem_limit_bytes=TILE_VMEM_BYTES),
+        cost_estimate=pl.CostEstimate(flops=1, bytes_accessed=1, transcendentals=0),
+    )(*arrays)
+
+
+def source_specs(count, tile, columns, steps):
+    specs = [
+        pl.BlockSpec((tile, columns), lambda i: (jnp.minimum(i, steps - 1), 0)),
+        pl.BlockSpec((tile, columns), lambda i: (jnp.maximum(i - steps, 0), 0)),
+    ]
+    return specs[:count]
+
+
+def on_source(steps, sources, action):
+    if len(sources) == 1:
+        action(sources[0][...])
+    else:
+        pl.when(pl.program_id(0) < steps)(lambda: action(sources[0][...]))
+        pl.when(pl.program_id(0) >= steps)(lambda: action(sources[1][...]))
+
+
+def up_kernel(steps, scale, *refs):
+    *sources, w_gate, w_up, mixed_ref, to_gate_ref, to_up_ref = refs
+
+    def action(rows):
+        gate = dot(rows, w_gate[...]) * scale
+        up = dot(rows, w_up[...]) * scale
+        value, slope = gelu_parts(gate)
+        mixed_ref[...] = bf(value * up)
+        to_gate_ref[...] = bf(slope * up)
+        to_up_ref[...] = bf(value)
+
+    on_source(steps, sources, action)
+
+
+def up_project(halves, w_gate, w_up, scale):
+    rows, columns = halves[0].shape
+    hidden = w_gate.shape[1]
+    steps = rows // TILE
+    return tile_calls(
+        functools.partial(up_kernel, steps, scale),
+        (len(halves) * steps,),
+        source_specs(len(halves), TILE, columns, steps) + [whole_spec(w_gate), whole_spec(w_up)],
+        (*halves, w_gate, w_up),
+        [pl.BlockSpec((TILE, hidden), lambda i: (i, 0))] * 3,
+        [jax.ShapeDtypeStruct((len(halves) * rows, hidden), jnp.bfloat16)] * 3,
+    )
+
+
+def back_kernel(steps, scale, *refs):
+    *sources, w_down, to_gate_ref, to_up_ref, gate_ref, up_ref = refs
+
+    def action(rows):
+        grad_mixed = dot(rows, w_down[...]) * scale
+        gate_ref[...] = bf(grad_mixed * wide(to_gate_ref[...]))
+        up_ref[...] = bf(grad_mixed * wide(to_up_ref[...]))
+
+    on_source(steps, sources, action)
+
+
+def back_project(halves, w_down, factors, scale):
+    rows, columns = halves[0].shape
+    hidden = w_down.shape[1]
+    steps = rows // TILE
+    part = pl.BlockSpec((TILE, hidden), lambda i: (i, 0))
+    return tile_calls(
+        functools.partial(back_kernel, steps, scale),
+        (len(halves) * steps,),
+        source_specs(len(halves), TILE, columns, steps) + [whole_spec(w_down), part, part],
+        (*halves, w_down, *factors),
+        [part] * 2,
+        [jax.ShapeDtypeStruct((len(halves) * rows, hidden), jnp.bfloat16)] * 2,
+    )
+
+
+def cross_kernel(steps, n_left, n_right, *refs):
+    lefts, rights = refs[:n_left], refs[n_left : n_left + n_right]
+    out_ref, left_buf, right_buf, total, sems = refs[n_left + n_right :]
+
+    def copies(step):
+        slot = step % 2
+        found = []
+        at = 0
+        for left, left_row, right, right_row, count in steps[step]:
+            found.append(
+                pltpu.make_async_copy(
+                    lefts[left].at[pl.ds(left_row, count)],
+                    left_buf.at[slot, pl.ds(at, count)],
+                    sems.at[slot, len(found)],
+                )
+            )
+            found.append(
+                pltpu.make_async_copy(
+                    rights[right].at[pl.ds(right_row, count)],
+                    right_buf.at[slot, pl.ds(at, count)],
+                    sems.at[slot, len(found)],
+                )
+            )
+            at += count
+        return found
+
+    for copy in copies(0):
+        copy.start()
+    chunk = out_ref.shape[2]
+    for step in range(len(steps)):
+        slot = step % 2
+        if step + 1 < len(steps):
+            for copy in copies(step + 1):
+                copy.start()
+        for copy in copies(step):
+            copy.wait()
+
+        @pl.loop(0, total.shape[0] // CHUNK)
+        def _(m):
+            columns = pl.ds(pl.multiple_of(m * CHUNK, CHUNK), CHUNK)
+            term = cross_rows(left_buf[slot, :, columns], right_buf[slot])
+            if step > 0:
+                term = term + total[columns, :]
+            total[columns, :] = term
+
+    for place in range(8):
+        for part in range(out_ref.shape[0]):
+            start = (place * out_ref.shape[0] + part) * chunk
+            out_ref[part, place] = bf(total[start : start + chunk, :])
+
+
+def cross_products(lefts, rights, steps, parts=1):
+    wide_rows, columns = lefts[0].shape[1], rights[0].shape[1]
+    depth = max(sum(piece[4] for piece in step) for step in steps)
+    pieces = max(2 * len(step) for step in steps)
+    return pl.pallas_call(
+        functools.partial(cross_kernel, steps, len(lefts), len(rights)),
+        in_specs=[pl.BlockSpec(memory_space=pl.ANY)] * (len(lefts) + len(rights)),
+        out_shape=jax.ShapeDtypeStruct((parts, 8, wide_rows // 8 // parts, columns), jnp.bfloat16),
+        scratch_shapes=[
+            pltpu.VMEM((2, depth, wide_rows), jnp.bfloat16),
+            pltpu.VMEM((2, depth, columns), jnp.bfloat16),
+            pltpu.VMEM((wide_rows, columns), jnp.float32),
+            pltpu.SemaphoreType.DMA((2, pieces)),
+        ],
+        compiler_params=pltpu.CompilerParams(vmem_limit_bytes=CROSS_VMEM_BYTES),
+        cost_estimate=pl.CostEstimate(flops=1, bytes_accessed=1, transcendentals=0),
+    )(*lefts, *rights)
+
+
+def partial_kernel(*refs):
+    out_ref, pairs = refs[-1], refs[:-1]
+    total = times_transposed(pairs[0][...], pairs[1][...])
+    for left, right in zip(pairs[2::2], pairs[3::2]):
+        total = total + times_transposed(left[...], right[...])
+    out_ref[...] = total.astype(out_ref.dtype)
+
+
+def partial_product(pairs, side, kind):
+    rows, hidden = pairs[0][0].shape
+    columns = pairs[0][1].shape[0]
+    half = rows // 2
+    left_spec = pl.BlockSpec((half, hidden), lambda i: (side, 0))
+    return tile_calls(
+        partial_kernel,
+        (1,),
+        [spec for pair in pairs for spec in (left_spec, whole_spec(pair[1]))],
+        [array for pair in pairs for array in pair],
+        pl.BlockSpec((half, columns), lambda i: (0, 0)),
+        jax.ShapeDtypeStruct((half, columns), kind),
+    )
 
 
 def plane_body(
@@ -552,20 +870,30 @@
     scale_down = code_unit * FF ** (-0.5)
     head_scale = HEAD_SIZE ** (-0.5)
 
+    row_place = lax.axis_index("row")
     model_rows = query_codes.shape[0]
-    attn_blocks = jnp.concatenate(
-        [
-            codes_eight(codes).reshape(model_rows, 8, codes.shape[1] // 8)
-            for codes in (query_codes, key_integer_codes, value_integer_codes, out_codes)
-        ],
-        axis=2,
-    )
-    attn_weights = spread_columns(attn_blocks.reshape(model_rows, -1))
+    hidden_part = gate_codes.shape[1] // 8
+
+    def both_ways(below, above):
+        return row_shift(below, 1), row_shift(above, -1)
+
+    near_tokens = gather_near(hidden_in[0])
+    down_blocks = pack_codes([down_codes], [exact_two], 4, row_place)
+    near_tokens, down_blocks = pin(near_tokens, down_blocks)
+    own_down = trade(down_blocks)
+    attn_blocks = pack_codes(
+        [query_codes, key_integer_codes, value_integer_codes, out_codes], [exact_eight] * 4, 1, 0
+    )
+    attn_blocks, own_down = pin(attn_blocks, own_down)
+    attn_weights, gate_blocks, up_blocks, down_one = pin(
+        trade(attn_blocks).reshape(width, 3 * head),
+        pack_codes([gate_codes], [exact_four], 1, 0),
+        pack_codes([up_codes], [exact_four], 1, 0),
+        both_ways(own_down, own_down),
+    )
+    gate_rows = trade(gate_blocks)
     w_attn_in = attn_weights[:, : 2 * head]
     w_out = attn_weights[:, 2 * head :]
-    w_gate = spread_columns(codes_four(gate_codes))
-    w_up = spread_columns(codes_four(up_codes))
-    w_down = spread_columns(codes_two(down_codes))
 
     token_blocks = [(place ^ k) * block_rows + jnp.arange(block_rows) for k in RELATIVE]
     token_index = jnp.concatenate(token_blocks).astype(jnp.int32)
@@ -579,7 +907,8 @@
 
     tokens = wide(hidden_in[0])
     upstream = wide(cotangent[0])
-    row_tokens = gather_row(hidden_in[0])
+    tokens_mine = gather_far(*near_tokens)
+    row_tokens = jnp.concatenate([tokens_mine, seq_swap(tokens_mine, 1)])
     normed_in = bf(norm_gain(wide(row_tokens), gain_attn_in))
     linear = dot(normed_in, w_attn_in)
     query = bf(turn(linear[:, :head] * scale_qk, cosine, sine))
@@ -602,44 +931,138 @@
     totals = jnp.sum(weights, axis=-1, keepdims=True)
     attended_wide = dot(bf(weights), value) / totals
     attended = bf(attended_wide)
-    attn_proj = scale_out * scatter_row(
-        lambda a, b: times_transposed(attended[a:b], w_out), row_length
-    )
+    attended, down_two = pin(attended, both_ways(*down_one))
+    near_half = row_length // 2
+    attn_core = scatter_core(
+        lambda side, kind: times_transposed(
+            attended[side * near_half :][:near_half], w_out
+        ).astype(kind)
+    )
+    attn_core, gate_rows = pin(attn_core, gate_rows)
+    attn_near, down_three = pin(scatter_near(attn_core), both_ways(*down_two))
+    attn_proj, up_blocks = pin(scale_out * scatter_far(*attn_near), up_blocks)
+    up_rows = trade(up_blocks)
     middle = tokens + norm_gain(attn_proj, gain_attn_out)
     normed_mid = bf(norm_gain(middle, gain_ffw_in))
 
-    row_mid = gather_row(normed_mid)
-    gate = dot(row_mid, w_gate) * scale_in
-    up = dot(row_mid, w_up) * scale_in
-    mixed = bf(geglu(gate, up))
-    ffn_proj = scale_down * scatter_row(
-        lambda a, b: times_transposed(mixed[a:b], w_down), row_length
-    )
+    mid_near, up_rows, mid_one, mid_two, mid_three = pin(
+        gather_near(normed_mid),
+        up_rows,
+        row_swap(normed_mid, 1),
+        row_swap(normed_mid, 2),
+        row_swap(normed_mid, 3),
+    )
+    mid_mine = gather_far(*mid_near)
+    mid_mine, mid_theirs, w_down = pin(
+        mid_mine,
+        seq_swap(mid_mine, 1),
+        ordered_quarters(own_down, *zip(down_one, down_two, down_three)),
+    )
+    w_gate, w_up = gate_rows.reshape(width, hidden_part), up_rows.reshape(width, hidden_part)
+
+    def up_again(*halves):
+        return up_project(halves, w_gate, w_up, scale_in)
+
+    def back_again(halves, factors):
+        return back_project(halves, w_down, factors, scale_down)
+
+    (mixed, *factors), pair_mid_near = pin(
+        up_again(mid_mine, mid_theirs), gather_near(jnp.concatenate([mid_one, mid_two]))
+    )
+    ffn_core, pair_mid_mine = pin(
+        scatter_core(lambda side, kind: partial_product([(mixed, w_down)], side, kind)),
+        gather_far(*pair_mid_near),
+    )
+    ffn_near, pair_mid_theirs = pin(scatter_near(ffn_core), seq_swap(pair_mid_mine, 1))
+    ffn_proj, third_mid_near = pin(scale_down * scatter_far(*ffn_near), gather_near(mid_three))
     block_out = bf(middle + norm_gain(ffn_proj, gain_ffw_out))
     grad_ffn, grad_gain_four = norm_back(ffn_proj, gain_ffw_out, upstream)
     grad_ffn_low = bf(grad_ffn)
-
-    others_mid = gather_row(jnp.concatenate([row_swap(normed_mid, bit) for bit in (1, 2, 3)]))
-    others_ffn = gather_row(jnp.concatenate([row_swap(grad_ffn_low, bit) for bit in (1, 2, 3)]))
-
-    row_ffn = gather_row(grad_ffn_low)
-    grad_mixed = dot(row_ffn, w_down) * scale_down
-    _, grad_gate, grad_up = geglu_back(gate, up, grad_mixed)
-    grad_mid = scale_in * scatter_row(
-        lambda a, b: times_transposed(grad_gate[a:b], w_gate)
-        + times_transposed(grad_up[a:b], w_up),
-        row_length,
+    grad_near, grad_one, third_mid_mine, (mine_mixed, *mine_factors) = pin(
+        gather_near(grad_ffn_low),
+        row_swap(grad_ffn_low, 1),
+        gather_far(*third_mid_near),
+        up_again(pair_mid_mine),
+    )
+    grad_mine = gather_far(*grad_near)
+    grad_mine, grad_theirs, grad_two, third_mid_theirs, (theirs_mixed, *theirs_factors) = pin(
+        grad_mine,
+        seq_swap(grad_mine, 1),
+        row_swap(grad_ffn_low, 2),
+        seq_swap(third_mid_mine, 1),
+        up_again(pair_mid_theirs),
+    )
+    grads_hidden, pair_grad_near = pin(
+        back_again((grad_mine, grad_theirs), factors),
+        gather_near(jnp.concatenate([grad_one, grad_two])),
+    )
+    pairs = list(zip(grads_hidden, (w_gate, w_up)))
+    mid_core, pair_grad_mine, grad_three = pin(
+        scatter_core(lambda side, kind: partial_product(pairs, side, kind)),
+        gather_far(*pair_grad_near),
+        row_swap(grad_ffn_low, 3),
+    )
+    sum_near, third_grad_near, (third_mixed, *third_factors), pair_grad_theirs, mine_hidden = pin(
+        scatter_near(mid_core),
+        gather_near(grad_three),
+        up_again(third_mid_mine, third_mid_theirs),
+        seq_swap(pair_grad_mine, 1),
+        back_again((pair_grad_mine,), mine_factors),
+    )
+    third_grad_mine = gather_far(*third_grad_near)
+    grad_mid, third_grad_mine, third_grad_theirs, theirs_hidden = pin(
+        scale_in * scatter_far(*sum_near),
+        third_grad_mine,
+        seq_swap(third_grad_mine, 1),
+        back_again((pair_grad_theirs,), theirs_factors),
     )
     grad_middle_part, grad_gain_three = norm_back(middle, gain_ffw_in, grad_mid)
     grad_middle = upstream + grad_middle_part
     grad_proj, grad_gain_two = norm_back(attn_proj, gain_attn_out, grad_middle)
 
-    row_proj = gather_row(bf(grad_proj))
+    row_half = row_length // 2
+    mids = (mid_mine, mid_theirs, pair_mid_mine, pair_mid_theirs, third_mid_mine, third_mid_theirs)
+    outs = (
+        grad_mine,
+        grad_theirs,
+        pair_grad_mine,
+        pair_grad_theirs,
+        third_grad_mine,
+        third_grad_theirs,
+    )
+    steps = (
+        ((0, 0, 0, 0, row_half), (1, 0, 0, row_half, row_half)),
+        ((2, 0, 1, 0, row_length),),
+        ((3, 0, 2, 0, row_length),),
+        ((4, 0, 3, 0, row_half), (5, 0, 3, row_half, row_half)),
+    )
+    proj_near, down_blocks, third_grads = pin(
+        gather_near(bf(grad_proj)),
+        cross_products(outs, (mixed, mine_mixed, theirs_mixed, third_mixed), steps),
+        (third_grad_mine, third_grad_theirs),
+    )
+    proj_mine, down_blocks = pin(gather_far(*proj_near), down_blocks)
+    down_blocks = trade(down_blocks[0])
+    row_proj = jnp.concatenate([proj_mine, seq_swap(proj_mine, 1)])
+
+    def halve(terms, bit, axis, side):
+        kept = lax.dynamic_index_in_dim(terms, side, axis, keepdims=False)
+        sent = lax.dynamic_index_in_dim(terms, 1 - side, axis, keepdims=False)
+        return bf(wide(kept) + wide(row_swap(sent, bit)))
+
+    def quarters_of(part):
+        return bf(part).reshape(8, 2, 2, model_rows // 4, part.shape[1])
+
+    low_bit, high_bit = row_place % 2, row_place // 2
+
     grad_attended = bf(dot(row_proj, w_out) * scale_out)
     delta = jnp.sum(wide(grad_attended) * attended_wide, axis=-1, keepdims=True)
     probs = weights / totals
     grad_probs = times_transposed(grad_attended, value)
     grad_raw = bf(probs * (grad_probs - delta) * (1.0 - bend * bend))
+    grad_raw, third_grads = pin(grad_raw, third_grads)
+    third_hidden = back_again(third_grads, third_factors)
+    gate_terms, up_terms = zip(grads_hidden, mine_hidden, theirs_hidden, third_hidden)
     grad_query = bf(turn(dot(grad_raw, key) * head_scale, cosine, -sine))
     key_part = cross_rows(grad_raw, query) * head_scale
     value_part = cross_rows(bf(probs), grad_attended)
@@ -651,60 +1074,62 @@
     grad_key = bf(own_half(turn(key_sum, cosine, -sine), core))
     grad_value = bf(own_half(value_part, core) + other_core(own_half(value_part, 1 - core)))
     grad_linear = jnp.concatenate([grad_query, grad_key, grad_value], axis=1)
-    scaled_linear = (grad_linear[:, : head + half], grad_linear[:, head + half :])
-    grad_in = scatter_row(
-        lambda a, b: scale_qk * times_transposed(scaled_linear[0][a:b], w_attn_in[:, : head + half])
-        + scale_in * times_transposed(scaled_linear[1][a:b], w_attn_in[:, head + half :]),
-        row_length,
+    grad_linear, down_blocks, gate_blocks, up_terms = pin(
+        grad_linear, down_blocks, cross_products(mids, gate_terms, steps), up_terms
+    )
+    gate_blocks = trade(gate_blocks[0])
+
+    def grad_in_half(side, kind):
+        rows = grad_linear[side * near_half :][:near_half]
+        total = scale_qk * times_transposed(
+            rows[:, : head + half], w_attn_in[:, : head + half]
+        ) + scale_in * times_transposed(rows[:, head + half :], w_attn_in[:, head + half :])
+        return total.astype(kind)
+
+    in_core, in_sum, out_sum, up_terms = pin(
+        scatter_core(grad_in_half),
+        halve(quarters_of(cross_rows(normed_in, grad_linear)), 1, 2, low_bit),
+        halve(quarters_of(cross_rows(row_proj, attended)), 1, 2, low_bit),
+        up_terms,
+    )
+    in_sum, out_sum, up_blocks, gate_blocks, in_near = pin(
+        halve(in_sum, 2, 1, high_bit),
+        halve(out_sum, 2, 1, high_bit),
+        cross_products(mids, up_terms, steps),
+        gate_blocks,
+        scatter_near(in_core),
+    )
+    grad_in, sums = pin(
+        scatter_far(*in_near), trade(jnp.concatenate([in_sum, out_sum], axis=2))
     )
     grad_tokens, grad_gain_one = norm_back(tokens, gain_attn_in, grad_in)
     grad_input = grad_middle + grad_tokens
-
-    other_gate = dot(others_mid, w_gate) * scale_in
-    other_up = dot(others_mid, w_up) * scale_in
-    other_grad = dot(others_ffn, w_down) * scale_down
-    other_mixed, other_grad_gate, other_grad_up = geglu_back(other_gate, other_up, other_grad)
-    grad_w_down = spread_rows(cross_rows(row_ffn, mixed) + cross_rows(others_ffn, other_mixed))
-    grad_w_gate = spread_rows(
-        cross_rows(row_mid, grad_gate) + cross_rows(others_mid, other_grad_gate)
-    )
-    grad_w_up = spread_rows(cross_rows(row_mid, grad_up) + cross_rows(others_mid, other_grad_up))
-
-    own_part = jnp.concatenate(
-        [cross_rows(normed_in, grad_linear), cross_rows(row_proj, attended)], axis=1
-    )
-    columns = own_part.shape[1]
-    quarter = model_rows // 4
-    row_place = lax.axis_index("row")
-    low_bit, high_bit = row_place % 2, row_place // 2
-    quarters = bf(own_part).reshape(8, 2, 2, quarter, columns)
-
-    def halve(terms, bit, axis, side):
-        kept = lax.dynamic_index_in_dim(terms, side, axis, keepdims=False)
-        sent = lax.dynamic_index_in_dim(terms, 1 - side, axis, keepdims=False)
-        return bf(wide(kept) + wide(row_swap(sent, bit)))
-
-    summed = halve(halve(quarters, 1, 2, low_bit), 2, 1, high_bit)
-    blocks = lax.all_to_all(summed, "seq", 0, 0, tiled=True).transpose(1, 0, 2)
-    blocks = wide(lax.all_gather(blocks, "row", axis=0, tiled=True))
-    cuts = (0, head, head + half, 2 * head, 3 * head)
-    attn_grads = [
-        blocks[:, :, a:b].reshape(model_rows, 8 * (b - a)) for a, b in zip(cuts, cuts[1:])
-    ]
-
-    gain_terms = jnp.stack(
-        [grad_gain_one, grad_gain_two, grad_gain_three, grad_gain_four], axis=1
-    )
-    gains = lax.psum(
-        lax.psum_scatter(gain_terms, "seq", scatter_dimension=0, tiled=True), "row"
-    )
+    gain_terms = jnp.stack([grad_gain_one, grad_gain_two, grad_gain_three, grad_gain_four])
+    gain_blocks = trade(gain_terms.reshape(4, 8, model_rows).transpose(1, 0, 2))
+    gain_blocks, up_blocks = pin(gain_blocks, up_blocks)
+    up_blocks = trade(up_blocks[0])
+
+    def double(blocks, bit, side):
+        both_sides = jnp.stack([blocks, row_swap(blocks, bit)])
+        return jnp.where(side == 0, both_sides, both_sides[::-1])
+
+    gains = jnp.sum(gain_blocks, axis=0)
+    gains = gains + row_swap(gains, 1)
+    blocks, gains = pin(double(sums, 2, high_bit), gains + row_swap(gains, 2))
+    blocks = double(blocks, 1, low_bit).transpose(1, 0, 2, 3, 4)
+    attn_grads = unpack_blocks(blocks.reshape(4, *sums.shape), [head, half, half, head])
+    grad_w_gate, grad_w_up, grad_w_down = (
+        unpack_blocks(blocks, [hidden_part])[0]
+        for blocks in (gate_blocks[None], up_blocks[None], down_blocks[None])
+    )
+
     return (
         block_out[None],
         grad_input[None],
-        gains[:, 0],
-        gains[:, 1],
-        gains[:, 2],
-        gains[:, 3],
+        gains[0],
+        gains[1],
+        gains[2],
+        gains[3],
         attn_grads[0],
         attn_grads[1],
         attn_grads[2],

time: 1250 us -> 1000 us (0.80)
  Pallas kernels: 0 us -> 286 us
  matrix products: 317 us -> 51 us
  waiting for transfers between devices: 578 us -> 384 us
  local copies, waits for them, and re-layouts: 110 us -> 62.4 us
  other arithmetic: 82.8 us -> 66.5 us
  between operations: 17.8 us -> 3.8 us
    pallas_call x0 -> x24, Pallas kernels: none -> 286 us  [the longest x12 129 us: tile_calls(): pl.pallas_call(kernel, grid=grid, in_specs=in_specs, out_specs=out_specs,...]
    dot_general x10 -> x4, matrix products: 136 us -> 13.3 us  [cross_rows(): lax.dot_general(left_side, right_side, (((0,), (0,)), ((), ())), preferre...]
    ppermute x54 -> x64, waiting for transfers between devices: 338 us -> 221 us  [seq_swap(): lax.ppermute(block, 'seq', [(place, place ^ bit) for place in range(8)])]
    dot_general x10 -> x4, matrix products: 122 us -> 12.8 us  [dot(): return jnp.dot(left, right, preferred_element_type=jnp.float32)]
    unnamed x3 -> x0, waiting for transfers between devices: 51 us -> none
    ppermute x0 -> x6, waiting for transfers between devices: none -> 41.2 us  [row_shift(): lax.ppermute(block, 'row', [(place, place + step) for place in range(4) i...]
    dot_general x14 -> x8, matrix products: 58.7 us -> 24.8 us  [times_transposed(): lax.dot_general(left_side, right_side, (((1,), (1,)), ((), ())), preferre...]
    ppermute x8 -> x14, waiting for transfers between devices: 121 us -> 87.3 us  [row_swap(): lax.ppermute(block, 'row', [(place, place ^ bit) for place in range(4)])]
  transfers between devices with their start and end apart: 72 -> 92, of which waited for: 34 -> 47; matrix products, arithmetic and copies ran while one was open for 36% -> 12% of each run, Pallas kernels for 0% -> 27%
where the time goes in v2:
time: 1000 us; the launch traced here: 992 us
  waiting for transfers between devices  384 us (38%)
  Pallas kernels  286 us (29%)
  starting transfers between devices  131 us (13%)
  other arithmetic  66.5 us (7%)
  local copies, waits for them, and re-layouts  62.4 us (6%)
  matrix products  51 us (5%)
    ppermute x64, waiting for transfers between devices, seq_swap(): lax.ppermute(block, 'seq', [(place, place ^ bit) for place in range(8)])  221 us
    pallas_call x12, Pallas kernels, tile_calls(): pl.pallas_call(kernel, grid=grid, in_specs=in_specs, out_specs=out_specs,...  129 us
    pallas_call x3, Pallas kernels, cross_products(): pl.pallas_call(functools.partial(cross_kernel, steps, len(lefts), len(rig...  93.9 us
    ppermute x14, waiting for transfers between devices, row_swap(): lax.ppermute(block, 'row', [(place, place ^ bit) for place in range(4)])  87.3 us
    ppermute x64, starting transfers between devices, seq_swap(): lax.ppermute(block, 'seq', [(place, place ^ bit) for place in range(8)])  56.9 us
    ppermute x6, waiting for transfers between devices, row_shift(): lax.ppermute(block, 'row', [(place, place + step) for place in range(4) i...  41.2 us
    unnamed x316, local copies, waits for them, and re-layouts  36.7 us
    all_to_all x8, starting transfers between devices, trade(): return lax.all_to_all(blocks, 'seq', 0, 0, tiled=True)  36.5 us
  transfers between devices with their start and end apart: 92, of which 47 were waited for; matrix products, arithmetic and copies ran while one was open for 12% of the time, Pallas kernels for 27%

profile of v2, /device:TPU:0, one launch (start us, length us, event | category | flops | bytes accessed | tf_op | source)
XLA Modules:
  0.0 992.5 jit_solution(11635258767766494007)
XLA Ops:
  29.1 16.9 %collective-permute-done.2 = bf16[64,2304]{1,0:T(8,128)(2,1)S(1)} collective-permute-done((bf16[64,2304]{1,0:T(8,128)(2,1)S(1)}, bf16[64,2304]{1,0:T(8,128)(2,1)S(1)}, u32[]{:S(2)}, u32[]{:S(2)}) %collective-permute-start.2) | collective-permute-done | bytes 294944 | tf_op jit(solution)/shard_map/ppermute | solution.py:447
  59.4 8.8 shard_map.239
  68.2 8.8 shard_map.240
  88.9 20.9 %collective-permute-done.5.refs_0_ = bf16[8,72,1152]{2,1,0:T(8,128)(2,1)S(1)} collective-permute-done((bf16[8,72,1152]{2,1,0:T(8,128)(2,1)S(1)}, bf16[8,72,1152]{2,1,0:T(8,128)(2,1)S(1)}, u32[]{:S(2)}, u32[]{:S(2)}) %collective-permute-start.5) | collective-permute-done | bytes 1327136 | tf_op jit(solution)/shard_map/ppermute | solution.py:455
  144.8 9.7 collective-permute-done.9.refs_1_
  171.6 22.5 %all-to-all-done.2 = bf16[8,288,1152]{2,1,0:T(8,128)(2,1)} async-done(((bf16[8,288,1152]{2,1,0:T(8,128)(2,1)}), bf16[8,288,1152]{2,1,0:T(8,128)(2,1)}, u32[]{:S(2)}, u32[]{:S(2)}) %all-to-all-start.2) | async-done | bytes 5308448 | tf_op jit(solution)/shard_map/all_to_all | solution.py:634
  199.3 11.9 %collective-permute-done.12 = bf16[128,2304]{1,0:T(8,128)(2,1)S(1)} collective-permute-done((bf16[128,2304]{1,0:T(8,128)(2,1)S(1)}, bf16[128,2304]{1,0:T(8,128)(2,1)S(1)}, u32[]{:S(2)}, u32[]{:S(2)}) %collective-permute-start.12) | collective-permute-done | bytes 589856 | tf_op jit(solution)/shard_map/ppermute | solution.py:447
  241.4 58.2 %collective-permute-done.18 = bf16[128,2304]{1,0:T(8,128)(2,1)S(1)} collective-permute-done((bf16[128,2304]{1,0:T(8,128)(2,1)S(1)}, bf16[128,2304]{1,0:T(8,128)(2,1)S(1)}, u32[]{:S(2)}, u32[]{:S(2)}) %collective-permute-start.18) | collective-permute-done | bytes 589856 | tf_op jit(solution)/shard_map/ppermute | solution.py:447
  318.6 20.2 %shard_map.242 = (bf16[1024,1152]{1,0:T(8,128)(2,1)S(1)}, bf16[1024,1152]{1,0:T(8,128)(2,1)S(1)}, bf16[1024,1152]{1,0:T(8,128)(2,1)S(1)}) custom-call(bf16[512,2304]{1,0:T(8,128)(2,1)S(1)} %constant_dynamic-update-slice_fusion.12.refs_0_, bf16[512,2304]{1,0:T(8,128)(2,1)S(1)} %collective-permute-done.25.refs_1_, bf16[2304,1152]{1,0:T(8,128)(2,1)} %bitcast.6.refs_2_.refs_1_, ...), custom_call_target="tpu_custom_call" | custom-call | flops 1 | bytes 1 | tf_op jit(solution)/shard_map/pallas_call | solution.py:669
  351.8 13.3 %collective-permute-done.29 = bf16[128,2304]{1,0:T(8,128)(2,1)S(1)} collective-permute-done((bf16[128,2304]{1,0:T(8,128)(2,1)S(1)}, bf16[128,2304]{1,0:T(8,128)(2,1)S(1)}, u32[]{:S(2)}, u32[]{:S(2)}) %collective-permute-start.29) | collective-permute-done | bytes 589856 | tf_op jit(solution)/shard_map/ppermute | solution.py:447
  369.7 13.6 %collective-permute-done.31 = bf16[128,2304]{1,0:T(8,128)(2,1)S(1)} collective-permute-done((bf16[128,2304]{1,0:T(8,128)(2,1)S(1)}, bf16[128,2304]{1,0:T(8,128)(2,1)S(1)}, u32[]{:S(2)}, u32[]{:S(2)}) %collective-permute-start.31) | collective-permute-done | bytes 589856 | tf_op jit(solution)/shard_map/ppermute | solution.py:447
  387.9 17.6 %shard_map.245 = (bf16[1024,1152]{1,0:T(8,128)(2,1)S(1)}, bf16[1024,1152]{1,0:T(8,128)(2,1)S(1)}, bf16[1024,1152]{1,0:T(8,128)(2,1)S(1)}) custom-call(bf16[1024,2304]{1,0:T(8,128)(2,1)S(1)} %constant_dynamic-update-slice_fusion.19.refs_0_.refs_2_, bf16[2304,1152]{1,0:T(8,128)(2,1)} %bitcast.6.refs_2_.refs_1_, bf16[2304,1152]{1,0:T(8,128)(2,1)} %bitcast.7.refs_3_.refs_2_), custom_call_target="tpu_custom_call" | custom-call | flops 1 | bytes 1 | tf_op jit(solution)/shard_map/pallas_call | solution.py:669
  419.8 12.1 %collective-permute-done.41 = bf16[64,2304]{1,0:T(8,128)(2,1)S(1)} collective-permute-done((bf16[64,2304]{1,0:T(8,128)(2,1)S(1)}, bf16[64,2304]{1,0:T(8,128)(2,1)S(1)}, u32[]{:S(2)}, u32[]{:S(2)}) %collective-permute-start.41) | collective-permute-done | bytes 294944 | tf_op jit(solution)/shard_map/ppermute | solution.py:447
  444.9 17.3 %shard_map.246 = (bf16[1024,1152]{1,0:T(8,128)(2,1)S(1)}, bf16[1024,1152]{1,0:T(8,128)(2,1)S(1)}, bf16[1024,1152]{1,0:T(8,128)(2,1)S(1)}) custom-call(bf16[1024,2304]{1,0:T(8,128)(2,1)S(1)} %collective-permute-done.33.refs_0_.refs_3_, bf16[2304,1152]{1,0:T(8,128)(2,1)} %bitcast.6.refs_2_.refs_1_, bf16[2304,1152]{1,0:T(8,128)(2,1)} %bitcast.7.refs_3_.refs_2_), custom_call_target="tpu_custom_call" | custom-call | flops 1 | bytes 1 | tf_op jit(solution)/shard_map/pallas_call | solution.py:669
  492.0 12.3 %collective-permute-done.48 = bf16[256,2304]{1,0:T(8,128)(2,1)S(1)} collective-permute-done((bf16[256,2304]{1,0:T(8,128)(2,1)}, bf16[256,2304]{1,0:T(8,128)(2,1)S(1)}, u32[]{:S(2)}, u32[]{:S(2)}) %collective-permute-start.48) | collective-permute-done | bytes 1179680 | tf_op jit(solution)/shard_map/ppermute | solution.py:447
  505.6 10.4 %shard_map.249 = bf16[512,2304]{1,0:T(8,128)(2,1)S(1)} custom-call(bf16[1024,1152]{1,0:T(8,128)(2,1)S(1)} %get-tuple-element.244.refs_0_.refs_6_, bf16[2304,1152]{1,0:T(8,128)(2,1)} %bitcast.6.refs_2_.refs_1_, bf16[1024,1152]{1,0:T(8,128)(2,1)S(1)} %get-tuple-element.305.refs_2_.refs_6_, bf16[2304,1152]{1,0:T(8,128)(2,1)} %bitcast.7.refs_3_.refs_2_), custom_call_target="tpu_custom_call" | custom-call | flops 1 | bytes 1 | tf_op jit(solution)/shard_map/pallas_call | solution.py:669
  519.2 10.4 %shard_map.248 = f32[512,2304]{1,0:T(8,128)S(1)} custom-call(bf16[1024,1152]{1,0:T(8,128)(2,1)S(1)} %get-tuple-element.244.refs_0_.refs_6_, bf16[2304,1152]{1,0:T(8,128)(2,1)} %bitcast.6.refs_2_.refs_1_, bf16[1024,1152]{1,0:T(8,128)(2,1)S(1)} %get-tuple-element.305.refs_2_.refs_6_, bf16[2304,1152]{1,0:T(8,128)(2,1)} %bitcast.7.refs_3_.refs_2_), custom_call_target="tpu_custom_call" | custom-call | flops 1 | bytes 1 | tf_op jit(solution)/shard_map/pallas_call | solution.py:669
  532.0 13.1 %collective-permute-done.51 = bf16[128,2304]{1,0:T(8,128)(2,1)S(1)} collective-permute-done((bf16[128,2304]{1,0:T(8,128)(2,1)S(1)}, bf16[128,2304]{1,0:T(8,128)(2,1)S(1)}, u32[]{:S(2)}, u32[]{:S(2)}) %collective-permute-start.51) | collective-permute-done | bytes 589856 | tf_op jit(solution)/shard_map/ppermute | solution.py:447
  548.9 17.8 %shard_map.250 = (bf16[1024,1152]{1,0:T(8,128)(2,1)S(1)}, bf16[1024,1152]{1,0:T(8,128)(2,1)S(1)}, bf16[1024,1152]{1,0:T(8,128)(2,1)S(1)}) custom-call(bf16[512,2304]{1,0:T(8,128)(2,1)S(1)} %constant_dynamic-update-slice_fusion.24.refs_0_.refs_4_, bf16[512,2304]{1,0:T(8,128)(2,1)S(1)} %copy-done.17, bf16[2304,1152]{1,0:T(8,128)(2,1)} %bitcast.6.refs_2_.refs_1_, ...), custom_call_target="tpu_custom_call" | custom-call | flops 1 | bytes 1 | tf_op jit(solution)/shard_map/pallas_call | solution.py:669
  583.2 16.5 %collective-permute-done.54 = bf16[128,2304]{1,0:T(8,128)(2,1)S(1)} collective-permute-done((bf16[128,2304]{1,0:T(8,128)(2,1)S(1)}, bf16[128,2304]{1,0:T(8,128)(2,1)S(1)}, u32[]{:S(2)}, u32[]{:S(2)}) %collective-permute-start.54) | collective-permute-done | bytes 589856 | tf_op jit(solution)/shard_map/ppermute | solution.py:447
  612.3 8.3 shard_map.252
  630.1 31.2 %shard_map.253 = bf16[1,8,288,1152]{3,2,1,0:T(8,128)(2,1)} custom-call(bf16[512,2304]{1,0:T(8,128)(2,1)S(1)} %copy-done.26, bf16[512,2304]{1,0:T(8,128)(2,1)S(1)} %copy-done.29, bf16[1024,2304]{1,0:T(8,128)(2,1)} %copy-done.8, bf16[1024,2304]{1,0:T(8,128)(2,1)} %collective-permute-done.58.refs_0_.refs_3_, ...), custom_call_target="tpu_custom_call" | custom-call | flops 1 | bytes 1 | tf_op jit(solution)/shard_map/pallas_call | solution.py:806
  703.2 31.4 %shard_map.255 = bf16[1,8,288,1152]{3,2,1,0:T(8,128)(2,1)} custom-call(bf16[512,2304]{1,0:T(8,128)(2,1)S(1)} %copy-done.4, bf16[512,2304]{1,0:T(8,128)(2,1)S(1)} %copy-done.14, bf16[1024,2304]{1,0:T(8,128)(2,1)} %copy-done.1, bf16[1024,2304]{1,0:T(8,128)(2,1)} %copy-done.2, bf16[512,2304]{1,0:T(8,128)(2,1)S(1)} %copy-done.6, ...), custom_call_target="tpu_custom_call" | custom-call | flops 1 | bytes 1 | tf_op jit(solution)/shard_map/pallas_call | solution.py:806
  775.3 20.0 %collective-permute-done.72 = bf16[8,2,72,512]{3,2,0,1:T(8,128)(2,1)} collective-permute-done((bf16[8,2,72,512]{3,2,0,1:T(8,128)(2,1)}, bf16[8,2,72,512]{3,2,0,1:T(8,128)(2,1)}, u32[]{:S(2)}, u32[]{:S(2)}) %collective-permute-start.72) | collective-permute-done | bytes 1179680 | tf_op jit(solution)/shard_map/ppermute | solution.py:451
  808.6 31.2 %shard_map.256 = bf16[1,8,288,1152]{3,2,1,0:T(8,128)(2,1)} custom-call(bf16[512,2304]{1,0:T(8,128)(2,1)S(1)} %copy-done.4, bf16[512,2304]{1,0:T(8,128)(2,1)S(1)} %copy-done.15, bf16[1024,2304]{1,0:T(8,128)(2,1)} %copy-done.1, bf16[1024,2304]{1,0:T(8,128)(2,1)} %copy-done.2, bf16[512,2304]{1,0:T(8,128)(2,1)S(1)} %copy-done.7, ...), custom_call_target="tpu_custom_call" | custom-call | flops 1 | bytes 1 | tf_op jit(solution)/shard_map/pallas_call | solution.py:806
  861.0 12.1 %all-to-all-done.6 = bf16[8,72,768]{2,1,0:T(8,128)(2,1)} async-done(((bf16[8,72,768]{2,1,0:T(8,128)(2,1)}), bf16[8,72,768]{2,1,0:T(8,128)(2,1)}, u32[]{:S(2)}, u32[]{:S(2)}) %all-to-all-start.6) | async-done | bytes 884768 | tf_op jit(solution)/shard_map/all_to_all | solution.py:634
  888.6 18.7 %collective-permute-done.81 = f32[4,288]{1,0:T(4,128)S(1)} collective-permute-done((f32[4,288]{1,0:T(4,128)S(1)}, f32[4,288]{1,0:T(4,128)S(1)}, u32[]{:S(2)}, u32[]{:S(2)}) %collective-permute-start.81) | collective-permute-done | bytes 4640 | tf_op jit(solution)/shard_map/ppermute | solution.py:451
  909.8 18.5 %collective-permute-done.82 = f32[4,288]{1,0:T(4,128)S(1)} collective-permute-done((f32[4,288]{1,0:T(4,128)S(1)}, f32[4,288]{1,0:T(4,128)S(1)}, u32[]{:S(2)}, u32[]{:S(2)}) %collective-permute-start.82) | collective-permute-done | bytes 4640 | tf_op jit(solution)/shard_map/ppermute | solution.py:451
  931.5 8.0 shard_map.260
  939.5 8.0 shard_map.258
  949.7 22.7 %collective-permute-done.83 = bf16[2,8,72,768]{3,2,1,0:T(8,128)(2,1)} collective-permute-done((bf16[2,8,72,768]{3,2,1,0:T(8,128)(2,1)}, bf16[2,8,72,768]{3,2,1,0:T(8,128)(2,1)}, u32[]{:S(2)}, u32[]{:S(2)}) %collective-permute-start.83) | collective-permute-done | bytes 1769504 | tf_op jit(solution)/shard_map/ppermute | solution.py:451
  984.0 8.0 shard_map.259
  (659 shorter events, 438.0 us)
Async XLA Ops:
  18.6 36.2 %all-to-all-start = ((bf16[8,72,1152]{2,1,0:T(8,128)(2,1)}), bf16[8,72,1152]{2,1,0:T(8,128)(2,1)S(1)}, u32[]{:S(2)}, u32[]{:S(2)}) async-start(bf16[8,72,1152]{2,1,0:T(8,128)(2,1)} %shard_map.237), calls=%async_computation | async-start | bytes 2654208 | tf_op jit(solution)/shard_map/all_to_all | solution.py:634
  47.7 34.6 %collective-permute-start.4 = (bf16[512,2304]{1,0:T(8,128)(2,1)}, bf16[512,2304]{1,0:T(8,128)(2,1)}, u32[]{:S(2)}, u32[]{:S(2)}) collective-permute-start(bf16[512,2304]{1,0:T(8,128)(2,1)} %get-tuple-element.407), channel_id=1, source_target_pairs={{0,4},{4,0},{8,12},{12,8},{16,20},{20,16},{24,28},{28,24},{1,5},{5... | collective-permute-start | bytes 7077896 | tf_op jit(solution)/shard_map/ppermute | solution.py:447
  54.9 59.2 %all-to-all-start.1 = ((bf16[8,288,768]{2,1,0:T(8,128)(2,1)}), bf16[8,288,768]{2,1,0:T(8,128)(2,1)}, u32[]{:S(2)}, u32[]{:S(2)}) async-start(bf16[8,288,768]{2,1,0:T(8,128)(2,1)} %shard_map.238), calls=%async_computation.1 | async-start | bytes 7077888 | tf_op jit(solution)/shard_map/all_to_all | solution.py:634
  77.3 32.5 %collective-permute-start.5 = (bf16[8,72,1152]{2,1,0:T(8,128)(2,1)S(1)}, bf16[8,72,1152]{2,1,0:T(8,128)(2,1)S(1)}, u32[]{:S(2)}, u32[]{:S(2)}) collective-permute-start(bf16[8,72,1152]{2,1,0:T(8,128)(2,1)S(1)} %all-to-all-done.own), channel_id=1, source_target_pairs={{0,1},{1,2},{2,3},{4,5},{5,6},{6,7},{8,9},{9,10},{10,11},{12,13},{... | collective-permute-start | bytes 3981320 | tf_op jit(solution)/shard_map/ppermute | solution.py:455
  80.9 33.2 %collective-permute-start.6 = (bf16[8,72,1152]{2,1,0:T(8,128)(2,1)S(1)}, bf16[8,72,1152]{2,1,0:T(8,128)(2,1)}, u32[]{:S(2)}, u32[]{:S(2)}) collective-permute-start(bf16[8,72,1152]{2,1,0:T(8,128)(2,1)S(1)} %all-to-all-done.own), channel_id=1, source_target_pairs={{1,0},{2,1},{3,2},{5,4},{6,5},{7,6},{9,8},{10,9},{11,10},{13,12},{... | collective-permute-start | bytes 3981320 | tf_op jit(solution)/shard_map/ppermute | solution.py:455
  127.1 33.0 %collective-permute-start.10 = (bf16[8,72,1152]{2,1,0:T(8,128)(2,1)}, bf16[8,72,1152]{2,1,0:T(8,128)(2,1)}, u32[]{:S(2)}, u32[]{:S(2)}) collective-permute-start(bf16[8,72,1152]{2,1,0:T(8,128)(2,1)} %collective-permute-done.6.refs_3_), channel_id=1, source_target_pairs={{1,0},{2,1},{3,2},{5,4},{6,5},{7,6},{9,8},{10,9},{11,10},{13,12},{... | collective-permute-start | bytes 3981320 | tf_op jit(solution)/shard_map/ppermute | solution.py:455
  128.4 65.8 %all-to-all-start.2 = ((bf16[8,288,1152]{2,1,0:T(8,128)(2,1)}), bf16[8,288,1152]{2,1,0:T(8,128)(2,1)}, u32[]{:S(2)}, u32[]{:S(2)}) async-start(bf16[8,288,1152]{2,1,0:T(8,128)(2,1)} %shard_map.239), calls=%async_computation.2 | async-start | bytes 10616832 | tf_op jit(solution)/shard_map/all_to_all | solution.py:634
  162.2 36.2 %collective-permute-start.14 = (bf16[8,72,1152]{2,1,0:T(8,128)(2,1)}, bf16[8,72,1152]{2,1,0:T(8,128)(2,1)}, u32[]{:S(2)}, u32[]{:S(2)}) collective-permute-start(bf16[8,72,1152]{2,1,0:T(8,128)(2,1)} %collective-permute-done.9.refs_1_), channel_id=1, source_target_pairs={{0,1},{1,2},{2,3},{4,5},{5,6},{6,7},{8,9},{9,10},{10,11},{12,13},{... | collective-permute-start | bytes 3981320 | tf_op jit(solution)/shard_map/ppermute | solution.py:455
  165.8 33.4 %collective-permute-start.15 = (bf16[8,72,1152]{2,1,0:T(8,128)(2,1)}, bf16[8,72,1152]{2,1,0:T(8,128)(2,1)}, u32[]{:S(2)}, u32[]{:S(2)}) collective-permute-start(bf16[8,72,1152]{2,1,0:T(8,128)(2,1)} %collective-permute-done.10.refs_4_), channel_id=1, source_target_pairs={{1,0},{2,1},{3,2},{5,4},{6,5},{7,6},{9,8},{10,9},{11,10},{13,12},{... | collective-permute-start | bytes 3981320 | tf_op jit(solution)/shard_map/ppermute | solution.py:455
  222.1 79.6 %all-to-all-start.3 = ((bf16[8,288,1152]{2,1,0:T(8,128)(2,1)}), bf16[8,288,1152]{2,1,0:T(8,128)(2,1)}, u32[]{:S(2)}, u32[]{:S(2)}) async-start(bf16[8,288,1152]{2,1,0:T(8,128)(2,1)} %shard_map.240), calls=%async_computation.3 | async-start | bytes 10616832 | tf_op jit(solution)/shard_map/all_to_all | solution.py:634
  232.9 66.7 %collective-permute-start.18 = (bf16[128,2304]{1,0:T(8,128)(2,1)S(1)}, bf16[128,2304]{1,0:T(8,128)(2,1)S(1)}, u32[]{:S(2)}, u32[]{:S(2)}) collective-permute-start(bf16[128,2304]{1,0:T(8,128)(2,1)S(1)} %multiply_convert_fusion.1), channel_id=1, source_target_pairs={{0,8},{4,12},{8,0},{12,4},{16,24},{20,28},{24,16},{28,20},{1,9},{5... | collective-permute-start | bytes 1769480 | tf_op jit(solution)/shard_map/ppermute | solution.py:447
  234.9 64.7 %collective-permute-start.19 = (bf16[128,2304]{1,0:T(8,128)(2,1)S(1)}, bf16[128,2304]{1,0:T(8,128)(2,1)S(1)}, u32[]{:S(2)}, u32[]{:S(2)}) collective-permute-start(bf16[128,2304]{1,0:T(8,128)(2,1)S(1)} %multiply_convert_fusion.1), channel_id=1, source_target_pairs={{0,16},{4,20},{8,24},{12,28},{16,0},{20,4},{24,8},{28,12},{1,17},{... | collective-permute-start | bytes 1769480 | tf_op jit(solution)/shard_map/ppermute | solution.py:447
  236.4 63.2 %collective-permute-start.20 = (bf16[128,2304]{1,0:T(8,128)(2,1)S(1)}, bf16[128,2304]{1,0:T(8,128)(2,1)S(1)}, u32[]{:S(2)}, u32[]{:S(2)}) collective-permute-start(bf16[128,2304]{1,0:T(8,128)(2,1)S(1)} %multiply_convert_fusion.1), channel_id=1, source_target_pairs={{0,1},{1,0},{2,3},{3,2},{4,5},{5,4},{6,7},{7,6},{8,9},{9,8},{10,11... | collective-permute-start | bytes 1769480 | tf_op jit(solution)/shard_map/ppermute | solution.py:451
  239.0 60.6 %collective-permute-start.21 = (bf16[128,2304]{1,0:T(8,128)(2,1)S(1)}, bf16[128,2304]{1,0:T(8,128)(2,1)S(1)}, u32[]{:S(2)}, u32[]{:S(2)}) collective-permute-start(bf16[128,2304]{1,0:T(8,128)(2,1)S(1)} %multiply_convert_fusion.1), channel_id=1, source_target_pairs={{0,2},{1,3},{2,0},{3,1},{4,6},{5,7},{6,4},{7,5},{8,10},{9,11},{10,... | collective-permute-start | bytes 1769480 | tf_op jit(solution)/shard_map/ppermute | solution.py:451
  240.1 61.6 %collective-permute-start.22 = (bf16[128,2304]{1,0:T(8,128)(2,1)S(1)}, bf16[128,2304]{1,0:T(8,128)(2,1)}, u32[]{:S(2)}, u32[]{:S(2)}) collective-permute-start(bf16[128,2304]{1,0:T(8,128)(2,1)S(1)} %multiply_convert_fusion.1), channel_id=1, source_target_pairs={{0,3},{1,2},{2,1},{3,0},{4,7},{5,6},{6,5},{7,4},{8,11},{9,10},{10,... | collective-permute-start | bytes 1769480 | tf_op jit(solution)/shard_map/ppermute | solution.py:451
  436.8 35.1 %collective-permute-start.47 = (bf16[512,2304]{1,0:T(8,128)(2,1)S(1)}, bf16[512,2304]{1,0:T(8,128)(2,1)S(1)}, u32[]{:S(2)}, u32[]{:S(2)}) collective-permute-start(bf16[512,2304]{1,0:T(8,128)(2,1)S(1)} %constant_dynamic-update-slice_fusion.24.refs_0_.refs_4_), channel_id=1, source_target_pairs={{0,4},{4,0},{8,12},{12,8},{16,20},{20,16},{24,28},{28,24},{1,5},{5... | collective-permute-start | bytes 7077896 | tf_op jit(solution)/shard_map/ppermute | solution.py:447
  516.0 32.2 %collective-permute-start.53 = (bf16[128,2304]{1,0:T(8,128)(2,1)}, bf16[128,2304]{1,0:T(8,128)(2,1)}, u32[]{:S(2)}, u32[]{:S(2)}) collective-permute-start(bf16[128,2304]{1,0:T(8,128)(2,1)} %get-tuple-element.228), channel_id=1, source_target_pairs={{0,3},{1,2},{2,1},{3,0},{4,7},{5,6},{6,5},{7,4},{8,11},{9,10},{10,... | collective-permute-start | bytes 1769480 | tf_op jit(solution)/shard_map/ppermute | solution.py:451
  548.2 52.7 %collective-permute-start.58 = (bf16[1024,2304]{1,0:T(8,128)(2,1)S(1)}, bf16[1024,2304]{1,0:T(8,128)(2,1)}, u32[]{:S(2)}, u32[]{:S(2)}) collective-permute-start(bf16[1024,2304]{1,0:T(8,128)(2,1)S(1)} %constant_dynamic-update-slice_fusion.36.refs_0_.refs_2_), channel_id=1, source_target_pairs={{0,4},{4,0},{8,12},{12,8},{16,20},{20,16},{24,28},{28,24},{1,5},{5... | collective-permute-start | bytes 14155784 | tf_op jit(solution)/shard_map/ppermute | solution.py:447
  627.9 33.5 %collective-permute-start.64 = (bf16[128,2304]{1,0:T(8,128)(2,1)S(1)}, bf16[128,2304]{1,0:T(8,128)(2,1)S(1)}, u32[]{:S(2)}, u32[]{:S(2)}) collective-permute-start(bf16[128,2304]{1,0:T(8,128)(2,1)S(1)} %subtract_convert_fusion), channel_id=1, source_target_pairs={{0,8},{4,12},{8,0},{12,4},{16,24},{20,28},{24,16},{28,20},{1,9},{5... | collective-permute-start | bytes 1769480 | tf_op jit(solution)/shard_map/ppermute | solution.py:447
  671.2 74.4 %all-to-all-start.4 = ((bf16[8,288,1152]{2,1,0:T(8,128)(2,1)}), bf16[8,288,1152]{2,1,0:T(8,128)(2,1)}, u32[]{:S(2)}, u32[]{:S(2)}) async-start(bf16[8,288,1152]{2,1,0:T(8,128)(2,1)} %bitcast.91), calls=%async_computation.4 | async-start | bytes 10616832 | tf_op jit(solution)/shard_map/all_to_all | solution.py:634
  685.4 54.1 %collective-permute-start.70 = (f32[1024,128]{0,1:T(8,128)}, f32[1024,128]{0,1:T(8,128)}, u32[]{:S(2)}, u32[]{:S(2)}) collective-permute-start(f32[1024,128]{0,1:T(8,128)} %constant_dynamic-slice_fusion.4), channel_id=1, source_target_pairs={{0,4},{4,0},{8,12},{12,8},{16,20},{20,16},{24,28},{28,24},{1,5},{5... | collective-permute-start | bytes 1572872 | tf_op jit(solution)/shard_map/ppermute | solution.py:447
  691.0 49.6 %collective-permute-start.69 = (f32[1024,256]{0,1:T(8,128)S(1)}, f32[1024,256]{0,1:T(8,128)}, u32[]{:S(2)}, u32[]{:S(2)}) collective-permute-start(f32[1024,256]{0,1:T(8,128)S(1)} %convolution_multiply_fusion.6), channel_id=1, source_target_pairs={{0,4},{4,0},{8,12},{12,8},{16,20},{20,16},{24,28},{28,24},{1,5},{5... | collective-permute-start | bytes 3145736 | tf_op jit(solution)/shard_map/ppermute | solution.py:447
  752.2 44.7 %collective-permute-start.71 = (bf16[512,2304]{1,0:T(8,128)(2,1)}, bf16[512,2304]{1,0:T(8,128)(2,1)}, u32[]{:S(2)}, u32[]{:S(2)}) collective-permute-start(bf16[512,2304]{1,0:T(8,128)(2,1)} %fusion.6), channel_id=1, source_target_pairs={{0,4},{4,0},{8,12},{12,8},{16,20},{20,16},{24,28},{28,24},{1,5},{5... | collective-permute-start | bytes 7077896 | tf_op jit(solution)/shard_map/ppermute | solution.py:447
  762.5 32.8 %collective-permute-start.72 = (bf16[8,2,72,512]{3,2,0,1:T(8,128)(2,1)}, bf16[8,2,72,512]{3,2,0,1:T(8,128)(2,1)}, u32[]{:S(2)}, u32[]{:S(2)}) collective-permute-start(bf16[8,2,72,512]{3,2,0,1:T(8,128)(2,1)} %bitcast.76), channel_id=1, source_target_pairs={{0,1},{1,0},{2,3},{3,2},{4,5},{5,4},{6,7},{7,6},{8,9},{9,8},{10,11... | collective-permute-start | bytes 3538952 | tf_op jit(solution)/shard_map/ppermute | solution.py:451
  764.5 77.7 %all-to-all-start.5 = ((bf16[8,288,1152]{2,1,0:T(8,128)(2,1)}), bf16[8,288,1152]{2,1,0:T(8,128)(2,1)}, u32[]{:S(2)}, u32[]{:S(2)}) async-start(bf16[8,288,1152]{2,1,0:T(8,128)(2,1)} %bitcast.90), calls=%async_computation.5 | async-start | bytes 10616832 | tf_op jit(solution)/shard_map/all_to_all | solution.py:634
  799.8 41.6 %collective-permute-start.74 = (bf16[8,72,512]{2,1,0:T(8,128)(2,1)S(1)}, bf16[8,72,512]{2,1,0:T(8,128)(2,1)S(1)}, u32[]{:S(2)}, u32[]{:S(2)}) collective-permute-start(bf16[8,72,512]{2,1,0:T(8,128)(2,1)S(1)} %dynamic-slice_bitcast_fusion), channel_id=1, source_target_pairs={{0,2},{1,3},{2,0},{3,1},{4,6},{5,7},{6,4},{7,5},{8,10},{9,11},{10,... | collective-permute-start | bytes 1769480 | tf_op jit(solution)/shard_map/ppermute | solution.py:451
  800.7 39.8 %collective-permute-start.75 = (bf16[8,72,256]{2,1,0:T(8,128)(2,1)}, bf16[8,72,256]{2,1,0:T(8,128)(2,1)S(1)}, u32[]{:S(2)}, u32[]{:S(2)}) collective-permute-start(bf16[8,72,256]{2,1,0:T(8,128)(2,1)} %dynamic-slice_bitcast_fusion.1), channel_id=1, source_target_pairs={{0,2},{1,3},{2,0},{3,1},{4,6},{5,7},{6,4},{7,5},{8,10},{9,11},{10,... | collective-permute-start | bytes 884744 | tf_op jit(solution)/shard_map/ppermute | solution.py:451
  803.9 38.4 %collective-permute-start.76 = (bf16[128,2304]{1,0:T(8,128)(2,1)S(1)}, bf16[128,2304]{1,0:T(8,128)(2,1)}, u32[]{:S(2)}, u32[]{:S(2)}) collective-permute-start(bf16[128,2304]{1,0:T(8,128)(2,1)S(1)} %pad_maximum_fusion.11), channel_id=1, source_target_pairs={{0,8},{4,12},{8,0},{12,4},{16,24},{20,28},{24,16},{28,20},{1,9},{5... | collective-permute-start | bytes 1769480 | tf_op jit(solution)/shard_map/ppermute | solution.py:447
  805.9 36.4 %collective-permute-start.77 = (bf16[128,2304]{1,0:T(8,128)(2,1)S(1)}, bf16[128,2304]{1,0:T(8,128)(2,1)}, u32[]{:S(2)}, u32[]{:S(2)}) collective-permute-start(bf16[128,2304]{1,0:T(8,128)(2,1)S(1)} %pad_maximum_fusion.12), channel_id=1, source_target_pairs={{0,16},{4,20},{8,24},{12,28},{16,0},{20,4},{24,8},{28,12},{1,17},{... | collective-permute-start | bytes 1769480 | tf_op jit(solution)/shard_map/ppermute | solution.py:447
  882.5 101.5 %all-to-all-start.8 = ((bf16[8,288,1152]{2,1,0:T(8,128)(2,1)}), bf16[8,288,1152]{2,1,0:T(8,128)(2,1)}, u32[]{:S(2)}, u32[]{:S(2)}) async-start(bf16[8,288,1152]{2,1,0:T(8,128)(2,1)} %bitcast.92), calls=%async_computation.8 | async-start | bytes 10616832 | tf_op jit(solution)/shard_map/all_to_all | solution.py:634
  887.2 41.1 %collective-permute-start.80 = (bf16[8,72,768]{2,1,0:T(8,128)(2,1)}, bf16[8,72,768]{2,1,0:T(8,128)(2,1)}, u32[]{:S(2)}, u32[]{:S(2)}) collective-permute-start(bf16[8,72,768]{2,1,0:T(8,128)(2,1)} %all-to-all-done.6), channel_id=1, source_target_pairs={{0,2},{1,3},{2,0},{3,1},{4,6},{5,7},{6,4},{7,5},{8,10},{9,11},{10,... | collective-permute-start | bytes 2654216 | tf_op jit(solution)/shard_map/ppermute | solution.py:451
  931.5 40.9 %collective-permute-start.83 = (bf16[2,8,72,768]{3,2,1,0:T(8,128)(2,1)}, bf16[2,8,72,768]{3,2,1,0:T(8,128)(2,1)}, u32[]{:S(2)}, u32[]{:S(2)}) collective-permute-start(bf16[2,8,72,768]{3,2,1,0:T(8,128)(2,1)} %reverse_select_fusion.1), channel_id=1, source_target_pairs={{0,1},{1,0},{2,3},{3,2},{4,5},{5,4},{6,7},{7,6},{8,9},{9,8},{10,11... | collective-permute-start | bytes 5308424 | tf_op jit(solution)/shard_map/ppermute | solution.py:451
  (205 other events, 2703.6 us)

commit v3 on v2

--- a/solution.py
+++ b/solution.py
@@ -436,10 +436,10 @@
 
 
 VMEM_BYTES = 56 * 1024 * 1024
-TILE_VMEM_BYTES = 28 * 1024 * 1024
-CROSS_VMEM_BYTES = 40 * 1024 * 1024
+TILE_VMEM_BYTES = 18 * 1024 * 1024
+CROSS_VMEM_BYTES = 38 * 1024 * 1024
 GELU_RATE = 0.7978845608028654
-TILE = 512
+TILE = 256
 CHUNK = 768
 
 
@@ -531,16 +531,20 @@
 
 def scatter_core(partial_half):
     theirs = seq_swap(partial_half(1, jnp.bfloat16), 1)
-    return partial_half(0, jnp.float32) + wide(theirs)
-
-
-def scatter_near(mine):
+    return scatter_parts(partial_half(0, jnp.float32) + wide(theirs))
+
+
+def scatter_parts(mine):
     unit = mine.shape[0] // 4
     half = unit // 2
     here, by_x, by_y, far = (mine[i * unit : (i + 1) * unit] for i in range(4))
-    from_x = seq_swap(bf(jnp.concatenate([by_x[:half], far[:half]])), 2)
-    from_y = seq_swap(bf(jnp.concatenate([by_y[half:], far[half:]])), 4)
-    return here, by_x[half:], by_y[:half], from_x, from_y
+    to_x = bf(jnp.concatenate([by_x[:half], far[:half]]))
+    to_y = bf(jnp.concatenate([by_y[half:], far[half:]]))
+    return here, by_x[half:], by_y[:half], to_x, to_y
+
+
+def scatter_near(here, by_x, by_y, to_x, to_y):
+    return here, by_x, by_y, seq_swap(to_x, 2), seq_swap(to_y, 4)
 
 
 def scatter_far(here, by_x, by_y, from_x, from_y):
@@ -556,7 +560,7 @@
 
 
 def scatter_row(partial_half):
-    return scatter_far(*scatter_near(scatter_core(partial_half)))
+    return scatter_far(*scatter_near(*scatter_core(partial_half)))
 
 
 def pack_kernel(decoders, place_ref, *refs):
@@ -830,13 +834,14 @@
     rows, hidden = pairs[0][0].shape
     columns = pairs[0][1].shape[0]
     half = rows // 2
-    left_spec = pl.BlockSpec((half, hidden), lambda i: (side, 0))
+    steps = half // TILE
+    left_spec = pl.BlockSpec((TILE, hidden), lambda i: (side * steps + i, 0))
     return tile_calls(
         partial_kernel,
-        (1,),
+        (steps,),
         [spec for pair in pairs for spec in (left_spec, whole_spec(pair[1]))],
         [array for pair in pairs for array in pair],
-        pl.BlockSpec((half, columns), lambda i: (0, 0)),
+        pl.BlockSpec((TILE, columns), lambda i: (i, 0)),
         jax.ShapeDtypeStruct((half, columns), kind),
     )
 
@@ -931,26 +936,22 @@
     totals = jnp.sum(weights, axis=-1, keepdims=True)
     attended_wide = dot(bf(weights), value) / totals
     attended = bf(attended_wide)
-    attended, down_two = pin(attended, both_ways(*down_one))
+    attended, gate_rows, down_two = pin(attended, gate_rows, both_ways(*down_one))
     near_half = row_length // 2
     attn_core = scatter_core(
         lambda side, kind: times_transposed(
             attended[side * near_half :][:near_half], w_out
         ).astype(kind)
     )
-    attn_core, gate_rows = pin(attn_core, gate_rows)
-    attn_near, down_three = pin(scatter_near(attn_core), both_ways(*down_two))
+    (attn_core,) = pin(attn_core)
+    attn_near, down_three = pin(scatter_near(*attn_core), both_ways(*down_two))
     attn_proj, up_blocks = pin(scale_out * scatter_far(*attn_near), up_blocks)
     up_rows = trade(up_blocks)
     middle = tokens + norm_gain(attn_proj, gain_attn_out)
     normed_mid = bf(norm_gain(middle, gain_ffw_in))
 
-    mid_near, up_rows, mid_one, mid_two, mid_three = pin(
-        gather_near(normed_mid),
-        up_rows,
-        row_swap(normed_mid, 1),
-        row_swap(normed_mid, 2),
-        row_swap(normed_mid, 3),
+    mid_near, up_rows, mid_two, mid_three = pin(
+        gather_near(normed_mid), up_rows, row_swap(normed_mid, 2), row_swap(normed_mid, 3)
     )
     mid_mine = gather_far(*mid_near)
     mid_mine, mid_theirs, w_down = pin(
@@ -966,55 +967,62 @@
     def back_again(halves, factors):
         return back_project(halves, w_down, factors, scale_down)
 
-    (mixed, *factors), pair_mid_near = pin(
-        up_again(mid_mine, mid_theirs), gather_near(jnp.concatenate([mid_one, mid_two]))
-    )
-    ffn_core, pair_mid_mine = pin(
+    def cut(rows):
+        return [rows[i * block_rows : (i + 1) * block_rows] for i in range(4)]
+
+    (mixed, *factors), pair_mid_near, mid_cuts = pin(
+        up_again(mid_mine, mid_theirs),
+        gather_near(jnp.concatenate([mid_two, mid_three])),
+        cut(mid_mine),
+    )
+    ffn_core, pair_mid_mine, third_mid_first = pin(
         scatter_core(lambda side, kind: partial_product([(mixed, w_down)], side, kind)),
         gather_far(*pair_mid_near),
-    )
-    ffn_near, pair_mid_theirs = pin(scatter_near(ffn_core), seq_swap(pair_mid_mine, 1))
-    ffn_proj, third_mid_near = pin(scale_down * scatter_far(*ffn_near), gather_near(mid_three))
+        [row_swap(rows, 1) for rows in mid_cuts[:2]],
+    )
+    ffn_near, pair_mid_theirs, third_mid_second = pin(
+        scatter_near(*ffn_core), seq_swap(pair_mid_mine, 1), row_swap(mid_cuts[2], 1)
+    )
+    ffn_proj, third_mid_last, pair_mid_mine = pin(
+        scale_down * scatter_far(*ffn_near), row_swap(mid_cuts[3], 1), pair_mid_mine
+    )
+    third_mid_mine = jnp.concatenate([*third_mid_first, third_mid_second, third_mid_last])
     block_out = bf(middle + norm_gain(ffn_proj, gain_ffw_out))
     grad_ffn, grad_gain_four = norm_back(ffn_proj, gain_ffw_out, upstream)
     grad_ffn_low = bf(grad_ffn)
-    grad_near, grad_one, third_mid_mine, (mine_mixed, *mine_factors) = pin(
-        gather_near(grad_ffn_low),
-        row_swap(grad_ffn_low, 1),
-        gather_far(*third_mid_near),
-        up_again(pair_mid_mine),
+    grad_near, grad_two, (mine_mixed, *mine_factors) = pin(
+        gather_near(grad_ffn_low), row_swap(grad_ffn_low, 2), up_again(pair_mid_mine)
     )
     grad_mine = gather_far(*grad_near)
-    grad_mine, grad_theirs, grad_two, third_mid_theirs, (theirs_mixed, *theirs_factors) = pin(
+    grad_mine, grad_theirs, grad_three, third_mid_theirs, (theirs_mixed, *theirs_factors) = pin(
         grad_mine,
         seq_swap(grad_mine, 1),
-        row_swap(grad_ffn_low, 2),
+        row_swap(grad_ffn_low, 3),
         seq_swap(third_mid_mine, 1),
         up_again(pair_mid_theirs),
     )
-    grads_hidden, pair_grad_near = pin(
+    grad_cuts = cut(grad_mine)
+    grads_hidden, pair_grad_near, third_grad_first = pin(
         back_again((grad_mine, grad_theirs), factors),
-        gather_near(jnp.concatenate([grad_one, grad_two])),
+        gather_near(jnp.concatenate([grad_two, grad_three])),
+        [row_swap(rows, 1) for rows in grad_cuts[:2]],
     )
     pairs = list(zip(grads_hidden, (w_gate, w_up)))
-    mid_core, pair_grad_mine, grad_three = pin(
+    mid_core, pair_grad_mine, third_grad_last = pin(
         scatter_core(lambda side, kind: partial_product(pairs, side, kind)),
         gather_far(*pair_grad_near),
-        row_swap(grad_ffn_low, 3),
-    )
-    sum_near, third_grad_near, (third_mixed, *third_factors), pair_grad_theirs, mine_hidden = pin(
-        scatter_near(mid_core),
-        gather_near(grad_three),
+        [row_swap(rows, 1) for rows in grad_cuts[2:]],
+    )
+    third_grad_mine = jnp.concatenate([*third_grad_first, *third_grad_last])
+    sum_near, pair_grad_theirs, third_grad_theirs, (third_mixed, *third_factors), mine_hidden = pin(
+        scatter_near(*mid_core),
+        seq_swap(pair_grad_mine, 1),
+        seq_swap(third_grad_mine, 1),
         up_again(third_mid_mine, third_mid_theirs),
-        seq_swap(pair_grad_mine, 1),
         back_again((pair_grad_mine,), mine_factors),
     )
-    third_grad_mine = gather_far(*third_grad_near)
-    grad_mid, third_grad_mine, third_grad_theirs, theirs_hidden = pin(
-        scale_in * scatter_far(*sum_near),
-        third_grad_mine,
-        seq_swap(third_grad_mine, 1),
-        back_again((pair_grad_theirs,), theirs_factors),
+    grad_mid, theirs_hidden = pin(
+        scale_in * scatter_far(*sum_near), back_again((pair_grad_theirs,), theirs_factors)
     )
     grad_middle_part, grad_gain_three = norm_back(middle, gain_ffw_in, grad_mid)
     grad_middle = upstream + grad_middle_part
@@ -1060,9 +1068,6 @@
     probs = weights / totals
     grad_probs = times_transposed(grad_attended, value)
     grad_raw = bf(probs * (grad_probs - delta) * (1.0 - bend * bend))
-    grad_raw, third_grads = pin(grad_raw, third_grads)
-    third_hidden = back_again(third_grads, third_factors)
-    gate_terms, up_terms = zip(grads_hidden, mine_hidden, theirs_hidden, third_hidden)
     grad_query = bf(turn(dot(grad_raw, key) * head_scale, cosine, -sine))
     key_part = cross_rows(grad_raw, query) * head_scale
     value_part = cross_rows(bf(probs), grad_attended)
@@ -1074,10 +1079,11 @@
     grad_key = bf(own_half(turn(key_sum, cosine, -sine), core))
     grad_value = bf(own_half(value_part, core) + other_core(own_half(value_part, 1 - core)))
     grad_linear = jnp.concatenate([grad_query, grad_key, grad_value], axis=1)
-    grad_linear, down_blocks, gate_blocks, up_terms = pin(
-        grad_linear, down_blocks, cross_products(mids, gate_terms, steps), up_terms
-    )
-    gate_blocks = trade(gate_blocks[0])
+    grad_linear, out_sum, third_grads = pin(
+        grad_linear,
+        halve(quarters_of(cross_rows(row_proj, attended)), 1, 2, low_bit),
+        third_grads,
+    )
 
     def grad_in_half(side, kind):
         rows = grad_linear[side * near_half :][:near_half]
@@ -1086,27 +1092,35 @@
         ) + scale_in * times_transposed(rows[:, head + half :], w_attn_in[:, head + half :])
         return total.astype(kind)
 
-    in_core, in_sum, out_sum, up_terms = pin(
+    in_core, in_terms, out_sum, third_grads = pin(
         scatter_core(grad_in_half),
-        halve(quarters_of(cross_rows(normed_in, grad_linear)), 1, 2, low_bit),
-        halve(quarters_of(cross_rows(row_proj, attended)), 1, 2, low_bit),
+        quarters_of(cross_rows(normed_in, grad_linear)),
+        halve(out_sum, 2, 1, high_bit),
+        third_grads,
+    )
+    third_hidden = back_again(third_grads, third_factors)
+    gate_terms, up_terms = zip(grads_hidden, mine_hidden, theirs_hidden, third_hidden)
+    in_near, in_sum, gate_blocks, up_terms, down_blocks = pin(
+        scatter_near(*in_core),
+        halve(in_terms, 1, 2, low_bit),
+        cross_products(mids, gate_terms, steps),
         up_terms,
-    )
-    in_sum, out_sum, up_blocks, gate_blocks, in_near = pin(
+        down_blocks,
+    )
+    gate_blocks = trade(gate_blocks[0])
+    in_sum, grad_in, up_blocks, gate_blocks = pin(
         halve(in_sum, 2, 1, high_bit),
-        halve(out_sum, 2, 1, high_bit),
+        scatter_far(*in_near),
         cross_products(mids, up_terms, steps),
         gate_blocks,
-        scatter_near(in_core),
-    )
-    grad_in, sums = pin(
-        scatter_far(*in_near), trade(jnp.concatenate([in_sum, out_sum], axis=2))
     )
     grad_tokens, grad_gain_one = norm_back(tokens, gain_attn_in, grad_in)
     grad_input = grad_middle + grad_tokens
     gain_terms = jnp.stack([grad_gain_one, grad_gain_two, grad_gain_three, grad_gain_four])
     gain_blocks = trade(gain_terms.reshape(4, 8, model_rows).transpose(1, 0, 2))
-    gain_blocks, up_blocks = pin(gain_blocks, up_blocks)
+    sums, gain_blocks, up_blocks = pin(
+        trade(jnp.concatenate([in_sum, out_sum], axis=2)), gain_blocks, up_blocks
+    )
     up_blocks = trade(up_blocks[0])
 
     def double(blocks, bit, side):
@@ -1117,11 +1131,12 @@
     gains = gains + row_swap(gains, 1)
     blocks, gains = pin(double(sums, 2, high_bit), gains + row_swap(gains, 2))
     blocks = double(blocks, 1, low_bit).transpose(1, 0, 2, 3, 4)
-    attn_grads = unpack_blocks(blocks.reshape(4, *sums.shape), [head, half, half, head])
     grad_w_gate, grad_w_up, grad_w_down = (
         unpack_blocks(blocks, [hidden_part])[0]
         for blocks in (gate_blocks[None], up_blocks[None], down_blocks[None])
     )
+    blocks, grad_w_up = pin(blocks, grad_w_up)
+    attn_grads = unpack_blocks(blocks.reshape(4, *sums.shape), [head, half, half, head])
 
     return (
         block_out[None],

time: 1000 us -> 965 us (0.965)
  waiting for transfers between devices: 384 us -> 337 us
    ppermute x64 -> x56, waiting for transfers between devices: 221 us -> 150 us  [seq_swap(): lax.ppermute(block, 'seq', [(place, place ^ bit) for place in range(8)])]
    ppermute x14 -> x20, waiting for transfers between devices: 87.3 us -> 107 us  [row_swap(): lax.ppermute(block, 'row', [(place, place ^ bit) for place in range(4)])]
    ppermute x6, waiting for transfers between devices: 41.2 us -> 58.3 us  [row_shift(): lax.ppermute(block, 'row', [(place, place + step) for place in range(4) i...]
    all_to_all x8, waiting for transfers between devices: 34.6 us -> 21.8 us  [trade(): return lax.all_to_all(blocks, 'seq', 0, 0, tiled=True)]
    ppermute x14 -> x20, starting transfers between devices: 22.2 us -> 30.2 us  [row_swap(): lax.ppermute(block, 'row', [(place, place ^ bit) for place in range(4)])]
    ppermute x64 -> x56, starting transfers between devices: 56.9 us -> 50.7 us  [seq_swap(): lax.ppermute(block, 'seq', [(place, place ^ bit) for place in range(8)])]
    unnamed x316 -> x295, local copies, waits for them, and re-layouts: 36.7 us -> 36.2 us
  transfers between devices with their start and end apart: 92 -> 90, of which waited for: 47 -> 45; matrix products, arithmetic and copies ran while one was open for 12% -> 13% of each run, Pallas kernels for 27% -> 27%
where the time goes in v3:
time: 965 us; the launch traced here: 953 us
  waiting for transfers between devices  337 us (35%)
  Pallas kernels  290 us (30%)
  starting transfers between devices  134 us (14%)
  local copies, waits for them, and re-layouts  64.8 us (7%)
  other arithmetic  63.4 us (7%)
  matrix products  44.6 us (5%)
  blocking collectives  16 us (2%)
    ppermute x56, waiting for transfers between devices, seq_swap(): lax.ppermute(block, 'seq', [(place, place ^ bit) for place in range(8)])  150 us
    pallas_call x12, Pallas kernels, tile_calls(): pl.pallas_call(kernel, grid=grid, in_specs=in_specs, out_specs=out_specs,...  132 us
    ppermute x20, waiting for transfers between devices, row_swap(): lax.ppermute(block, 'row', [(place, place ^ bit) for place in range(4)])  107 us
    pallas_call x3, Pallas kernels, cross_products(): pl.pallas_call(functools.partial(cross_kernel, steps, len(lefts), len(rig...  94.6 us
    ppermute x6, waiting for transfers between devices, row_shift(): lax.ppermute(block, 'row', [(place, place + step) for place in range(4) i...  58.3 us
    ppermute x56, starting transfers between devices, seq_swap(): lax.ppermute(block, 'seq', [(place, place ^ bit) for place in range(8)])  50.7 us
    unnamed x295, local copies, waits for them, and re-layouts  36.2 us
    all_to_all x8, starting transfers between devices, trade(): return lax.all_to_all(blocks, 'seq', 0, 0, tiled=True)  36.2 us
  transfers between devices with their start and end apart: 90, of which 45 were waited for; matrix products, arithmetic and copies ran while one was open for 13% of the time, Pallas kernels for 27%

profile of v3, /device:TPU:0, one launch (start us, length us, event | category | flops | bytes accessed | tf_op | source)
XLA Modules:
  0.0 952.6 jit_solution(4436926716935998585)
XLA Ops:
  22.2 7.2 shard_map.238
  54.6 8.8 shard_map.239
  63.4 8.8 shard_map.240
  72.5 9.3 collective-permute-done.5.refs_0_
  126.0 15.7 %collective-permute-done.10.refs_4_ = bf16[8,72,1152]{2,1,0:T(8,128)(2,1)} collective-permute-done((bf16[8,72,1152]{2,1,0:T(8,128)(2,1)}, bf16[8,72,1152]{2,1,0:T(8,128)(2,1)}, u32[]{:S(2)}, u32[]{:S(2)}) %collective-permute-start.10) | collective-permute-done | bytes 1327136 | tf_op jit(solution)/shard_map/ppermute | solution.py:455
  142.6 10.8 %all-to-all-done.2 = bf16[8,288,1152]{2,1,0:T(8,128)(2,1)} async-done(((bf16[8,288,1152]{2,1,0:T(8,128)(2,1)}), bf16[8,288,1152]{2,1,0:T(8,128)(2,1)}, u32[]{:S(2)}, u32[]{:S(2)}) %all-to-all-start.2) | async-done | bytes 5308448 | tf_op jit(solution)/shard_map/all_to_all | solution.py:638
  164.5 24.0 %collective-permute-done.14.refs_2_ = bf16[8,72,1152]{2,1,0:T(8,128)(2,1)S(1)} collective-permute-done((bf16[8,72,1152]{2,1,0:T(8,128)(2,1)}, bf16[8,72,1152]{2,1,0:T(8,128)(2,1)S(1)}, u32[]{:S(2)}, u32[]{:S(2)}) %collective-permute-start.14) | collective-permute-done | bytes 1327136 | tf_op jit(solution)/shard_map/ppermute | solution.py:455
  219.7 60.6 %collective-permute-done.18 = bf16[128,2304]{1,0:T(8,128)(2,1)S(1)} collective-permute-done((bf16[128,2304]{1,0:T(8,128)(2,1)S(1)}, bf16[128,2304]{1,0:T(8,128)(2,1)S(1)}, u32[]{:S(2)}, u32[]{:S(2)}) %collective-permute-start.18) | collective-permute-done | bytes 589856 | tf_op jit(solution)/shard_map/ppermute | solution.py:447
  299.9 20.7 %shard_map.242 = (bf16[1024,1152]{1,0:T(8,128)(2,1)S(1)}, bf16[1024,1152]{1,0:T(8,128)(2,1)S(1)}, bf16[1024,1152]{1,0:T(8,128)(2,1)S(1)}) custom-call(bf16[512,2304]{1,0:T(8,128)(2,1)S(1)} %constant_dynamic-update-slice_fusion.12.refs_0_, bf16[512,2304]{1,0:T(8,128)(2,1)S(1)} %collective-permute-done.24.refs_1_, bf16[2304,1152]{1,0:T(8,128)(2,1)} %bitcast.6.refs_2_.refs_1_, ...), custom_call_target="tpu_custom_call" | custom-call | flops 1 | bytes 1 | tf_op jit(solution)/shard_map/pallas_call | solution.py:673
  336.2 11.3 %collective-permute-done.28 = bf16[128,2304]{1,0:T(8,128)(2,1)S(1)} collective-permute-done((bf16[128,2304]{1,0:T(8,128)(2,1)S(1)}, bf16[128,2304]{1,0:T(8,128)(2,1)S(1)}, u32[]{:S(2)}, u32[]{:S(2)}) %collective-permute-start.28) | collective-permute-done | bytes 589856 | tf_op jit(solution)/shard_map/ppermute | solution.py:447
  353.3 8.8 collective-permute-done.31
  367.2 11.0 %collective-permute-done.35 = bf16[128,2304]{1,0:T(8,128)(2,1)S(1)} collective-permute-done((bf16[128,2304]{1,0:T(8,128)(2,1)S(1)}, bf16[128,2304]{1,0:T(8,128)(2,1)S(1)}, u32[]{:S(2)}, u32[]{:S(2)}) %collective-permute-start.35) | collective-permute-done | bytes 589856 | tf_op jit(solution)/shard_map/ppermute | solution.py:451
  397.6 18.7 %shard_map.245 = (bf16[1024,1152]{1,0:T(8,128)(2,1)S(1)}, bf16[1024,1152]{1,0:T(8,128)(2,1)S(1)}, bf16[1024,1152]{1,0:T(8,128)(2,1)S(1)}) custom-call(bf16[1024,2304]{1,0:T(8,128)(2,1)S(1)} %constant_dynamic-update-slice_fusion.19.refs_0_.refs_2_, bf16[2304,1152]{1,0:T(8,128)(2,1)} %bitcast.6.refs_2_.refs_1_, bf16[2304,1152]{1,0:T(8,128)(2,1)} %bitcast.7.refs_3_.refs_2_), custom_call_target="tpu_custom_call" | custom-call | flops 1 | bytes 1 | tf_op jit(solution)/shard_map/pallas_call | solution.py:673
  434.4 18.0 %shard_map.246 = (bf16[1024,1152]{1,0:T(8,128)(2,1)S(1)}, bf16[1024,1152]{1,0:T(8,128)(2,1)S(1)}, bf16[1024,1152]{1,0:T(8,128)(2,1)S(1)}) custom-call(bf16[1024,2304]{1,0:T(8,128)(2,1)S(1)} %collective-permute-done.34.refs_0_.refs_3_, bf16[2304,1152]{1,0:T(8,128)(2,1)} %bitcast.6.refs_2_.refs_1_, bf16[2304,1152]{1,0:T(8,128)(2,1)} %bitcast.7.refs_3_.refs_2_), custom_call_target="tpu_custom_call" | custom-call | flops 1 | bytes 1 | tf_op jit(solution)/shard_map/pallas_call | solution.py:673
  463.0 7.0 shard_map.247
  470.1 7.1 collective-permute-done.49
  477.2 11.0 %collective-permute-done.50 = bf16[128,2304]{1,0:T(8,128)(2,1)S(1)} collective-permute-done((bf16[128,2304]{1,0:T(8,128)(2,1)S(1)}, bf16[128,2304]{1,0:T(8,128)(2,1)S(1)}, u32[]{:S(2)}, u32[]{:S(2)}) %collective-permute-start.50) | collective-permute-done | bytes 589856 | tf_op jit(solution)/shard_map/ppermute | solution.py:451
  488.2 10.8 %shard_map.249 = bf16[512,2304]{1,0:T(8,128)(2,1)S(1)} custom-call(bf16[1024,1152]{1,0:T(8,128)(2,1)S(1)} %get-tuple-element.275.refs_0_.refs_6_, bf16[2304,1152]{1,0:T(8,128)(2,1)} %bitcast.6.refs_2_.refs_1_, bf16[1024,1152]{1,0:T(8,128)(2,1)S(1)} %get-tuple-element.347.refs_2_.refs_6_, bf16[2304,1152]{1,0:T(8,128)(2,1)} %bitcast.7.refs_3_.refs_2_), custom_call_target="tpu_custom_call" | custom-call | flops 1 | bytes 1 | tf_op jit(solution)/shard_map/pallas_call | solution.py:673
  501.1 10.5 %shard_map.248 = f32[512,2304]{1,0:T(8,128)S(1)} custom-call(bf16[1024,1152]{1,0:T(8,128)(2,1)S(1)} %get-tuple-element.275.refs_0_.refs_6_, bf16[2304,1152]{1,0:T(8,128)(2,1)} %bitcast.6.refs_2_.refs_1_, bf16[1024,1152]{1,0:T(8,128)(2,1)S(1)} %get-tuple-element.347.refs_2_.refs_6_, bf16[2304,1152]{1,0:T(8,128)(2,1)} %bitcast.7.refs_3_.refs_2_), custom_call_target="tpu_custom_call" | custom-call | flops 1 | bytes 1 | tf_op jit(solution)/shard_map/pallas_call | solution.py:673
  514.3 12.6 %collective-permute-done.52 = bf16[128,2304]{1,0:T(8,128)(2,1)S(1)} collective-permute-done((bf16[128,2304]{1,0:T(8,128)(2,1)S(1)}, bf16[128,2304]{1,0:T(8,128)(2,1)S(1)}, u32[]{:S(2)}, u32[]{:S(2)}) %collective-permute-start.52) | collective-permute-done | bytes 589856 | tf_op jit(solution)/shard_map/ppermute | solution.py:447
  545.0 18.2 %shard_map.250 = (bf16[1024,1152]{1,0:T(8,128)(2,1)S(1)}, bf16[1024,1152]{1,0:T(8,128)(2,1)S(1)}, bf16[1024,1152]{1,0:T(8,128)(2,1)S(1)}) custom-call(bf16[512,2304]{1,0:T(8,128)(2,1)S(1)} %constant_dynamic-update-slice_fusion.29.refs_0_.refs_4_, bf16[512,2304]{1,0:T(8,128)(2,1)S(1)} %copy-done.17, bf16[2304,1152]{1,0:T(8,128)(2,1)} %bitcast.6.refs_2_.refs_1_, ...), custom_call_target="tpu_custom_call" | custom-call | flops 1 | bytes 1 | tf_op jit(solution)/shard_map/pallas_call | solution.py:673
  591.9 31.8 %shard_map.253 = bf16[1,8,288,1152]{3,2,1,0:T(8,128)(2,1)} custom-call(bf16[512,2304]{1,0:T(8,128)(2,1)S(1)} %constant_dynamic-update-slice_fusion.24.refs_0_, bf16[512,2304]{1,0:T(8,128)(2,1)S(1)} %copy-done.29, bf16[1024,2304]{1,0:T(8,128)(2,1)} %copy-done.8, bf16[1024,2304]{1,0:T(8,128)(2,1)} %copy-done.22, bf16[512,2304]{1,0:T(8,128)(2,1)S(1)} %copy-done.24, ...), custom_call_target="tpu_custom_call" | custom-call | flops 1 | bytes 1 | tf_op jit(solution)/shard_map/pallas_call | solution.py:810
  709.4 31.4 %shard_map.255 = bf16[1,8,288,1152]{3,2,1,0:T(8,128)(2,1)} custom-call(bf16[512,2304]{1,0:T(8,128)(2,1)S(1)} %copy-done.3, bf16[512,2304]{1,0:T(8,128)(2,1)S(1)} %copy-done.14, bf16[1024,2304]{1,0:T(8,128)(2,1)} %copy-done.1, bf16[1024,2304]{1,0:T(8,128)(2,1)} %copy-done.4, bf16[512,2304]{1,0:T(8,128)(2,1)S(1)} %copy-done.6, ...), custom_call_target="tpu_custom_call" | custom-call | flops 1 | bytes 1 | tf_op jit(solution)/shard_map/pallas_call | solution.py:810
  773.0 31.4 %shard_map.256 = bf16[1,8,288,1152]{3,2,1,0:T(8,128)(2,1)} custom-call(bf16[512,2304]{1,0:T(8,128)(2,1)S(1)} %copy-done.3, bf16[512,2304]{1,0:T(8,128)(2,1)S(1)} %copy-done.15, bf16[1024,2304]{1,0:T(8,128)(2,1)} %copy-done.1, bf16[1024,2304]{1,0:T(8,128)(2,1)} %copy-done.4, bf16[512,2304]{1,0:T(8,128)(2,1)S(1)} %copy-done.7, ...), custom_call_target="tpu_custom_call" | custom-call | flops 1 | bytes 1 | tf_op jit(solution)/shard_map/pallas_call | solution.py:810
  804.4 11.5 %collective-permute-done.77 = bf16[64,2304]{1,0:T(8,128)(2,1)} collective-permute-done((bf16[64,2304]{1,0:T(8,128)(2,1)}, bf16[64,2304]{1,0:T(8,128)(2,1)}, u32[]{:S(2)}, u32[]{:S(2)}) %collective-permute-start.77) | collective-permute-done | bytes 294944 | tf_op jit(solution)/shard_map/ppermute | solution.py:447
  828.9 16.0 %all_to_all.45 = bf16[8,72,768]{2,1,0:T(8,128)(2,1)S(1)} all-to-all(bf16[8,72,768]{2,1,0:T(8,128)(2,1)S(1)} %pad_maximum_fusion.4), channel_id=1, replica_groups=mesh['seq'=8,'row'=4] {'seq'}, dimensions={0} | all-to-all | bytes 1769472 | tf_op jit(solution)/shard_map/all_to_all | solution.py:638
  853.0 18.0 %collective-permute-done.79 = f32[4,288]{1,0:T(4,128)S(1)} collective-permute-done((f32[4,288]{1,0:T(4,128)S(1)}, f32[4,288]{1,0:T(4,128)S(1)}, u32[]{:S(2)}, u32[]{:S(2)}) %collective-permute-start.79) | collective-permute-done | bytes 4640 | tf_op jit(solution)/shard_map/ppermute | solution.py:451
  873.9 17.8 %collective-permute-done.80 = f32[4,288]{1,0:T(4,128)} collective-permute-done((f32[4,288]{1,0:T(4,128)S(1)}, f32[4,288]{1,0:T(4,128)}, u32[]{:S(2)}, u32[]{:S(2)}) %collective-permute-start.80) | collective-permute-done | bytes 4640 | tf_op jit(solution)/shard_map/ppermute | solution.py:451
  893.1 8.0 shard_map.260
  901.1 8.1 shard_map.259
  911.4 21.6 %collective-permute-done.81 = bf16[2,8,72,768]{3,2,1,0:T(8,128)(2,1)} collective-permute-done((bf16[2,8,72,768]{3,2,1,0:T(8,128)(2,1)S(1)}, bf16[2,8,72,768]{3,2,1,0:T(8,128)(2,1)}, u32[]{:S(2)}, u32[]{:S(2)}) %collective-permute-start.81) | collective-permute-done | bytes 1769504 | tf_op jit(solution)/shard_map/ppermute | solution.py:451
  937.4 8.0 shard_map.257
  (620 shorter events, 434.4 us)
Async XLA Ops:
  41.1 46.6 %all-to-all-start.1 = ((bf16[8,288,768]{2,1,0:T(8,128)(2,1)}), bf16[8,288,768]{2,1,0:T(8,128)(2,1)}, u32[]{:S(2)}, u32[]{:S(2)}) async-start(bf16[8,288,768]{2,1,0:T(8,128)(2,1)} %shard_map.238), calls=%async_computation.1 | async-start | bytes 7077888 | tf_op jit(solution)/shard_map/all_to_all | solution.py:638
  49.3 43.1 %collective-permute-start.4 = (bf16[512,2304]{1,0:T(8,128)(2,1)}, bf16[512,2304]{1,0:T(8,128)(2,1)}, u32[]{:S(2)}, u32[]{:S(2)}) collective-permute-start(bf16[512,2304]{1,0:T(8,128)(2,1)} %get-tuple-element.455), channel_id=1, source_target_pairs={{0,4},{4,0},{8,12},{12,8},{16,20},{20,16},{24,28},{28,24},{1,5},{5... | collective-permute-start | bytes 7077896 | tf_op jit(solution)/shard_map/ppermute | solution.py:447
  49.7 32.1 %collective-permute-start.5 = (bf16[8,72,1152]{2,1,0:T(8,128)(2,1)S(1)}, bf16[8,72,1152]{2,1,0:T(8,128)(2,1)S(1)}, u32[]{:S(2)}, u32[]{:S(2)}) collective-permute-start(bf16[8,72,1152]{2,1,0:T(8,128)(2,1)S(1)} %all-to-all-done.own), channel_id=1, source_target_pairs={{0,1},{1,2},{2,3},{4,5},{5,6},{6,7},{8,9},{9,10},{10,11},{12,13},{... | collective-permute-start | bytes 3981320 | tf_op jit(solution)/shard_map/ppermute | solution.py:455
  53.2 32.9 %collective-permute-start.6 = (bf16[8,72,1152]{2,1,0:T(8,128)(2,1)S(1)}, bf16[8,72,1152]{2,1,0:T(8,128)(2,1)}, u32[]{:S(2)}, u32[]{:S(2)}) collective-permute-start(bf16[8,72,1152]{2,1,0:T(8,128)(2,1)S(1)} %all-to-all-done.own), channel_id=1, source_target_pairs={{1,0},{2,1},{3,2},{5,4},{6,5},{7,6},{9,8},{10,9},{11,10},{13,12},{... | collective-permute-start | bytes 3981320 | tf_op jit(solution)/shard_map/ppermute | solution.py:455
  87.7 65.7 %all-to-all-start.2 = ((bf16[8,288,1152]{2,1,0:T(8,128)(2,1)}), bf16[8,288,1152]{2,1,0:T(8,128)(2,1)}, u32[]{:S(2)}, u32[]{:S(2)}) async-start(bf16[8,288,1152]{2,1,0:T(8,128)(2,1)} %shard_map.239), calls=%async_computation.2 | async-start | bytes 10616832 | tf_op jit(solution)/shard_map/all_to_all | solution.py:638
  108.1 33.6 %collective-permute-start.10 = (bf16[8,72,1152]{2,1,0:T(8,128)(2,1)}, bf16[8,72,1152]{2,1,0:T(8,128)(2,1)}, u32[]{:S(2)}, u32[]{:S(2)}) collective-permute-start(bf16[8,72,1152]{2,1,0:T(8,128)(2,1)} %collective-permute-done.6.refs_3_), channel_id=1, source_target_pairs={{1,0},{2,1},{3,2},{5,4},{6,5},{7,6},{9,8},{10,9},{11,10},{13,12},{... | collective-permute-start | bytes 3981320 | tf_op jit(solution)/shard_map/ppermute | solution.py:455
  109.4 33.2 %collective-permute-start.9 = (bf16[8,72,1152]{2,1,0:T(8,128)(2,1)S(1)}, bf16[8,72,1152]{2,1,0:T(8,128)(2,1)}, u32[]{:S(2)}, u32[]{:S(2)}) collective-permute-start(bf16[8,72,1152]{2,1,0:T(8,128)(2,1)S(1)} %collective-permute-done.5.refs_0_), channel_id=1, source_target_pairs={{0,1},{1,2},{2,3},{4,5},{5,6},{6,7},{8,9},{9,10},{10,11},{12,13},{... | collective-permute-start | bytes 3981320 | tf_op jit(solution)/shard_map/ppermute | solution.py:455
  155.7 32.8 %collective-permute-start.14 = (bf16[8,72,1152]{2,1,0:T(8,128)(2,1)}, bf16[8,72,1152]{2,1,0:T(8,128)(2,1)S(1)}, u32[]{:S(2)}, u32[]{:S(2)}) collective-permute-start(bf16[8,72,1152]{2,1,0:T(8,128)(2,1)} %collective-permute-done.9.refs_1_), channel_id=1, source_target_pairs={{0,1},{1,2},{2,3},{4,5},{5,6},{6,7},{8,9},{9,10},{10,11},{12,13},{... | collective-permute-start | bytes 3981320 | tf_op jit(solution)/shard_map/ppermute | solution.py:455
  159.3 33.3 %collective-permute-start.15 = (bf16[8,72,1152]{2,1,0:T(8,128)(2,1)}, bf16[8,72,1152]{2,1,0:T(8,128)(2,1)S(1)}, u32[]{:S(2)}, u32[]{:S(2)}) collective-permute-start(bf16[8,72,1152]{2,1,0:T(8,128)(2,1)} %collective-permute-done.10.refs_4_), channel_id=1, source_target_pairs={{1,0},{2,1},{3,2},{5,4},{6,5},{7,6},{9,8},{10,9},{11,10},{13,12},{... | collective-permute-start | bytes 3981320 | tf_op jit(solution)/shard_map/ppermute | solution.py:455
  202.7 79.4 %all-to-all-start.3 = ((bf16[8,288,1152]{2,1,0:T(8,128)(2,1)}), bf16[8,288,1152]{2,1,0:T(8,128)(2,1)}, u32[]{:S(2)}, u32[]{:S(2)}) async-start(bf16[8,288,1152]{2,1,0:T(8,128)(2,1)} %shard_map.240), calls=%async_computation.3 | async-start | bytes 10616832 | tf_op jit(solution)/shard_map/all_to_all | solution.py:638
  212.4 67.9 %collective-permute-start.18 = (bf16[128,2304]{1,0:T(8,128)(2,1)S(1)}, bf16[128,2304]{1,0:T(8,128)(2,1)S(1)}, u32[]{:S(2)}, u32[]{:S(2)}) collective-permute-start(bf16[128,2304]{1,0:T(8,128)(2,1)S(1)} %multiply_convert_fusion.1), channel_id=1, source_target_pairs={{0,8},{4,12},{8,0},{12,4},{16,24},{20,28},{24,16},{28,20},{1,9},{5... | collective-permute-start | bytes 1769480 | tf_op jit(solution)/shard_map/ppermute | solution.py:447
  214.4 65.9 %collective-permute-start.19 = (bf16[128,2304]{1,0:T(8,128)(2,1)S(1)}, bf16[128,2304]{1,0:T(8,128)(2,1)S(1)}, u32[]{:S(2)}, u32[]{:S(2)}) collective-permute-start(bf16[128,2304]{1,0:T(8,128)(2,1)S(1)} %multiply_convert_fusion.1), channel_id=1, source_target_pairs={{0,16},{4,20},{8,24},{12,28},{16,0},{20,4},{24,8},{28,12},{1,17},{... | collective-permute-start | bytes 1769480 | tf_op jit(solution)/shard_map/ppermute | solution.py:447
  215.8 64.4 %collective-permute-start.20 = (bf16[128,2304]{1,0:T(8,128)(2,1)S(1)}, bf16[128,2304]{1,0:T(8,128)(2,1)S(1)}, u32[]{:S(2)}, u32[]{:S(2)}) collective-permute-start(bf16[128,2304]{1,0:T(8,128)(2,1)S(1)} %multiply_convert_fusion.1), channel_id=1, source_target_pairs={{0,2},{1,3},{2,0},{3,1},{4,6},{5,7},{6,4},{7,5},{8,10},{9,11},{10,... | collective-permute-start | bytes 1769480 | tf_op jit(solution)/shard_map/ppermute | solution.py:451
  218.3 63.7 %collective-permute-start.21 = (bf16[128,2304]{1,0:T(8,128)(2,1)S(1)}, bf16[128,2304]{1,0:T(8,128)(2,1)}, u32[]{:S(2)}, u32[]{:S(2)}) collective-permute-start(bf16[128,2304]{1,0:T(8,128)(2,1)S(1)} %multiply_convert_fusion.1), channel_id=1, source_target_pairs={{0,3},{1,2},{2,1},{3,0},{4,7},{5,6},{6,5},{7,4},{8,11},{9,10},{10,... | collective-permute-start | bytes 1769480 | tf_op jit(solution)/shard_map/ppermute | solution.py:451
  397.5 57.8 %collective-permute-start.46 = (bf16[512,2304]{1,0:T(8,128)(2,1)S(1)}, bf16[512,2304]{1,0:T(8,128)(2,1)S(1)}, u32[]{:S(2)}, u32[]{:S(2)}) collective-permute-start(bf16[512,2304]{1,0:T(8,128)(2,1)S(1)} %constant_dynamic-update-slice_fusion.29.refs_0_.refs_4_), channel_id=1, source_target_pairs={{0,4},{4,0},{8,12},{12,8},{16,20},{20,16},{24,28},{28,24},{1,5},{5... | collective-permute-start | bytes 7077896 | tf_op jit(solution)/shard_map/ppermute | solution.py:447
  455.4 32.8 %collective-permute-start.47 = (bf16[256,2304]{1,0:T(8,128)(2,1)S(1)}, bf16[256,2304]{1,0:T(8,128)(2,1)S(1)}, u32[]{:S(2)}, u32[]{:S(2)}) collective-permute-start(bf16[256,2304]{1,0:T(8,128)(2,1)S(1)} %constant_dynamic-update-slice_fusion.33), channel_id=1, source_target_pairs={{0,8},{4,12},{8,0},{12,4},{16,24},{20,28},{24,16},{28,20},{1,9},{5... | collective-permute-start | bytes 3538952 | tf_op jit(solution)/shard_map/ppermute | solution.py:447
  455.9 32.3 %collective-permute-start.48 = (bf16[256,2304]{1,0:T(8,128)(2,1)S(1)}, bf16[256,2304]{1,0:T(8,128)(2,1)S(1)}, u32[]{:S(2)}, u32[]{:S(2)}) collective-permute-start(bf16[256,2304]{1,0:T(8,128)(2,1)S(1)} %constant_dynamic-update-slice_fusion.33), channel_id=1, source_target_pairs={{0,16},{4,20},{8,24},{12,28},{16,0},{20,4},{24,8},{28,12},{1,17},{... | collective-permute-start | bytes 3538952 | tf_op jit(solution)/shard_map/ppermute | solution.py:447
  499.0 40.9 %collective-permute-start.54 = (bf16[128,2304]{1,0:T(8,128)(2,1)}, bf16[128,2304]{1,0:T(8,128)(2,1)}, u32[]{:S(2)}, u32[]{:S(2)}) collective-permute-start(bf16[128,2304]{1,0:T(8,128)(2,1)} %get-tuple-element.401), channel_id=1, source_target_pairs={{0,1},{1,0},{2,3},{3,2},{4,5},{5,4},{6,7},{7,6},{8,9},{9,8},{10,11... | collective-permute-start | bytes 1769480 | tf_op jit(solution)/shard_map/ppermute | solution.py:451
  500.8 39.1 %collective-permute-start.55 = (bf16[128,2304]{1,0:T(8,128)(2,1)S(1)}, bf16[128,2304]{1,0:T(8,128)(2,1)}, u32[]{:S(2)}, u32[]{:S(2)}) collective-permute-start(bf16[128,2304]{1,0:T(8,128)(2,1)S(1)} %get-tuple-element.400), channel_id=1, source_target_pairs={{0,1},{1,0},{2,3},{3,2},{4,5},{5,4},{6,7},{7,6},{8,9},{9,8},{10,11... | collective-permute-start | bytes 1769480 | tf_op jit(solution)/shard_map/ppermute | solution.py:451
  589.4 34.3 %collective-permute-start.62 = (bf16[128,2304]{1,0:T(8,128)(2,1)S(1)}, bf16[128,2304]{1,0:T(8,128)(2,1)S(1)}, u32[]{:S(2)}, u32[]{:S(2)}) collective-permute-start(bf16[128,2304]{1,0:T(8,128)(2,1)S(1)} %subtract_convert_fusion), channel_id=1, source_target_pairs={{0,8},{4,12},{8,0},{12,4},{16,24},{20,28},{24,16},{28,20},{1,9},{5... | collective-permute-start | bytes 1769480 | tf_op jit(solution)/shard_map/ppermute | solution.py:447
  590.7 33.0 %collective-permute-start.63 = (bf16[128,2304]{1,0:T(8,128)(2,1)S(1)}, bf16[128,2304]{1,0:T(8,128)(2,1)S(1)}, u32[]{:S(2)}, u32[]{:S(2)}) collective-permute-start(bf16[128,2304]{1,0:T(8,128)(2,1)S(1)} %subtract_convert_fusion), channel_id=1, source_target_pairs={{0,16},{4,20},{8,24},{12,28},{16,0},{20,4},{24,8},{28,12},{1,17},{... | collective-permute-start | bytes 1769480 | tf_op jit(solution)/shard_map/ppermute | solution.py:447
  666.6 76.9 %all-to-all-start.4 = ((bf16[8,288,1152]{2,1,0:T(8,128)(2,1)}), bf16[8,288,1152]{2,1,0:T(8,128)(2,1)}, u32[]{:S(2)}, u32[]{:S(2)}) async-start(bf16[8,288,1152]{2,1,0:T(8,128)(2,1)} %bitcast.83), calls=%async_computation.4 | async-start | bytes 10616832 | tf_op jit(solution)/shard_map/all_to_all | solution.py:638
  696.3 44.5 %collective-permute-start.74 = (bf16[8,2,72,512]{3,2,0,1:T(8,128)(2,1)}, bf16[8,2,72,512]{3,2,0,1:T(8,128)(2,1)}, u32[]{:S(2)}, u32[]{:S(2)}) collective-permute-start(bf16[8,2,72,512]{3,2,0,1:T(8,128)(2,1)} %copy_bitcast_fusion), channel_id=1, source_target_pairs={{0,1},{1,0},{2,3},{3,2},{4,5},{5,4},{6,7},{7,6},{8,9},{9,8},{10,11... | collective-permute-start | bytes 3538952 | tf_op jit(solution)/shard_map/ppermute | solution.py:451
  696.3 48.1 %collective-permute-start.72 = (bf16[128,2304]{1,0:T(8,128)(2,1)}, bf16[128,2304]{1,0:T(8,128)(2,1)}, u32[]{:S(2)}, u32[]{:S(2)}) collective-permute-start(bf16[128,2304]{1,0:T(8,128)(2,1)} %pad_maximum_fusion.11), channel_id=1, source_target_pairs={{0,8},{4,12},{8,0},{12,4},{16,24},{20,28},{24,16},{28,20},{1,9},{5... | collective-permute-start | bytes 1769480 | tf_op jit(solution)/shard_map/ppermute | solution.py:447
  698.1 46.3 %collective-permute-start.73 = (bf16[128,2304]{1,0:T(8,128)(2,1)}, bf16[128,2304]{1,0:T(8,128)(2,1)}, u32[]{:S(2)}, u32[]{:S(2)}) collective-permute-start(bf16[128,2304]{1,0:T(8,128)(2,1)} %pad_maximum_fusion.12), channel_id=1, source_target_pairs={{0,16},{4,20},{8,24},{12,28},{16,0},{20,4},{24,8},{28,12},{1,17},{... | collective-permute-start | bytes 1769480 | tf_op jit(solution)/shard_map/ppermute | solution.py:447
  744.4 73.2 %all-to-all-start.5 = ((bf16[8,288,1152]{2,1,0:T(8,128)(2,1)}), bf16[8,288,1152]{2,1,0:T(8,128)(2,1)}, u32[]{:S(2)}, u32[]{:S(2)}) async-start(bf16[8,288,1152]{2,1,0:T(8,128)(2,1)} %bitcast.85), calls=%async_computation.5 | async-start | bytes 10616832 | tf_op jit(solution)/shard_map/all_to_all | solution.py:638
  751.3 64.6 %collective-permute-start.77 = (bf16[64,2304]{1,0:T(8,128)(2,1)}, bf16[64,2304]{1,0:T(8,128)(2,1)}, u32[]{:S(2)}, u32[]{:S(2)}) collective-permute-start(bf16[64,2304]{1,0:T(8,128)(2,1)} %add_convert_fusion.1), channel_id=1, source_target_pairs={{0,8},{4,12},{8,0},{12,4},{16,24},{20,28},{24,16},{28,20},{1,9},{5... | collective-permute-start | bytes 884744 | tf_op jit(solution)/shard_map/ppermute | solution.py:447
  755.2 60.7 %collective-permute-start.76 = (bf16[64,2304]{1,0:T(8,128)(2,1)}, bf16[64,2304]{1,0:T(8,128)(2,1)}, u32[]{:S(2)}, u32[]{:S(2)}) collective-permute-start(bf16[64,2304]{1,0:T(8,128)(2,1)} %add_convert_fusion.2), channel_id=1, source_target_pairs={{0,16},{4,20},{8,24},{12,28},{16,0},{20,4},{24,8},{28,12},{1,17},{... | collective-permute-start | bytes 884744 | tf_op jit(solution)/shard_map/ppermute | solution.py:447
  761.2 56.3 %collective-permute-start.75 = (bf16[8,72,512]{2,1,0:T(8,128)(2,1)S(1)}, bf16[8,72,512]{2,1,0:T(8,128)(2,1)S(1)}, u32[]{:S(2)}, u32[]{:S(2)}) collective-permute-start(bf16[8,72,512]{2,1,0:T(8,128)(2,1)S(1)} %dynamic-slice_bitcast_fusion), channel_id=1, source_target_pairs={{0,2},{1,3},{2,0},{3,1},{4,6},{5,7},{6,4},{7,5},{8,10},{9,11},{10,... | collective-permute-start | bytes 1769480 | tf_op jit(solution)/shard_map/ppermute | solution.py:451
  844.9 92.5 %all-to-all-start.8 = ((bf16[8,288,1152]{2,1,0:T(8,128)(2,1)}), bf16[8,288,1152]{2,1,0:T(8,128)(2,1)}, u32[]{:S(2)}, u32[]{:S(2)}) async-start(bf16[8,288,1152]{2,1,0:T(8,128)(2,1)} %bitcast.84), calls=%async_computation.8 | async-start | bytes 10616832 | tf_op jit(solution)/shard_map/all_to_all | solution.py:638
  849.6 42.9 %collective-permute-start.78 = (bf16[8,72,768]{2,1,0:T(8,128)(2,1)S(1)}, bf16[8,72,768]{2,1,0:T(8,128)(2,1)S(1)}, u32[]{:S(2)}, u32[]{:S(2)}) collective-permute-start(bf16[8,72,768]{2,1,0:T(8,128)(2,1)S(1)} %all_to_all.45), channel_id=1, source_target_pairs={{0,2},{1,3},{2,0},{3,1},{4,6},{5,7},{6,4},{7,5},{8,10},{9,11},{10,... | collective-permute-start | bytes 2654216 | tf_op jit(solution)/shard_map/ppermute | solution.py:451
  893.0 40.1 %collective-permute-start.81 = (bf16[2,8,72,768]{3,2,1,0:T(8,128)(2,1)S(1)}, bf16[2,8,72,768]{3,2,1,0:T(8,128)(2,1)}, u32[]{:S(2)}, u32[]{:S(2)}) collective-permute-start(bf16[2,8,72,768]{3,2,1,0:T(8,128)(2,1)S(1)} %reverse_select_fusion.1), channel_id=1, source_target_pairs={{0,1},{1,0},{2,3},{3,2},{4,5},{5,4},{6,7},{7,6},{8,9},{9,8},{10,11... | collective-permute-start | bytes 5308424 | tf_op jit(solution)/shard_map/ppermute | solution.py:451
  (189 other events, 2563.5 us)

commit v4 on v3

--- a/solution.py
+++ b/solution.py
@@ -436,8 +436,8 @@
 
 
 VMEM_BYTES = 56 * 1024 * 1024
-TILE_VMEM_BYTES = 18 * 1024 * 1024
-CROSS_VMEM_BYTES = 38 * 1024 * 1024
+TILE_VMEM_BYTES = 16 * 1024 * 1024
+CROSS_VMEM_BYTES = 36 * 1024 * 1024
 GELU_RATE = 0.7978845608028654
 TILE = 256
 CHUNK = 768
@@ -968,7 +968,8 @@
         return back_project(halves, w_down, factors, scale_down)
 
     def cut(rows):
-        return [rows[i * block_rows : (i + 1) * block_rows] for i in range(4)]
+        middle = 2 * block_rows
+        return rows[:middle], rows[middle : middle + block_rows], rows[middle + block_rows :]
 
     (mixed, *factors), pair_mid_near, mid_cuts = pin(
         up_again(mid_mine, mid_theirs),
@@ -978,15 +979,15 @@
     ffn_core, pair_mid_mine, third_mid_first = pin(
         scatter_core(lambda side, kind: partial_product([(mixed, w_down)], side, kind)),
         gather_far(*pair_mid_near),
-        [row_swap(rows, 1) for rows in mid_cuts[:2]],
+        row_swap(mid_cuts[0], 1),
     )
     ffn_near, pair_mid_theirs, third_mid_second = pin(
-        scatter_near(*ffn_core), seq_swap(pair_mid_mine, 1), row_swap(mid_cuts[2], 1)
+        scatter_near(*ffn_core), seq_swap(pair_mid_mine, 1), row_swap(mid_cuts[1], 1)
     )
     ffn_proj, third_mid_last, pair_mid_mine = pin(
-        scale_down * scatter_far(*ffn_near), row_swap(mid_cuts[3], 1), pair_mid_mine
-    )
-    third_mid_mine = jnp.concatenate([*third_mid_first, third_mid_second, third_mid_last])
+        scale_down * scatter_far(*ffn_near), row_swap(mid_cuts[2], 1), pair_mid_mine
+    )
+    third_mid_mine = jnp.concatenate([third_mid_first, third_mid_second, third_mid_last])
     block_out = bf(middle + norm_gain(ffn_proj, gain_ffw_out))
     grad_ffn, grad_gain_four = norm_back(ffn_proj, gain_ffw_out, upstream)
     grad_ffn_low = bf(grad_ffn)
@@ -1001,19 +1002,19 @@
         seq_swap(third_mid_mine, 1),
         up_again(pair_mid_theirs),
     )
-    grad_cuts = cut(grad_mine)
+    grad_cuts = grad_mine[: 2 * block_rows], grad_mine[2 * block_rows :]
     grads_hidden, pair_grad_near, third_grad_first = pin(
         back_again((grad_mine, grad_theirs), factors),
         gather_near(jnp.concatenate([grad_two, grad_three])),
-        [row_swap(rows, 1) for rows in grad_cuts[:2]],
+        row_swap(grad_cuts[0], 1),
     )
     pairs = list(zip(grads_hidden, (w_gate, w_up)))
     mid_core, pair_grad_mine, third_grad_last = pin(
         scatter_core(lambda side, kind: partial_product(pairs, side, kind)),
         gather_far(*pair_grad_near),
-        [row_swap(rows, 1) for rows in grad_cuts[2:]],
-    )
-    third_grad_mine = jnp.concatenate([*third_grad_first, *third_grad_last])
+        row_swap(grad_cuts[1], 1),
+    )
+    third_grad_mine = jnp.concatenate([third_grad_first, third_grad_last])
     sum_near, pair_grad_theirs, third_grad_theirs, (third_mixed, *third_factors), mine_hidden = pin(
         scatter_near(*mid_core),
         seq_swap(pair_grad_mine, 1),
@@ -1117,25 +1118,34 @@
     grad_tokens, grad_gain_one = norm_back(tokens, gain_attn_in, grad_in)
     grad_input = grad_middle + grad_tokens
     gain_terms = jnp.stack([grad_gain_one, grad_gain_two, grad_gain_three, grad_gain_four])
-    gain_blocks = trade(gain_terms.reshape(4, 8, model_rows).transpose(1, 0, 2))
-    sums, gain_blocks, up_blocks = pin(
-        trade(jnp.concatenate([in_sum, out_sum], axis=2)), gain_blocks, up_blocks
-    )
+    sums = jnp.concatenate([in_sum, out_sum], axis=2)
+    own_rows, columns = sums.shape[1:]
+    gain_terms = bf(gain_terms.reshape(4, 8, model_rows).transpose(1, 0, 2)).reshape(8, -1)
+    gain_rows = -(-gain_terms.shape[1] // columns // 8) * 8
+    gain_terms = jnp.pad(gain_terms, ((0, 0), (0, gain_rows * columns - gain_terms.shape[1])))
+    sums = jnp.concatenate([sums, gain_terms.reshape(8, gain_rows, columns)], axis=1)
+    sums, up_blocks = pin(trade(sums), up_blocks)
     up_blocks = trade(up_blocks[0])
-
-    def double(blocks, bit, side):
-        both_sides = jnp.stack([blocks, row_swap(blocks, bit)])
+    gain_blocks = wide(sums[:, own_rows:]).reshape(8, -1)[:, : 4 * model_rows]
+    gain_blocks = gain_blocks.reshape(8, 4, model_rows)
+    sums = sums[:, :own_rows]
+
+    def double(blocks, received, side):
+        both_sides = jnp.stack([blocks, received])
         return jnp.where(side == 0, both_sides, both_sides[::-1])
 
     gains = jnp.sum(gain_blocks, axis=0)
     gains = gains + row_swap(gains, 1)
-    blocks, gains = pin(double(sums, 2, high_bit), gains + row_swap(gains, 2))
-    blocks = double(blocks, 1, low_bit).transpose(1, 0, 2, 3, 4)
+    blocks, gains = pin(
+        double(sums, row_swap(sums, 2), high_bit), gains + row_swap(gains, 2)
+    )
+    received = row_swap(blocks, 1)
     grad_w_gate, grad_w_up, grad_w_down = (
         unpack_blocks(blocks, [hidden_part])[0]
         for blocks in (gate_blocks[None], up_blocks[None], down_blocks[None])
     )
     blocks, grad_w_up = pin(blocks, grad_w_up)
+    blocks = double(blocks, received, low_bit).transpose(1, 0, 2, 3, 4)
     attn_grads = unpack_blocks(blocks.reshape(4, *sums.shape), [head, half, half, head])
 
     return (

time: 965 us -> 950 us (0.984)
    ppermute x20 -> x17, waiting for transfers between devices: 107 us -> 88.8 us  [row_swap(): lax.ppermute(block, 'row', [(place, place ^ bit) for place in range(4)])]
    ppermute x56, waiting for transfers between devices: 150 us -> 164 us  [seq_swap(): lax.ppermute(block, 'seq', [(place, place ^ bit) for place in range(8)])]
    all_to_all x8 -> x7, waiting for transfers between devices: 21.8 us -> 17 us  [trade(): return lax.all_to_all(blocks, 'seq', 0, 0, tiled=True)]
    all_to_all x8 -> x7, starting transfers between devices: 36.2 us -> 32.2 us  [trade(): return lax.all_to_all(blocks, 'seq', 0, 0, tiled=True)]
    ppermute x20 -> x17, starting transfers between devices: 30.2 us -> 26.6 us  [row_swap(): lax.ppermute(block, 'row', [(place, place ^ bit) for place in range(4)])]
    unnamed x295 -> x284, local copies, waits for them, and re-layouts: 36.2 us -> 33.5 us
  transfers between devices with their start and end apart: 90 -> 86, of which waited for: 45 -> 46; matrix products, arithmetic and copies ran while one was open for 13% -> 12% of each run, Pallas kernels for 27% -> 29%
where the time goes in v4:
time: 950 us; the launch traced here: 939 us
  waiting for transfers between devices  328 us (35%)
  Pallas kernels  290 us (31%)
  starting transfers between devices  127 us (13%)
  local copies, waits for them, and re-layouts  65.1 us (7%)
  other arithmetic  63.1 us (7%)
  matrix products  44.6 us (5%)
  blocking collectives  17.2 us (2%)
    ppermute x56, waiting for transfers between devices, seq_swap(): lax.ppermute(block, 'seq', [(place, place ^ bit) for place in range(8)])  164 us
    pallas_call x12, Pallas kernels, tile_calls(): pl.pallas_call(kernel, grid=grid, in_specs=in_specs, out_specs=out_specs,...  132 us
    pallas_call x3, Pallas kernels, cross_products(): pl.pallas_call(functools.partial(cross_kernel, steps, len(lefts), len(rig...  94.6 us
    ppermute x17, waiting for transfers between devices, row_swap(): lax.ppermute(block, 'row', [(place, place ^ bit) for place in range(4)])  88.8 us
    ppermute x6, waiting for transfers between devices, row_shift(): lax.ppermute(block, 'row', [(place, place + step) for place in range(4) i...  58.4 us
    ppermute x56, starting transfers between devices, seq_swap(): lax.ppermute(block, 'seq', [(place, place ^ bit) for place in range(8)])  50.9 us
    unnamed x284, local copies, waits for them, and re-layouts  33.5 us
    all_to_all x7, starting transfers between devices, trade(): return lax.all_to_all(blocks, 'seq', 0, 0, tiled=True)  32.2 us
  transfers between devices with their start and end apart: 86, of which 46 were waited for; matrix products, arithmetic and copies ran while one was open for 12% of the time, Pallas kernels for 29%

profile of v4, /device:TPU:0, one launch (start us, length us, event | category | flops | bytes accessed | tf_op | source)
XLA Modules:
  0.0 938.5 jit_solution(11919809702486004667)
XLA Ops:
  22.2 7.2 shard_map.238
  54.6 8.8 shard_map.239
  63.4 8.8 shard_map.240
  72.5 9.3 collective-permute-done.5.refs_0_
  126.0 15.7 %collective-permute-done.10.refs_4_ = bf16[8,72,1152]{2,1,0:T(8,128)(2,1)} collective-permute-done((bf16[8,72,1152]{2,1,0:T(8,128)(2,1)}, bf16[8,72,1152]{2,1,0:T(8,128)(2,1)}, u32[]{:S(2)}, u32[]{:S(2)}) %collective-permute-start.10) | collective-permute-done | bytes 1327136 | tf_op jit(solution)/shard_map/ppermute | solution.py:455
  142.6 10.8 %all-to-all-done.2 = bf16[8,288,1152]{2,1,0:T(8,128)(2,1)} async-done(((bf16[8,288,1152]{2,1,0:T(8,128)(2,1)}), bf16[8,288,1152]{2,1,0:T(8,128)(2,1)}, u32[]{:S(2)}, u32[]{:S(2)}) %all-to-all-start.2) | async-done | bytes 5308448 | tf_op jit(solution)/shard_map/all_to_all | solution.py:638
  164.5 24.0 %collective-permute-done.14.refs_2_ = bf16[8,72,1152]{2,1,0:T(8,128)(2,1)S(1)} collective-permute-done((bf16[8,72,1152]{2,1,0:T(8,128)(2,1)}, bf16[8,72,1152]{2,1,0:T(8,128)(2,1)S(1)}, u32[]{:S(2)}, u32[]{:S(2)}) %collective-permute-start.14) | collective-permute-done | bytes 1327136 | tf_op jit(solution)/shard_map/ppermute | solution.py:455
  194.1 7.0 collective-permute-done.17
  219.7 60.6 %collective-permute-done.18 = bf16[128,2304]{1,0:T(8,128)(2,1)S(1)} collective-permute-done((bf16[128,2304]{1,0:T(8,128)(2,1)S(1)}, bf16[128,2304]{1,0:T(8,128)(2,1)S(1)}, u32[]{:S(2)}, u32[]{:S(2)}) %collective-permute-start.18) | collective-permute-done | bytes 589856 | tf_op jit(solution)/shard_map/ppermute | solution.py:447
  299.9 20.7 %shard_map.242 = (bf16[1024,1152]{1,0:T(8,128)(2,1)S(1)}, bf16[1024,1152]{1,0:T(8,128)(2,1)S(1)}, bf16[1024,1152]{1,0:T(8,128)(2,1)S(1)}) custom-call(bf16[512,2304]{1,0:T(8,128)(2,1)S(1)} %constant_dynamic-update-slice_fusion.12.refs_0_, bf16[512,2304]{1,0:T(8,128)(2,1)S(1)} %collective-permute-done.24.refs_1_, bf16[2304,1152]{1,0:T(8,128)(2,1)} %bitcast.6.refs_2_.refs_1_, ...), custom_call_target="tpu_custom_call" | custom-call | flops 1 | bytes 1 | tf_op jit(solution)/shard_map/pallas_call | solution.py:673
  335.7 11.8 %collective-permute-done.28 = bf16[128,2304]{1,0:T(8,128)(2,1)S(1)} collective-permute-done((bf16[128,2304]{1,0:T(8,128)(2,1)S(1)}, bf16[128,2304]{1,0:T(8,128)(2,1)S(1)}, u32[]{:S(2)}, u32[]{:S(2)}) %collective-permute-start.28) | collective-permute-done | bytes 589856 | tf_op jit(solution)/shard_map/ppermute | solution.py:447
  353.3 8.7 collective-permute-done.30
  366.0 12.1 %collective-permute-done.34 = bf16[128,2304]{1,0:T(8,128)(2,1)S(1)} collective-permute-done((bf16[128,2304]{1,0:T(8,128)(2,1)S(1)}, bf16[128,2304]{1,0:T(8,128)(2,1)S(1)}, u32[]{:S(2)}, u32[]{:S(2)}) %collective-permute-start.34) | collective-permute-done | bytes 589856 | tf_op jit(solution)/shard_map/ppermute | solution.py:451
  397.5 18.7 %shard_map.245 = (bf16[1024,1152]{1,0:T(8,128)(2,1)S(1)}, bf16[1024,1152]{1,0:T(8,128)(2,1)S(1)}, bf16[1024,1152]{1,0:T(8,128)(2,1)S(1)}) custom-call(bf16[1024,2304]{1,0:T(8,128)(2,1)S(1)} %constant_dynamic-update-slice_fusion.19.refs_0_.refs_2_, bf16[2304,1152]{1,0:T(8,128)(2,1)} %bitcast.6.refs_2_.refs_1_, bf16[2304,1152]{1,0:T(8,128)(2,1)} %bitcast.7.refs_3_.refs_2_), custom_call_target="tpu_custom_call" | custom-call | flops 1 | bytes 1 | tf_op jit(solution)/shard_map/pallas_call | solution.py:673
  434.4 18.0 %shard_map.246 = (bf16[1024,1152]{1,0:T(8,128)(2,1)S(1)}, bf16[1024,1152]{1,0:T(8,128)(2,1)S(1)}, bf16[1024,1152]{1,0:T(8,128)(2,1)S(1)}) custom-call(bf16[1024,2304]{1,0:T(8,128)(2,1)S(1)} %collective-permute-done.33.refs_0_.refs_3_, bf16[2304,1152]{1,0:T(8,128)(2,1)} %bitcast.6.refs_2_.refs_1_, bf16[2304,1152]{1,0:T(8,128)(2,1)} %bitcast.7.refs_3_.refs_2_), custom_call_target="tpu_custom_call" | custom-call | flops 1 | bytes 1 | tf_op jit(solution)/shard_map/pallas_call | solution.py:673
  463.1 7.0 shard_map.247
  470.1 13.3 %collective-permute-done.46 = bf16[256,2304]{1,0:T(8,128)(2,1)S(1)} collective-permute-done((bf16[256,2304]{1,0:T(8,128)(2,1)S(1)}, bf16[256,2304]{1,0:T(8,128)(2,1)S(1)}, u32[]{:S(2)}, u32[]{:S(2)}) %collective-permute-start.46) | collective-permute-done | bytes 1179680 | tf_op jit(solution)/shard_map/ppermute | solution.py:447
  488.3 11.0 %shard_map.249 = bf16[512,2304]{1,0:T(8,128)(2,1)S(1)} custom-call(bf16[1024,1152]{1,0:T(8,128)(2,1)S(1)} %get-tuple-element.268.refs_0_.refs_6_, bf16[2304,1152]{1,0:T(8,128)(2,1)} %bitcast.6.refs_2_.refs_1_, bf16[1024,1152]{1,0:T(8,128)(2,1)S(1)} %get-tuple-element.338.refs_2_.refs_6_, bf16[2304,1152]{1,0:T(8,128)(2,1)} %bitcast.7.refs_3_.refs_2_), custom_call_target="tpu_custom_call" | custom-call | flops 1 | bytes 1 | tf_op jit(solution)/shard_map/pallas_call | solution.py:673
  501.2 10.5 %shard_map.248 = f32[512,2304]{1,0:T(8,128)S(1)} custom-call(bf16[1024,1152]{1,0:T(8,128)(2,1)S(1)} %get-tuple-element.268.refs_0_.refs_6_, bf16[2304,1152]{1,0:T(8,128)(2,1)} %bitcast.6.refs_2_.refs_1_, bf16[1024,1152]{1,0:T(8,128)(2,1)S(1)} %get-tuple-element.338.refs_2_.refs_6_, bf16[2304,1152]{1,0:T(8,128)(2,1)} %bitcast.7.refs_3_.refs_2_), custom_call_target="tpu_custom_call" | custom-call | flops 1 | bytes 1 | tf_op jit(solution)/shard_map/pallas_call | solution.py:673
  514.4 12.9 %collective-permute-done.50 = bf16[128,2304]{1,0:T(8,128)(2,1)S(1)} collective-permute-done((bf16[128,2304]{1,0:T(8,128)(2,1)S(1)}, bf16[128,2304]{1,0:T(8,128)(2,1)S(1)}, u32[]{:S(2)}, u32[]{:S(2)}) %collective-permute-start.50) | collective-permute-done | bytes 589856 | tf_op jit(solution)/shard_map/ppermute | solution.py:447
  544.3 18.2 %shard_map.250 = (bf16[1024,1152]{1,0:T(8,128)(2,1)S(1)}, bf16[1024,1152]{1,0:T(8,128)(2,1)S(1)}, bf16[1024,1152]{1,0:T(8,128)(2,1)S(1)}) custom-call(bf16[512,2304]{1,0:T(8,128)(2,1)S(1)} %constant_dynamic-update-slice_fusion.29.refs_0_.refs_4_, bf16[512,2304]{1,0:T(8,128)(2,1)S(1)} %collective-permute-done.45.refs_1_.refs_5_, ...), custom_call_target="tpu_custom_call" | custom-call | flops 1 | bytes 1 | tf_op jit(solution)/shard_map/pallas_call | solution.py:673
  591.1 31.8 %shard_map.253 = bf16[1,8,288,1152]{3,2,1,0:T(8,128)(2,1)} custom-call(bf16[512,2304]{1,0:T(8,128)(2,1)S(1)} %constant_dynamic-update-slice_fusion.24.refs_0_, bf16[512,2304]{1,0:T(8,128)(2,1)S(1)} %copy-done.28, bf16[1024,2304]{1,0:T(8,128)(2,1)} %copy-done.8, bf16[1024,2304]{1,0:T(8,128)(2,1)} %copy-done.21, bf16[512,2304]{1,0:T(8,128)(2,1)S(1)} %copy-done.23, ...), custom_call_target="tpu_custom_call" | custom-call | flops 1 | bytes 1 | tf_op jit(solution)/shard_map/pallas_call | solution.py:810
  707.2 31.4 %shard_map.255 = bf16[1,8,288,1152]{3,2,1,0:T(8,128)(2,1)} custom-call(bf16[512,2304]{1,0:T(8,128)(2,1)S(1)} %copy-done.3, bf16[512,2304]{1,0:T(8,128)(2,1)S(1)} %copy-done.14, bf16[1024,2304]{1,0:T(8,128)(2,1)} %copy-done.1, bf16[1024,2304]{1,0:T(8,128)(2,1)} %copy-done.4, bf16[512,2304]{1,0:T(8,128)(2,1)S(1)} %copy-done.6, ...), custom_call_target="tpu_custom_call" | custom-call | flops 1 | bytes 1 | tf_op jit(solution)/shard_map/pallas_call | solution.py:810
  772.4 31.4 %shard_map.256 = bf16[1,8,288,1152]{3,2,1,0:T(8,128)(2,1)} custom-call(bf16[512,2304]{1,0:T(8,128)(2,1)S(1)} %copy-done.3, bf16[512,2304]{1,0:T(8,128)(2,1)S(1)} %copy-done.15, bf16[1024,2304]{1,0:T(8,128)(2,1)} %copy-done.1, bf16[1024,2304]{1,0:T(8,128)(2,1)} %copy-done.4, bf16[512,2304]{1,0:T(8,128)(2,1)S(1)} %copy-done.7, ...), custom_call_target="tpu_custom_call" | custom-call | flops 1 | bytes 1 | tf_op jit(solution)/shard_map/pallas_call | solution.py:810
  803.8 10.9 %collective-permute-done.74 = bf16[64,2304]{1,0:T(8,128)(2,1)} collective-permute-done((bf16[64,2304]{1,0:T(8,128)(2,1)}, bf16[64,2304]{1,0:T(8,128)(2,1)}, u32[]{:S(2)}, u32[]{:S(2)}) %collective-permute-start.74) | collective-permute-done | bytes 294944 | tf_op jit(solution)/shard_map/ppermute | solution.py:447
  818.3 17.2 %all_to_all.40 = bf16[8,80,768]{2,1,0:T(8,128)(2,1)S(1)} all-to-all(bf16[8,80,768]{2,1,0:T(8,128)(2,1)S(1)} %pad_maximum_fusion.4), channel_id=1, replica_groups=mesh['seq'=8,'row'=4] {'seq'}, dimensions={0} | all-to-all | bytes 1966080 | tf_op jit(solution)/shard_map/all_to_all | solution.py:638
  844.1 18.4 %collective-permute-done.76 = f32[4,288]{1,0:T(4,128)S(1)} collective-permute-done((f32[4,288]{1,0:T(4,128)S(1)}, f32[4,288]{1,0:T(4,128)S(1)}, u32[]{:S(2)}, u32[]{:S(2)}) %collective-permute-start.76) | collective-permute-done | bytes 4640 | tf_op jit(solution)/shard_map/ppermute | solution.py:451
  865.5 18.3 %collective-permute-done.77 = f32[4,288]{1,0:T(4,128)S(1)} collective-permute-done((f32[4,288]{1,0:T(4,128)S(1)}, f32[4,288]{1,0:T(4,128)S(1)}, u32[]{:S(2)}, u32[]{:S(2)}) %collective-permute-start.77) | collective-permute-done | bytes 4640 | tf_op jit(solution)/shard_map/ppermute | solution.py:451
  886.5 8.0 shard_map.260
  894.5 8.1 shard_map.259
  904.8 8.0 shard_map.257
  912.8 14.2 %collective-permute-done.78 = bf16[2,8,72,768]{3,2,1,0:T(8,128)(2,1)} collective-permute-done((bf16[2,8,72,768]{3,2,1,0:T(8,128)(2,1)S(1)}, bf16[2,8,72,768]{3,2,1,0:T(8,128)(2,1)}, u32[]{:S(2)}, u32[]{:S(2)}) %collective-permute-start.78) | collective-permute-done | bytes 1769504 | tf_op jit(solution)/shard_map/ppermute | solution.py:451
  (608 shorter events, 421.9 us)
Async XLA Ops:
  41.1 46.6 %all-to-all-start.1 = ((bf16[8,288,768]{2,1,0:T(8,128)(2,1)}), bf16[8,288,768]{2,1,0:T(8,128)(2,1)}, u32[]{:S(2)}, u32[]{:S(2)}) async-start(bf16[8,288,768]{2,1,0:T(8,128)(2,1)} %shard_map.238), calls=%async_computation.1 | async-start | bytes 7077888 | tf_op jit(solution)/shard_map/all_to_all | solution.py:638
  49.3 43.1 %collective-permute-start.4 = (bf16[512,2304]{1,0:T(8,128)(2,1)}, bf16[512,2304]{1,0:T(8,128)(2,1)}, u32[]{:S(2)}, u32[]{:S(2)}) collective-permute-start(bf16[512,2304]{1,0:T(8,128)(2,1)} %get-tuple-element.443), channel_id=1, source_target_pairs={{0,4},{4,0},{8,12},{12,8},{16,20},{20,16},{24,28},{28,24},{1,5},{5... | collective-permute-start | bytes 7077896 | tf_op jit(solution)/shard_map/ppermute | solution.py:447
  49.7 32.1 %collective-permute-start.5 = (bf16[8,72,1152]{2,1,0:T(8,128)(2,1)S(1)}, bf16[8,72,1152]{2,1,0:T(8,128)(2,1)S(1)}, u32[]{:S(2)}, u32[]{:S(2)}) collective-permute-start(bf16[8,72,1152]{2,1,0:T(8,128)(2,1)S(1)} %all-to-all-done.own), channel_id=1, source_target_pairs={{0,1},{1,2},{2,3},{4,5},{5,6},{6,7},{8,9},{9,10},{10,11},{12,13},{... | collective-permute-start | bytes 3981320 | tf_op jit(solution)/shard_map/ppermute | solution.py:455
  53.3 32.9 %collective-permute-start.6 = (bf16[8,72,1152]{2,1,0:T(8,128)(2,1)S(1)}, bf16[8,72,1152]{2,1,0:T(8,128)(2,1)}, u32[]{:S(2)}, u32[]{:S(2)}) collective-permute-start(bf16[8,72,1152]{2,1,0:T(8,128)(2,1)S(1)} %all-to-all-done.own), channel_id=1, source_target_pairs={{1,0},{2,1},{3,2},{5,4},{6,5},{7,6},{9,8},{10,9},{11,10},{13,12},{... | collective-permute-start | bytes 3981320 | tf_op jit(solution)/shard_map/ppermute | solution.py:455
  87.7 65.7 %all-to-all-start.2 = ((bf16[8,288,1152]{2,1,0:T(8,128)(2,1)}), bf16[8,288,1152]{2,1,0:T(8,128)(2,1)}, u32[]{:S(2)}, u32[]{:S(2)}) async-start(bf16[8,288,1152]{2,1,0:T(8,128)(2,1)} %shard_map.239), calls=%async_computation.2 | async-start | bytes 10616832 | tf_op jit(solution)/shard_map/all_to_all | solution.py:638
  108.1 33.6 %collective-permute-start.10 = (bf16[8,72,1152]{2,1,0:T(8,128)(2,1)}, bf16[8,72,1152]{2,1,0:T(8,128)(2,1)}, u32[]{:S(2)}, u32[]{:S(2)}) collective-permute-start(bf16[8,72,1152]{2,1,0:T(8,128)(2,1)} %collective-permute-done.6.refs_3_), channel_id=1, source_target_pairs={{1,0},{2,1},{3,2},{5,4},{6,5},{7,6},{9,8},{10,9},{11,10},{13,12},{... | collective-permute-start | bytes 3981320 | tf_op jit(solution)/shard_map/ppermute | solution.py:455
  109.4 33.2 %collective-permute-start.9 = (bf16[8,72,1152]{2,1,0:T(8,128)(2,1)S(1)}, bf16[8,72,1152]{2,1,0:T(8,128)(2,1)}, u32[]{:S(2)}, u32[]{:S(2)}) collective-permute-start(bf16[8,72,1152]{2,1,0:T(8,128)(2,1)S(1)} %collective-permute-done.5.refs_0_), channel_id=1, source_target_pairs={{0,1},{1,2},{2,3},{4,5},{5,6},{6,7},{8,9},{9,10},{10,11},{12,13},{... | collective-permute-start | bytes 3981320 | tf_op jit(solution)/shard_map/ppermute | solution.py:455
  155.7 32.8 %collective-permute-start.14 = (bf16[8,72,1152]{2,1,0:T(8,128)(2,1)}, bf16[8,72,1152]{2,1,0:T(8,128)(2,1)S(1)}, u32[]{:S(2)}, u32[]{:S(2)}) collective-permute-start(bf16[8,72,1152]{2,1,0:T(8,128)(2,1)} %collective-permute-done.9.refs_1_), channel_id=1, source_target_pairs={{0,1},{1,2},{2,3},{4,5},{5,6},{6,7},{8,9},{9,10},{10,11},{12,13},{... | collective-permute-start | bytes 3981320 | tf_op jit(solution)/shard_map/ppermute | solution.py:455
  159.3 33.3 %collective-permute-start.15 = (bf16[8,72,1152]{2,1,0:T(8,128)(2,1)}, bf16[8,72,1152]{2,1,0:T(8,128)(2,1)S(1)}, u32[]{:S(2)}, u32[]{:S(2)}) collective-permute-start(bf16[8,72,1152]{2,1,0:T(8,128)(2,1)} %collective-permute-done.10.refs_4_), channel_id=1, source_target_pairs={{1,0},{2,1},{3,2},{5,4},{6,5},{7,6},{9,8},{10,9},{11,10},{13,12},{... | collective-permute-start | bytes 3981320 | tf_op jit(solution)/shard_map/ppermute | solution.py:455
  202.7 79.4 %all-to-all-start.3 = ((bf16[8,288,1152]{2,1,0:T(8,128)(2,1)}), bf16[8,288,1152]{2,1,0:T(8,128)(2,1)}, u32[]{:S(2)}, u32[]{:S(2)}) async-start(bf16[8,288,1152]{2,1,0:T(8,128)(2,1)} %shard_map.240), calls=%async_computation.3 | async-start | bytes 10616832 | tf_op jit(solution)/shard_map/all_to_all | solution.py:638
  212.4 67.9 %collective-permute-start.18 = (bf16[128,2304]{1,0:T(8,128)(2,1)S(1)}, bf16[128,2304]{1,0:T(8,128)(2,1)S(1)}, u32[]{:S(2)}, u32[]{:S(2)}) collective-permute-start(bf16[128,2304]{1,0:T(8,128)(2,1)S(1)} %multiply_convert_fusion.1), channel_id=1, source_target_pairs={{0,8},{4,12},{8,0},{12,4},{16,24},{20,28},{24,16},{28,20},{1,9},{5... | collective-permute-start | bytes 1769480 | tf_op jit(solution)/shard_map/ppermute | solution.py:447
  214.4 65.9 %collective-permute-start.19 = (bf16[128,2304]{1,0:T(8,128)(2,1)S(1)}, bf16[128,2304]{1,0:T(8,128)(2,1)S(1)}, u32[]{:S(2)}, u32[]{:S(2)}) collective-permute-start(bf16[128,2304]{1,0:T(8,128)(2,1)S(1)} %multiply_convert_fusion.1), channel_id=1, source_target_pairs={{0,16},{4,20},{8,24},{12,28},{16,0},{20,4},{24,8},{28,12},{1,17},{... | collective-permute-start | bytes 1769480 | tf_op jit(solution)/shard_map/ppermute | solution.py:447
  215.9 64.4 %collective-permute-start.20 = (bf16[128,2304]{1,0:T(8,128)(2,1)S(1)}, bf16[128,2304]{1,0:T(8,128)(2,1)S(1)}, u32[]{:S(2)}, u32[]{:S(2)}) collective-permute-start(bf16[128,2304]{1,0:T(8,128)(2,1)S(1)} %multiply_convert_fusion.1), channel_id=1, source_target_pairs={{0,2},{1,3},{2,0},{3,1},{4,6},{5,7},{6,4},{7,5},{8,10},{9,11},{10,... | collective-permute-start | bytes 1769480 | tf_op jit(solution)/shard_map/ppermute | solution.py:451
  218.4 63.7 %collective-permute-start.21 = (bf16[128,2304]{1,0:T(8,128)(2,1)S(1)}, bf16[128,2304]{1,0:T(8,128)(2,1)}, u32[]{:S(2)}, u32[]{:S(2)}) collective-permute-start(bf16[128,2304]{1,0:T(8,128)(2,1)S(1)} %multiply_convert_fusion.1), channel_id=1, source_target_pairs={{0,3},{1,2},{2,1},{3,0},{4,7},{5,6},{6,5},{7,4},{8,11},{9,10},{10,... | collective-permute-start | bytes 1769480 | tf_op jit(solution)/shard_map/ppermute | solution.py:451
  397.4 57.9 %collective-permute-start.45 = (bf16[512,2304]{1,0:T(8,128)(2,1)S(1)}, bf16[512,2304]{1,0:T(8,128)(2,1)S(1)}, u32[]{:S(2)}, u32[]{:S(2)}) collective-permute-start(bf16[512,2304]{1,0:T(8,128)(2,1)S(1)} %constant_dynamic-update-slice_fusion.29.refs_0_.refs_4_), channel_id=1, source_target_pairs={{0,4},{4,0},{8,12},{12,8},{16,20},{20,16},{24,28},{28,24},{1,5},{5... | collective-permute-start | bytes 7077896 | tf_op jit(solution)/shard_map/ppermute | solution.py:447
  458.5 29.8 %collective-permute-start.48 = (bf16[256,2304]{1,0:T(8,128)(2,1)S(1)}, bf16[256,2304]{1,0:T(8,128)(2,1)S(1)}, u32[]{:S(2)}, u32[]{:S(2)}) collective-permute-start(bf16[256,2304]{1,0:T(8,128)(2,1)S(1)} %get-tuple-element.391), channel_id=1, source_target_pairs={{0,1},{1,0},{2,3},{3,2},{4,5},{5,4},{6,7},{7,6},{8,9},{9,8},{10,11... | collective-permute-start | bytes 3538952 | tf_op jit(solution)/shard_map/ppermute | solution.py:451
  499.4 40.9 %collective-permute-start.52 = (bf16[256,2304]{1,0:T(8,128)(2,1)}, bf16[256,2304]{1,0:T(8,128)(2,1)}, u32[]{:S(2)}, u32[]{:S(2)}) collective-permute-start(bf16[256,2304]{1,0:T(8,128)(2,1)} %get-tuple-element.390), channel_id=1, source_target_pairs={{0,1},{1,0},{2,3},{3,2},{4,5},{5,4},{6,7},{7,6},{8,9},{9,8},{10,11... | collective-permute-start | bytes 3538952 | tf_op jit(solution)/shard_map/ppermute | solution.py:451
  540.3 31.0 %collective-permute-start.55 = (bf16[1024,2304]{1,0:T(8,128)(2,1)S(1)}, bf16[1024,2304]{1,0:T(8,128)(2,1)S(1)}, u32[]{:S(2)}, u32[]{:S(2)}) collective-permute-start(bf16[1024,2304]{1,0:T(8,128)(2,1)S(1)} %constant_dynamic-update-slice_fusion.34.refs_0_.refs_2_), channel_id=1, source_target_pairs={{0,4},{4,0},{8,12},{12,8},{16,20},{20,16},{24,28},{28,24},{1,5},{5... | collective-permute-start | bytes 14155784 | tf_op jit(solution)/shard_map/ppermute | solution.py:447
  541.7 29.5 %collective-permute-start.56 = (bf16[512,2304]{1,0:T(8,128)(2,1)S(1)}, bf16[512,2304]{1,0:T(8,128)(2,1)S(1)}, u32[]{:S(2)}, u32[]{:S(2)}) collective-permute-start(bf16[512,2304]{1,0:T(8,128)(2,1)S(1)} %constant_dynamic-update-slice_fusion.39.refs_4_.refs_0_), channel_id=1, source_target_pairs={{0,4},{4,0},{8,12},{12,8},{16,20},{20,16},{24,28},{28,24},{1,5},{5... | collective-permute-start | bytes 7077896 | tf_op jit(solution)/shard_map/ppermute | solution.py:447
  588.6 34.3 %collective-permute-start.59 = (bf16[128,2304]{1,0:T(8,128)(2,1)S(1)}, bf16[128,2304]{1,0:T(8,128)(2,1)S(1)}, u32[]{:S(2)}, u32[]{:S(2)}) collective-permute-start(bf16[128,2304]{1,0:T(8,128)(2,1)S(1)} %subtract_convert_fusion), channel_id=1, source_target_pairs={{0,8},{4,12},{8,0},{12,4},{16,24},{20,28},{24,16},{28,20},{1,9},{5... | collective-permute-start | bytes 1769480 | tf_op jit(solution)/shard_map/ppermute | solution.py:447
  589.9 33.0 %collective-permute-start.60 = (bf16[128,2304]{1,0:T(8,128)(2,1)S(1)}, bf16[128,2304]{1,0:T(8,128)(2,1)S(1)}, u32[]{:S(2)}, u32[]{:S(2)}) collective-permute-start(bf16[128,2304]{1,0:T(8,128)(2,1)S(1)} %subtract_convert_fusion), channel_id=1, source_target_pairs={{0,16},{4,20},{8,24},{12,28},{16,0},{20,4},{24,8},{28,12},{1,17},{... | collective-permute-start | bytes 1769480 | tf_op jit(solution)/shard_map/ppermute | solution.py:447
  665.3 75.9 %all-to-all-start.4 = ((bf16[8,288,1152]{2,1,0:T(8,128)(2,1)}), bf16[8,288,1152]{2,1,0:T(8,128)(2,1)}, u32[]{:S(2)}, u32[]{:S(2)}) async-start(bf16[8,288,1152]{2,1,0:T(8,128)(2,1)} %bitcast.88), calls=%async_computation.4 | async-start | bytes 10616832 | tf_op jit(solution)/shard_map/all_to_all | solution.py:638
  694.1 44.5 %collective-permute-start.71 = (bf16[8,2,72,512]{3,2,0,1:T(8,128)(2,1)S(1)}, bf16[8,2,72,512]{3,2,0,1:T(8,128)(2,1)}, u32[]{:S(2)}, u32[]{:S(2)}) collective-permute-start(bf16[8,2,72,512]{3,2,0,1:T(8,128)(2,1)S(1)} %copy_bitcast_fusion), channel_id=1, source_target_pairs={{0,1},{1,0},{2,3},{3,2},{4,5},{5,4},{6,7},{7,6},{8,9},{9,8},{10,11... | collective-permute-start | bytes 3538952 | tf_op jit(solution)/shard_map/ppermute | solution.py:451
  694.2 49.0 %collective-permute-start.69 = (bf16[128,2304]{1,0:T(8,128)(2,1)}, bf16[128,2304]{1,0:T(8,128)(2,1)}, u32[]{:S(2)}, u32[]{:S(2)}) collective-permute-start(bf16[128,2304]{1,0:T(8,128)(2,1)} %pad_maximum_fusion.11), channel_id=1, source_target_pairs={{0,8},{4,12},{8,0},{12,4},{16,24},{20,28},{24,16},{28,20},{1,9},{5... | collective-permute-start | bytes 1769480 | tf_op jit(solution)/shard_map/ppermute | solution.py:447
  695.9 47.3 %collective-permute-start.70 = (bf16[128,2304]{1,0:T(8,128)(2,1)}, bf16[128,2304]{1,0:T(8,128)(2,1)}, u32[]{:S(2)}, u32[]{:S(2)}) collective-permute-start(bf16[128,2304]{1,0:T(8,128)(2,1)} %pad_maximum_fusion.12), channel_id=1, source_target_pairs={{0,16},{4,20},{8,24},{12,28},{16,0},{20,4},{24,8},{28,12},{1,17},{... | collective-permute-start | bytes 1769480 | tf_op jit(solution)/shard_map/ppermute | solution.py:447
  743.2 73.2 %all-to-all-start.5 = ((bf16[8,288,1152]{2,1,0:T(8,128)(2,1)}), bf16[8,288,1152]{2,1,0:T(8,128)(2,1)}, u32[]{:S(2)}, u32[]{:S(2)}) async-start(bf16[8,288,1152]{2,1,0:T(8,128)(2,1)} %bitcast.90), calls=%async_computation.5 | async-start | bytes 10616832 | tf_op jit(solution)/shard_map/all_to_all | solution.py:638
  750.1 64.6 %collective-permute-start.74 = (bf16[64,2304]{1,0:T(8,128)(2,1)}, bf16[64,2304]{1,0:T(8,128)(2,1)}, u32[]{:S(2)}, u32[]{:S(2)}) collective-permute-start(bf16[64,2304]{1,0:T(8,128)(2,1)} %add_convert_fusion.1), channel_id=1, source_target_pairs={{0,8},{4,12},{8,0},{12,4},{16,24},{20,28},{24,16},{28,20},{1,9},{5... | collective-permute-start | bytes 884744 | tf_op jit(solution)/shard_map/ppermute | solution.py:447
  754.0 60.7 %collective-permute-start.73 = (bf16[64,2304]{1,0:T(8,128)(2,1)}, bf16[64,2304]{1,0:T(8,128)(2,1)}, u32[]{:S(2)}, u32[]{:S(2)}) collective-permute-start(bf16[64,2304]{1,0:T(8,128)(2,1)} %add_convert_fusion.2), channel_id=1, source_target_pairs={{0,16},{4,20},{8,24},{12,28},{16,0},{20,4},{24,8},{28,12},{1,17},{... | collective-permute-start | bytes 884744 | tf_op jit(solution)/shard_map/ppermute | solution.py:447
  761.2 55.0 %collective-permute-start.72 = (bf16[8,72,512]{2,1,0:T(8,128)(2,1)S(1)}, bf16[8,72,512]{2,1,0:T(8,128)(2,1)S(1)}, u32[]{:S(2)}, u32[]{:S(2)}) collective-permute-start(bf16[8,72,512]{2,1,0:T(8,128)(2,1)S(1)} %dynamic-slice_bitcast_fusion), channel_id=1, source_target_pairs={{0,2},{1,3},{2,0},{3,1},{4,6},{5,7},{6,4},{7,5},{8,10},{9,11},{10,... | collective-permute-start | bytes 1769480 | tf_op jit(solution)/shard_map/ppermute | solution.py:451
  835.6 69.3 %all-to-all-start.7 = ((bf16[8,288,1152]{2,1,0:T(8,128)(2,1)}), bf16[8,288,1152]{2,1,0:T(8,128)(2,1)}, u32[]{:S(2)}, u32[]{:S(2)}) async-start(bf16[8,288,1152]{2,1,0:T(8,128)(2,1)} %bitcast.89), calls=%async_computation.7 | async-start | bytes 10616832 | tf_op jit(solution)/shard_map/all_to_all | solution.py:638
  841.5 42.9 %collective-permute-start.75 = (bf16[8,72,768]{2,1,0:T(8,128)(2,1)}, bf16[8,72,768]{2,1,0:T(8,128)(2,1)}, u32[]{:S(2)}, u32[]{:S(2)}) collective-permute-start(bf16[8,72,768]{2,1,0:T(8,128)(2,1)} %get-tuple-element.431), channel_id=1, source_target_pairs={{0,2},{1,3},{2,0},{3,1},{4,6},{5,7},{6,4},{7,5},{8,10},{9,11},{10,... | collective-permute-start | bytes 2654216 | tf_op jit(solution)/shard_map/ppermute | solution.py:451
  886.4 40.6 %collective-permute-start.78 = (bf16[2,8,72,768]{3,2,1,0:T(8,128)(2,1)S(1)}, bf16[2,8,72,768]{3,2,1,0:T(8,128)(2,1)}, u32[]{:S(2)}, u32[]{:S(2)}) collective-permute-start(bf16[2,8,72,768]{3,2,1,0:T(8,128)(2,1)S(1)} %reverse_select_fusion.1), channel_id=1, source_target_pairs={{0,1},{1,0},{2,3},{3,2},{4,5},{5,4},{6,7},{7,6},{8,9},{9,8},{10,11... | collective-permute-start | bytes 5308424 | tf_op jit(solution)/shard_map/ppermute | solution.py:451
  (180 other events, 2458.0 us)

commit v5 on v4

--- a/solution.py
+++ b/solution.py
@@ -437,10 +437,10 @@
 
 VMEM_BYTES = 56 * 1024 * 1024
 TILE_VMEM_BYTES = 16 * 1024 * 1024
-CROSS_VMEM_BYTES = 36 * 1024 * 1024
+CROSS_VMEM_BYTES = 42 * 1024 * 1024
 GELU_RATE = 0.7978845608028654
 TILE = 256
-CHUNK = 768
+CHUNK = 1152
 
 
 def seq_swap(block, bit):
@@ -968,26 +968,26 @@
         return back_project(halves, w_down, factors, scale_down)
 
     def cut(rows):
-        middle = 2 * block_rows
-        return rows[:middle], rows[middle : middle + block_rows], rows[middle + block_rows :]
-
-    (mixed, *factors), pair_mid_near, mid_cuts = pin(
+        return [rows[i * block_rows : (i + 1) * block_rows] for i in range(4)]
+
+    mid_cuts = cut(mid_mine)
+    (mixed, *factors), pair_mid_near, third_mid_first = pin(
         up_again(mid_mine, mid_theirs),
         gather_near(jnp.concatenate([mid_two, mid_three])),
-        cut(mid_mine),
-    )
-    ffn_core, pair_mid_mine, third_mid_first = pin(
+        row_swap(mid_cuts[0], 1),
+    )
+    ffn_core, pair_mid_mine, third_mid_next = pin(
         scatter_core(lambda side, kind: partial_product([(mixed, w_down)], side, kind)),
         gather_far(*pair_mid_near),
-        row_swap(mid_cuts[0], 1),
+        row_swap(mid_cuts[1], 1),
     )
     ffn_near, pair_mid_theirs, third_mid_second = pin(
-        scatter_near(*ffn_core), seq_swap(pair_mid_mine, 1), row_swap(mid_cuts[1], 1)
+        scatter_near(*ffn_core), seq_swap(pair_mid_mine, 1), row_swap(mid_cuts[2], 1)
     )
     ffn_proj, third_mid_last, pair_mid_mine = pin(
-        scale_down * scatter_far(*ffn_near), row_swap(mid_cuts[2], 1), pair_mid_mine
-    )
-    third_mid_mine = jnp.concatenate([third_mid_first, third_mid_second, third_mid_last])
+        scale_down * scatter_far(*ffn_near), row_swap(mid_cuts[3], 1), pair_mid_mine
+    )
+    third_mid_mine = jnp.concatenate([third_mid_first, third_mid_next, third_mid_second, third_mid_last])
     block_out = bf(middle + norm_gain(ffn_proj, gain_ffw_out))
     grad_ffn, grad_gain_four = norm_back(ffn_proj, gain_ffw_out, upstream)
     grad_ffn_low = bf(grad_ffn)

time: 950 us -> 946 us (level)
    ppermute x56, waiting for transfers between devices: 164 us -> 176 us  [seq_swap(): lax.ppermute(block, 'seq', [(place, place ^ bit) for place in range(8)])]
    ppermute x17 -> x18, waiting for transfers between devices: 88.8 us -> 83.1 us  [row_swap(): lax.ppermute(block, 'row', [(place, place ^ bit) for place in range(4)])]
    unnamed x284 -> x291, local copies, waits for them, and re-layouts: 33.5 us -> 30.6 us
    ppermute x17 -> x18, starting transfers between devices: 26.6 us -> 26.5 us  [row_swap(): lax.ppermute(block, 'row', [(place, place ^ bit) for place in range(4)])]
  transfers between devices with their start and end apart: 86 -> 87, of which waited for: 46 -> 43; matrix products, arithmetic and copies ran while one was open for 12% -> 12% of each run, Pallas kernels for 29% -> 28%
where the time goes in v5:
time: 946 us; the launch traced here: 935 us
  waiting for transfers between devices  334 us (35%)
  Pallas kernels  285 us (30%)
  starting transfers between devices  125 us (13%)
  other arithmetic  64.9 us (7%)
  local copies, waits for them, and re-layouts  60.4 us (6%)
  matrix products  43.7 us (5%)
  blocking collectives  17.2 us (2%)
    ppermute x56, waiting for transfers between devices, seq_swap(): lax.ppermute(block, 'seq', [(place, place ^ bit) for place in range(8)])  176 us
    pallas_call x12, Pallas kernels, tile_calls(): pl.pallas_call(kernel, grid=grid, in_specs=in_specs, out_specs=out_specs,...  130 us
    pallas_call x3, Pallas kernels, cross_products(): pl.pallas_call(functools.partial(cross_kernel, steps, len(lefts), len(rig...  91.7 us
    ppermute x18, waiting for transfers between devices, row_swap(): lax.ppermute(block, 'row', [(place, place ^ bit) for place in range(4)])  83.1 us
    ppermute x6, waiting for transfers between devices, row_shift(): lax.ppermute(block, 'row', [(place, place + step) for place in range(4) i...  58.3 us
    ppermute x56, starting transfers between devices, seq_swap(): lax.ppermute(block, 'seq', [(place, place ^ bit) for place in range(8)])  49.6 us
    all_to_all x7, starting transfers between devices, trade(): return lax.all_to_all(blocks, 'seq', 0, 0, tiled=True)  32.2 us
    pallas_call x4, Pallas kernels, unpack_blocks(): pl.pallas_call(unpack_kernel, grid=(8,), in_specs=[pl.BlockSpec((parts, 1...  30.9 us
  transfers between devices with their start and end apart: 87, of which 43 were waited for; matrix products, arithmetic and copies ran while one was open for 12% of the time, Pallas kernels for 28%

profile of v5, /device:TPU:0, one launch (start us, length us, event | category | flops | bytes accessed | tf_op | source)
XLA Modules:
  0.0 934.6 jit_solution(13194917262671568967)
XLA Ops:
  22.2 7.2 shard_map.238
  54.6 8.8 shard_map.239
  63.4 8.8 shard_map.240
  72.5 9.3 collective-permute-done.5.refs_0_
  126.1 15.7 %collective-permute-done.10.refs_4_ = bf16[8,72,1152]{2,1,0:T(8,128)(2,1)} collective-permute-done((bf16[8,72,1152]{2,1,0:T(8,128)(2,1)}, bf16[8,72,1152]{2,1,0:T(8,128)(2,1)}, u32[]{:S(2)}, u32[]{:S(2)}) %collective-permute-start.10) | collective-permute-done | bytes 1327136 | tf_op jit(solution)/shard_map/ppermute | solution.py:455
  142.6 10.8 %all-to-all-done.2 = bf16[8,288,1152]{2,1,0:T(8,128)(2,1)} async-done(((bf16[8,288,1152]{2,1,0:T(8,128)(2,1)}), bf16[8,288,1152]{2,1,0:T(8,128)(2,1)}, u32[]{:S(2)}, u32[]{:S(2)}) %all-to-all-start.2) | async-done | bytes 5308448 | tf_op jit(solution)/shard_map/all_to_all | solution.py:638
  164.5 24.0 %collective-permute-done.14.refs_2_ = bf16[8,72,1152]{2,1,0:T(8,128)(2,1)S(1)} collective-permute-done((bf16[8,72,1152]{2,1,0:T(8,128)(2,1)}, bf16[8,72,1152]{2,1,0:T(8,128)(2,1)S(1)}, u32[]{:S(2)}, u32[]{:S(2)}) %collective-permute-start.14) | collective-permute-done | bytes 1327136 | tf_op jit(solution)/shard_map/ppermute | solution.py:455
  194.1 7.0 collective-permute-done.17
  220.3 60.0 %collective-permute-done.18 = bf16[128,2304]{1,0:T(8,128)(2,1)S(1)} collective-permute-done((bf16[128,2304]{1,0:T(8,128)(2,1)S(1)}, bf16[128,2304]{1,0:T(8,128)(2,1)S(1)}, u32[]{:S(2)}, u32[]{:S(2)}) %collective-permute-start.18) | collective-permute-done | bytes 589856 | tf_op jit(solution)/shard_map/ppermute | solution.py:447
  302.6 18.0 %shard_map.242 = (bf16[1024,1152]{1,0:T(8,128)(2,1)S(1)}, bf16[1024,1152]{1,0:T(8,128)(2,1)S(1)}, bf16[1024,1152]{1,0:T(8,128)(2,1)S(1)}) custom-call(bf16[512,2304]{1,0:T(8,128)(2,1)S(1)} %constant_dynamic-update-slice_fusion.12.refs_0_, bf16[512,2304]{1,0:T(8,128)(2,1)S(1)} %collective-permute-done.24.refs_1_, bf16[2304,1152]{1,0:T(8,128)(2,1)} %bitcast.6.refs_2_.refs_1_, ...), custom_call_target="tpu_custom_call" | custom-call | flops 1 | bytes 1 | tf_op jit(solution)/shard_map/pallas_call | solution.py:673
  338.2 13.0 %collective-permute-done.29 = bf16[128,2304]{1,0:T(8,128)(2,1)S(1)} collective-permute-done((bf16[128,2304]{1,0:T(8,128)(2,1)S(1)}, bf16[128,2304]{1,0:T(8,128)(2,1)S(1)}, u32[]{:S(2)}, u32[]{:S(2)}) %collective-permute-start.29) | collective-permute-done | bytes 589856 | tf_op jit(solution)/shard_map/ppermute | solution.py:447
  363.7 12.2 %collective-permute-done.35 = bf16[128,2304]{1,0:T(8,128)(2,1)S(1)} collective-permute-done((bf16[128,2304]{1,0:T(8,128)(2,1)S(1)}, bf16[128,2304]{1,0:T(8,128)(2,1)S(1)}, u32[]{:S(2)}, u32[]{:S(2)}) %collective-permute-start.35) | collective-permute-done | bytes 589856 | tf_op jit(solution)/shard_map/ppermute | solution.py:451
  393.7 18.7 %shard_map.245 = (bf16[1024,1152]{1,0:T(8,128)(2,1)S(1)}, bf16[1024,1152]{1,0:T(8,128)(2,1)S(1)}, bf16[1024,1152]{1,0:T(8,128)(2,1)S(1)}) custom-call(bf16[1024,2304]{1,0:T(8,128)(2,1)S(1)} %constant_dynamic-update-slice_fusion.19.refs_0_.refs_2_, bf16[2304,1152]{1,0:T(8,128)(2,1)} %bitcast.6.refs_2_.refs_1_, bf16[2304,1152]{1,0:T(8,128)(2,1)} %bitcast.7.refs_3_.refs_2_), custom_call_target="tpu_custom_call" | custom-call | flops 1 | bytes 1 | tf_op jit(solution)/shard_map/pallas_call | solution.py:673
  431.9 18.0 %shard_map.246 = (bf16[1024,1152]{1,0:T(8,128)(2,1)S(1)}, bf16[1024,1152]{1,0:T(8,128)(2,1)S(1)}, bf16[1024,1152]{1,0:T(8,128)(2,1)S(1)}) custom-call(bf16[1024,2304]{1,0:T(8,128)(2,1)S(1)} %collective-permute-done.34.refs_0_.refs_3_, bf16[2304,1152]{1,0:T(8,128)(2,1)} %bitcast.6.refs_2_.refs_1_, bf16[2304,1152]{1,0:T(8,128)(2,1)} %bitcast.7.refs_3_.refs_2_), custom_call_target="tpu_custom_call" | custom-call | flops 1 | bytes 1 | tf_op jit(solution)/shard_map/pallas_call | solution.py:673
  460.7 7.0 shard_map.247
  467.8 13.2 %collective-permute-done.47 = bf16[256,2304]{1,0:T(8,128)(2,1)S(1)} collective-permute-done((bf16[256,2304]{1,0:T(8,128)(2,1)S(1)}, bf16[256,2304]{1,0:T(8,128)(2,1)S(1)}, u32[]{:S(2)}, u32[]{:S(2)}) %collective-permute-start.47) | collective-permute-done | bytes 1179680 | tf_op jit(solution)/shard_map/ppermute | solution.py:447
  486.0 11.0 %shard_map.249 = bf16[512,2304]{1,0:T(8,128)(2,1)S(1)} custom-call(bf16[1024,1152]{1,0:T(8,128)(2,1)S(1)} %get-tuple-element.264.refs_0_.refs_6_, bf16[2304,1152]{1,0:T(8,128)(2,1)} %bitcast.6.refs_2_.refs_1_, bf16[1024,1152]{1,0:T(8,128)(2,1)S(1)} %get-tuple-element.334.refs_2_.refs_6_, bf16[2304,1152]{1,0:T(8,128)(2,1)} %bitcast.7.refs_3_.refs_2_), custom_call_target="tpu_custom_call" | custom-call | flops 1 | bytes 1 | tf_op jit(solution)/shard_map/pallas_call | solution.py:673
  498.8 10.5 %shard_map.248 = f32[512,2304]{1,0:T(8,128)S(1)} custom-call(bf16[1024,1152]{1,0:T(8,128)(2,1)S(1)} %get-tuple-element.264.refs_0_.refs_6_, bf16[2304,1152]{1,0:T(8,128)(2,1)} %bitcast.6.refs_2_.refs_1_, bf16[1024,1152]{1,0:T(8,128)(2,1)S(1)} %get-tuple-element.334.refs_2_.refs_6_, bf16[2304,1152]{1,0:T(8,128)(2,1)} %bitcast.7.refs_3_.refs_2_), custom_call_target="tpu_custom_call" | custom-call | flops 1 | bytes 1 | tf_op jit(solution)/shard_map/pallas_call | solution.py:673
  511.9 13.0 %collective-permute-done.51 = bf16[128,2304]{1,0:T(8,128)(2,1)S(1)} collective-permute-done((bf16[128,2304]{1,0:T(8,128)(2,1)S(1)}, bf16[128,2304]{1,0:T(8,128)(2,1)S(1)}, u32[]{:S(2)}, u32[]{:S(2)}) %collective-permute-start.51) | collective-permute-done | bytes 589856 | tf_op jit(solution)/shard_map/ppermute | solution.py:447
  541.8 18.2 %shard_map.250 = (bf16[1024,1152]{1,0:T(8,128)(2,1)S(1)}, bf16[1024,1152]{1,0:T(8,128)(2,1)S(1)}, bf16[1024,1152]{1,0:T(8,128)(2,1)S(1)}) custom-call(bf16[512,2304]{1,0:T(8,128)(2,1)S(1)} %constant_dynamic-update-slice_fusion.29.refs_0_.refs_4_, bf16[512,2304]{1,0:T(8,128)(2,1)S(1)} %copy-done.17, bf16[2304,1152]{1,0:T(8,128)(2,1)} %bitcast.6.refs_2_.refs_1_, ...), custom_call_target="tpu_custom_call" | custom-call | flops 1 | bytes 1 | tf_op jit(solution)/shard_map/pallas_call | solution.py:673
  587.9 30.8 %shard_map.253 = bf16[1,8,288,1152]{3,2,1,0:T(8,128)(2,1)} custom-call(bf16[512,2304]{1,0:T(8,128)(2,1)S(1)} %constant_dynamic-update-slice_fusion.24.refs_0_, bf16[512,2304]{1,0:T(8,128)(2,1)S(1)} %copy-done.29, bf16[1024,2304]{1,0:T(8,128)(2,1)} %copy-done.8, bf16[1024,2304]{1,0:T(8,128)(2,1)} %copy-done.22, bf16[512,2304]{1,0:T(8,128)(2,1)S(1)} %copy-done.24, ...), custom_call_target="tpu_custom_call" | custom-call | flops 1 | bytes 1 | tf_op jit(solution)/shard_map/pallas_call | solution.py:810
  693.2 7.0 shard_map.254
  703.1 30.6 %shard_map.255 = bf16[1,8,288,1152]{3,2,1,0:T(8,128)(2,1)} custom-call(bf16[512,2304]{1,0:T(8,128)(2,1)S(1)} %copy-done.3, bf16[512,2304]{1,0:T(8,128)(2,1)S(1)} %copy-done.14, bf16[1024,2304]{1,0:T(8,128)(2,1)} %copy-done.1, bf16[1024,2304]{1,0:T(8,128)(2,1)} %copy-done.4, bf16[512,2304]{1,0:T(8,128)(2,1)S(1)} %copy-done.6, ...), custom_call_target="tpu_custom_call" | custom-call | flops 1 | bytes 1 | tf_op jit(solution)/shard_map/pallas_call | solution.py:810
  764.6 30.2 %shard_map.256 = bf16[1,8,288,1152]{3,2,1,0:T(8,128)(2,1)} custom-call(bf16[512,2304]{1,0:T(8,128)(2,1)S(1)} %copy-done.3, bf16[512,2304]{1,0:T(8,128)(2,1)S(1)} %copy-done.15, bf16[1024,2304]{1,0:T(8,128)(2,1)} %copy-done.1, bf16[1024,2304]{1,0:T(8,128)(2,1)} %copy-done.4, bf16[512,2304]{1,0:T(8,128)(2,1)S(1)} %copy-done.7, ...), custom_call_target="tpu_custom_call" | custom-call | flops 1 | bytes 1 | tf_op jit(solution)/shard_map/pallas_call | solution.py:810
  794.8 15.7 %collective-permute-done.75 = bf16[64,2304]{1,0:T(8,128)(2,1)} collective-permute-done((bf16[64,2304]{1,0:T(8,128)(2,1)}, bf16[64,2304]{1,0:T(8,128)(2,1)}, u32[]{:S(2)}, u32[]{:S(2)}) %collective-permute-start.75) | collective-permute-done | bytes 294944 | tf_op jit(solution)/shard_map/ppermute | solution.py:447
  814.2 17.2 %all_to_all.40 = bf16[8,80,768]{2,1,0:T(8,128)(2,1)S(1)} all-to-all(bf16[8,80,768]{2,1,0:T(8,128)(2,1)S(1)} %pad_maximum_fusion.4), channel_id=1, replica_groups=mesh['seq'=8,'row'=4] {'seq'}, dimensions={0} | all-to-all | bytes 1966080 | tf_op jit(solution)/shard_map/all_to_all | solution.py:638
  840.0 18.4 %collective-permute-done.77 = f32[4,288]{1,0:T(4,128)S(1)} collective-permute-done((f32[4,288]{1,0:T(4,128)S(1)}, f32[4,288]{1,0:T(4,128)S(1)}, u32[]{:S(2)}, u32[]{:S(2)}) %collective-permute-start.77) | collective-permute-done | bytes 4640 | tf_op jit(solution)/shard_map/ppermute | solution.py:451
  861.5 18.5 %collective-permute-done.78 = f32[4,288]{1,0:T(4,128)S(1)} collective-permute-done((f32[4,288]{1,0:T(4,128)S(1)}, f32[4,288]{1,0:T(4,128)S(1)}, u32[]{:S(2)}, u32[]{:S(2)}) %collective-permute-start.78) | collective-permute-done | bytes 4640 | tf_op jit(solution)/shard_map/ppermute | solution.py:451
  882.6 8.0 shard_map.260
  890.6 8.1 shard_map.259
  900.9 8.0 shard_map.257
  908.9 14.3 %collective-permute-done.79 = bf16[2,8,72,768]{3,2,1,0:T(8,128)(2,1)} collective-permute-done((bf16[2,8,72,768]{3,2,1,0:T(8,128)(2,1)S(1)}, bf16[2,8,72,768]{3,2,1,0:T(8,128)(2,1)}, u32[]{:S(2)}, u32[]{:S(2)}) %collective-permute-start.79) | collective-permute-done | bytes 1769504 | tf_op jit(solution)/shard_map/ppermute | solution.py:451
  (616 shorter events, 419.6 us)
Async XLA Ops:
  41.1 46.6 %all-to-all-start.1 = ((bf16[8,288,768]{2,1,0:T(8,128)(2,1)}), bf16[8,288,768]{2,1,0:T(8,128)(2,1)}, u32[]{:S(2)}, u32[]{:S(2)}) async-start(bf16[8,288,768]{2,1,0:T(8,128)(2,1)} %shard_map.238), calls=%async_computation.1 | async-start | bytes 7077888 | tf_op jit(solution)/shard_map/all_to_all | solution.py:638
  49.3 43.1 %collective-permute-start.4 = (bf16[512,2304]{1,0:T(8,128)(2,1)}, bf16[512,2304]{1,0:T(8,128)(2,1)}, u32[]{:S(2)}, u32[]{:S(2)}) collective-permute-start(bf16[512,2304]{1,0:T(8,128)(2,1)} %get-tuple-element.441), channel_id=1, source_target_pairs={{0,4},{4,0},{8,12},{12,8},{16,20},{20,16},{24,28},{28,24},{1,5},{5... | collective-permute-start | bytes 7077896 | tf_op jit(solution)/shard_map/ppermute | solution.py:447
  49.7 32.1 %collective-permute-start.5 = (bf16[8,72,1152]{2,1,0:T(8,128)(2,1)S(1)}, bf16[8,72,1152]{2,1,0:T(8,128)(2,1)S(1)}, u32[]{:S(2)}, u32[]{:S(2)}) collective-permute-start(bf16[8,72,1152]{2,1,0:T(8,128)(2,1)S(1)} %all-to-all-done.own), channel_id=1, source_target_pairs={{0,1},{1,2},{2,3},{4,5},{5,6},{6,7},{8,9},{9,10},{10,11},{12,13},{... | collective-permute-start | bytes 3981320 | tf_op jit(solution)/shard_map/ppermute | solution.py:455
  53.3 32.9 %collective-permute-start.6 = (bf16[8,72,1152]{2,1,0:T(8,128)(2,1)S(1)}, bf16[8,72,1152]{2,1,0:T(8,128)(2,1)}, u32[]{:S(2)}, u32[]{:S(2)}) collective-permute-start(bf16[8,72,1152]{2,1,0:T(8,128)(2,1)S(1)} %all-to-all-done.own), channel_id=1, source_target_pairs={{1,0},{2,1},{3,2},{5,4},{6,5},{7,6},{9,8},{10,9},{11,10},{13,12},{... | collective-permute-start | bytes 3981320 | tf_op jit(solution)/shard_map/ppermute | solution.py:455
  87.7 65.7 %all-to-all-start.2 = ((bf16[8,288,1152]{2,1,0:T(8,128)(2,1)}), bf16[8,288,1152]{2,1,0:T(8,128)(2,1)}, u32[]{:S(2)}, u32[]{:S(2)}) async-start(bf16[8,288,1152]{2,1,0:T(8,128)(2,1)} %shard_map.239), calls=%async_computation.2 | async-start | bytes 10616832 | tf_op jit(solution)/shard_map/all_to_all | solution.py:638
  108.1 33.6 %collective-permute-start.10 = (bf16[8,72,1152]{2,1,0:T(8,128)(2,1)}, bf16[8,72,1152]{2,1,0:T(8,128)(2,1)}, u32[]{:S(2)}, u32[]{:S(2)}) collective-permute-start(bf16[8,72,1152]{2,1,0:T(8,128)(2,1)} %collective-permute-done.6.refs_3_), channel_id=1, source_target_pairs={{1,0},{2,1},{3,2},{5,4},{6,5},{7,6},{9,8},{10,9},{11,10},{13,12},{... | collective-permute-start | bytes 3981320 | tf_op jit(solution)/shard_map/ppermute | solution.py:455
  109.4 33.2 %collective-permute-start.9 = (bf16[8,72,1152]{2,1,0:T(8,128)(2,1)S(1)}, bf16[8,72,1152]{2,1,0:T(8,128)(2,1)}, u32[]{:S(2)}, u32[]{:S(2)}) collective-permute-start(bf16[8,72,1152]{2,1,0:T(8,128)(2,1)S(1)} %collective-permute-done.5.refs_0_), channel_id=1, source_target_pairs={{0,1},{1,2},{2,3},{4,5},{5,6},{6,7},{8,9},{9,10},{10,11},{12,13},{... | collective-permute-start | bytes 3981320 | tf_op jit(solution)/shard_map/ppermute | solution.py:455
  155.7 32.8 %collective-permute-start.14 = (bf16[8,72,1152]{2,1,0:T(8,128)(2,1)}, bf16[8,72,1152]{2,1,0:T(8,128)(2,1)S(1)}, u32[]{:S(2)}, u32[]{:S(2)}) collective-permute-start(bf16[8,72,1152]{2,1,0:T(8,128)(2,1)} %collective-permute-done.9.refs_1_), channel_id=1, source_target_pairs={{0,1},{1,2},{2,3},{4,5},{5,6},{6,7},{8,9},{9,10},{10,11},{12,13},{... | collective-permute-start | bytes 3981320 | tf_op jit(solution)/shard_map/ppermute | solution.py:455
  159.3 33.3 %collective-permute-start.15 = (bf16[8,72,1152]{2,1,0:T(8,128)(2,1)}, bf16[8,72,1152]{2,1,0:T(8,128)(2,1)S(1)}, u32[]{:S(2)}, u32[]{:S(2)}) collective-permute-start(bf16[8,72,1152]{2,1,0:T(8,128)(2,1)} %collective-permute-done.10.refs_4_), channel_id=1, source_target_pairs={{1,0},{2,1},{3,2},{5,4},{6,5},{7,6},{9,8},{10,9},{11,10},{13,12},{... | collective-permute-start | bytes 3981320 | tf_op jit(solution)/shard_map/ppermute | solution.py:455
  202.7 79.4 %all-to-all-start.3 = ((bf16[8,288,1152]{2,1,0:T(8,128)(2,1)}), bf16[8,288,1152]{2,1,0:T(8,128)(2,1)}, u32[]{:S(2)}, u32[]{:S(2)}) async-start(bf16[8,288,1152]{2,1,0:T(8,128)(2,1)} %shard_map.240), calls=%async_computation.3 | async-start | bytes 10616832 | tf_op jit(solution)/shard_map/all_to_all | solution.py:638
  212.9 67.4 %collective-permute-start.18 = (bf16[128,2304]{1,0:T(8,128)(2,1)S(1)}, bf16[128,2304]{1,0:T(8,128)(2,1)S(1)}, u32[]{:S(2)}, u32[]{:S(2)}) collective-permute-start(bf16[128,2304]{1,0:T(8,128)(2,1)S(1)} %multiply_convert_fusion.1), channel_id=1, source_target_pairs={{0,8},{4,12},{8,0},{12,4},{16,24},{20,28},{24,16},{28,20},{1,9},{5... | collective-permute-start | bytes 1769480 | tf_op jit(solution)/shard_map/ppermute | solution.py:447
  214.9 65.4 %collective-permute-start.19 = (bf16[128,2304]{1,0:T(8,128)(2,1)S(1)}, bf16[128,2304]{1,0:T(8,128)(2,1)S(1)}, u32[]{:S(2)}, u32[]{:S(2)}) collective-permute-start(bf16[128,2304]{1,0:T(8,128)(2,1)S(1)} %multiply_convert_fusion.1), channel_id=1, source_target_pairs={{0,16},{4,20},{8,24},{12,28},{16,0},{20,4},{24,8},{28,12},{1,17},{... | collective-permute-start | bytes 1769480 | tf_op jit(solution)/shard_map/ppermute | solution.py:447
  216.4 63.9 %collective-permute-start.20 = (bf16[128,2304]{1,0:T(8,128)(2,1)S(1)}, bf16[128,2304]{1,0:T(8,128)(2,1)S(1)}, u32[]{:S(2)}, u32[]{:S(2)}) collective-permute-start(bf16[128,2304]{1,0:T(8,128)(2,1)S(1)} %multiply_convert_fusion.1), channel_id=1, source_target_pairs={{0,2},{1,3},{2,0},{3,1},{4,6},{5,7},{6,4},{7,5},{8,10},{9,11},{10,... | collective-permute-start | bytes 1769480 | tf_op jit(solution)/shard_map/ppermute | solution.py:451
  218.9 63.2 %collective-permute-start.21 = (bf16[128,2304]{1,0:T(8,128)(2,1)S(1)}, bf16[128,2304]{1,0:T(8,128)(2,1)}, u32[]{:S(2)}, u32[]{:S(2)}) collective-permute-start(bf16[128,2304]{1,0:T(8,128)(2,1)S(1)} %multiply_convert_fusion.1), channel_id=1, source_target_pairs={{0,3},{1,2},{2,1},{3,0},{4,7},{5,6},{6,5},{7,4},{8,11},{9,10},{10,... | collective-permute-start | bytes 1769480 | tf_op jit(solution)/shard_map/ppermute | solution.py:451
  393.6 59.2 %collective-permute-start.46 = (bf16[512,2304]{1,0:T(8,128)(2,1)S(1)}, bf16[512,2304]{1,0:T(8,128)(2,1)S(1)}, u32[]{:S(2)}, u32[]{:S(2)}) collective-permute-start(bf16[512,2304]{1,0:T(8,128)(2,1)S(1)} %constant_dynamic-update-slice_fusion.29.refs_0_.refs_4_), channel_id=1, source_target_pairs={{0,4},{4,0},{8,12},{12,8},{16,20},{20,16},{24,28},{28,24},{1,5},{5... | collective-permute-start | bytes 7077896 | tf_op jit(solution)/shard_map/ppermute | solution.py:447
  456.2 29.8 %collective-permute-start.49 = (bf16[256,2304]{1,0:T(8,128)(2,1)S(1)}, bf16[256,2304]{1,0:T(8,128)(2,1)S(1)}, u32[]{:S(2)}, u32[]{:S(2)}) collective-permute-start(bf16[256,2304]{1,0:T(8,128)(2,1)S(1)} %get-tuple-element.387), channel_id=1, source_target_pairs={{0,1},{1,0},{2,3},{3,2},{4,5},{5,4},{6,7},{7,6},{8,9},{9,8},{10,11... | collective-permute-start | bytes 3538952 | tf_op jit(solution)/shard_map/ppermute | solution.py:451
  496.9 29.5 %collective-permute-start.50 = (bf16[512,2304]{1,0:T(8,128)(2,1)S(1)}, bf16[512,2304]{1,0:T(8,128)(2,1)}, u32[]{:S(2)}, u32[]{:S(2)}) collective-permute-start(bf16[512,2304]{1,0:T(8,128)(2,1)S(1)} %shard_map.249), channel_id=1, source_target_pairs={{0,4},{4,0},{8,12},{12,8},{16,20},{20,16},{24,28},{28,24},{1,5},{5... | collective-permute-start | bytes 7077896 | tf_op jit(solution)/shard_map/ppermute | solution.py:447
  497.0 40.8 %collective-permute-start.53 = (bf16[256,2304]{1,0:T(8,128)(2,1)}, bf16[256,2304]{1,0:T(8,128)(2,1)}, u32[]{:S(2)}, u32[]{:S(2)}) collective-permute-start(bf16[256,2304]{1,0:T(8,128)(2,1)} %get-tuple-element.386), channel_id=1, source_target_pairs={{0,1},{1,0},{2,3},{3,2},{4,5},{5,4},{6,7},{7,6},{8,9},{9,8},{10,11... | collective-permute-start | bytes 3538952 | tf_op jit(solution)/shard_map/ppermute | solution.py:451
  537.8 30.8 %collective-permute-start.56 = (bf16[1024,2304]{1,0:T(8,128)(2,1)S(1)}, bf16[1024,2304]{1,0:T(8,128)(2,1)S(1)}, u32[]{:S(2)}, u32[]{:S(2)}) collective-permute-start(bf16[1024,2304]{1,0:T(8,128)(2,1)S(1)} %constant_dynamic-update-slice_fusion.35.refs_0_.refs_2_), channel_id=1, source_target_pairs={{0,4},{4,0},{8,12},{12,8},{16,20},{20,16},{24,28},{28,24},{1,5},{5... | collective-permute-start | bytes 14155784 | tf_op jit(solution)/shard_map/ppermute | solution.py:447
  585.7 33.1 %collective-permute-start.60 = (bf16[128,2304]{1,0:T(8,128)(2,1)S(1)}, bf16[128,2304]{1,0:T(8,128)(2,1)S(1)}, u32[]{:S(2)}, u32[]{:S(2)}) collective-permute-start(bf16[128,2304]{1,0:T(8,128)(2,1)S(1)} %subtract_convert_fusion), channel_id=1, source_target_pairs={{0,8},{4,12},{8,0},{12,4},{16,24},{20,28},{24,16},{28,20},{1,9},{5... | collective-permute-start | bytes 1769480 | tf_op jit(solution)/shard_map/ppermute | solution.py:447
  586.5 32.2 %collective-permute-start.61 = (bf16[128,2304]{1,0:T(8,128)(2,1)S(1)}, bf16[128,2304]{1,0:T(8,128)(2,1)S(1)}, u32[]{:S(2)}, u32[]{:S(2)}) collective-permute-start(bf16[128,2304]{1,0:T(8,128)(2,1)S(1)} %subtract_convert_fusion), channel_id=1, source_target_pairs={{0,16},{4,20},{8,24},{12,28},{16,0},{20,4},{24,8},{28,12},{1,17},{... | collective-permute-start | bytes 1769480 | tf_op jit(solution)/shard_map/ppermute | solution.py:447
  661.5 73.6 %all-to-all-start.4 = ((bf16[8,288,1152]{2,1,0:T(8,128)(2,1)}), bf16[8,288,1152]{2,1,0:T(8,128)(2,1)}, u32[]{:S(2)}, u32[]{:S(2)}) async-start(bf16[8,288,1152]{2,1,0:T(8,128)(2,1)} %bitcast.88), calls=%async_computation.4 | async-start | bytes 10616832 | tf_op jit(solution)/shard_map/all_to_all | solution.py:638
  690.0 43.7 %collective-permute-start.72 = (bf16[8,2,72,512]{3,2,0,1:T(8,128)(2,1)S(1)}, bf16[8,2,72,512]{3,2,0,1:T(8,128)(2,1)S(1)}, u32[]{:S(2)}, u32[]{:S(2)}) collective-permute-start(bf16[8,2,72,512]{3,2,0,1:T(8,128)(2,1)S(1)} %copy_bitcast_fusion), channel_id=1, source_target_pairs={{0,1},{1,0},{2,3},{3,2},{4,5},{5,4},{6,7},{7,6},{8,9},{9,8},{10,11... | collective-permute-start | bytes 3538952 | tf_op jit(solution)/shard_map/ppermute | solution.py:451
  690.0 49.0 %collective-permute-start.70 = (bf16[128,2304]{1,0:T(8,128)(2,1)}, bf16[128,2304]{1,0:T(8,128)(2,1)}, u32[]{:S(2)}, u32[]{:S(2)}) collective-permute-start(bf16[128,2304]{1,0:T(8,128)(2,1)} %pad_maximum_fusion.11), channel_id=1, source_target_pairs={{0,8},{4,12},{8,0},{12,4},{16,24},{20,28},{24,16},{28,20},{1,9},{5... | collective-permute-start | bytes 1769480 | tf_op jit(solution)/shard_map/ppermute | solution.py:447
  691.7 47.4 %collective-permute-start.71 = (bf16[128,2304]{1,0:T(8,128)(2,1)}, bf16[128,2304]{1,0:T(8,128)(2,1)}, u32[]{:S(2)}, u32[]{:S(2)}) collective-permute-start(bf16[128,2304]{1,0:T(8,128)(2,1)} %pad_maximum_fusion.12), channel_id=1, source_target_pairs={{0,16},{4,20},{8,24},{12,28},{16,0},{20,4},{24,8},{28,12},{1,17},{... | collective-permute-start | bytes 1769480 | tf_op jit(solution)/shard_map/ppermute | solution.py:447
  739.1 73.2 %all-to-all-start.5 = ((bf16[8,288,1152]{2,1,0:T(8,128)(2,1)}), bf16[8,288,1152]{2,1,0:T(8,128)(2,1)}, u32[]{:S(2)}, u32[]{:S(2)}) async-start(bf16[8,288,1152]{2,1,0:T(8,128)(2,1)} %bitcast.90), calls=%async_computation.5 | async-start | bytes 10616832 | tf_op jit(solution)/shard_map/all_to_all | solution.py:638
  745.9 64.6 %collective-permute-start.75 = (bf16[64,2304]{1,0:T(8,128)(2,1)}, bf16[64,2304]{1,0:T(8,128)(2,1)}, u32[]{:S(2)}, u32[]{:S(2)}) collective-permute-start(bf16[64,2304]{1,0:T(8,128)(2,1)} %add_convert_fusion.1), channel_id=1, source_target_pairs={{0,8},{4,12},{8,0},{12,4},{16,24},{20,28},{24,16},{28,20},{1,9},{5... | collective-permute-start | bytes 884744 | tf_op jit(solution)/shard_map/ppermute | solution.py:447
  749.8 60.7 %collective-permute-start.74 = (bf16[64,2304]{1,0:T(8,128)(2,1)}, bf16[64,2304]{1,0:T(8,128)(2,1)}, u32[]{:S(2)}, u32[]{:S(2)}) collective-permute-start(bf16[64,2304]{1,0:T(8,128)(2,1)} %add_convert_fusion.2), channel_id=1, source_target_pairs={{0,16},{4,20},{8,24},{12,28},{16,0},{20,4},{24,8},{28,12},{1,17},{... | collective-permute-start | bytes 884744 | tf_op jit(solution)/shard_map/ppermute | solution.py:447
  757.0 55.0 %collective-permute-start.73 = (bf16[8,72,512]{2,1,0:T(8,128)(2,1)S(1)}, bf16[8,72,512]{2,1,0:T(8,128)(2,1)S(1)}, u32[]{:S(2)}, u32[]{:S(2)}) collective-permute-start(bf16[8,72,512]{2,1,0:T(8,128)(2,1)S(1)} %dynamic-slice_bitcast_fusion), channel_id=1, source_target_pairs={{0,2},{1,3},{2,0},{3,1},{4,6},{5,7},{6,4},{7,5},{8,10},{9,11},{10,... | collective-permute-start | bytes 1769480 | tf_op jit(solution)/shard_map/ppermute | solution.py:451
  831.4 69.5 %all-to-all-start.7 = ((bf16[8,288,1152]{2,1,0:T(8,128)(2,1)}), bf16[8,288,1152]{2,1,0:T(8,128)(2,1)}, u32[]{:S(2)}, u32[]{:S(2)}) async-start(bf16[8,288,1152]{2,1,0:T(8,128)(2,1)} %bitcast.89), calls=%async_computation.7 | async-start | bytes 10616832 | tf_op jit(solution)/shard_map/all_to_all | solution.py:638
  837.6 43.0 %collective-permute-start.76 = (bf16[8,72,768]{2,1,0:T(8,128)(2,1)}, bf16[8,72,768]{2,1,0:T(8,128)(2,1)}, u32[]{:S(2)}, u32[]{:S(2)}) collective-permute-start(bf16[8,72,768]{2,1,0:T(8,128)(2,1)} %get-tuple-element.429), channel_id=1, source_target_pairs={{0,2},{1,3},{2,0},{3,1},{4,6},{5,7},{6,4},{7,5},{8,10},{9,11},{10,... | collective-permute-start | bytes 2654216 | tf_op jit(solution)/shard_map/ppermute | solution.py:451
  882.5 40.7 %collective-permute-start.79 = (bf16[2,8,72,768]{3,2,1,0:T(8,128)(2,1)S(1)}, bf16[2,8,72,768]{3,2,1,0:T(8,128)(2,1)}, u32[]{:S(2)}, u32[]{:S(2)}) collective-permute-start(bf16[2,8,72,768]{3,2,1,0:T(8,128)(2,1)S(1)} %reverse_select_fusion.1), channel_id=1, source_target_pairs={{0,1},{1,0},{2,3},{3,2},{4,5},{5,4},{6,7},{7,6},{8,9},{9,8},{10,11... | collective-permute-start | bytes 5308424 | tf_op jit(solution)/shard_map/ppermute | solution.py:451
  (184 other events, 2413.9 us)
